TPU v7x, 32 devices: a whole 2x2x4 slice. The times are simulated.
32 devices in a mesh: section: 2 (over core), dp: 4 (over z), mp: 4 (over y, x).
Axes of the slice: x: 2, y: 2, z: 4, core: 2. Of those that a mesh axis runs over, the one named last changes fastest.
Arguments:
- fwd_in: bfloat16 [2, 4, 4, 256, 3072], P('section', 'dp', 'mp'), may hold values from -6 to 6
- kept_in: bfloat16 [2, 4, 4, 256, 3072], P('section', 'dp', 'mp'), may hold values from -6 to 6
- cotangent: bfloat16 [2, 4, 4, 256, 3072], P('section', 'dp', 'mp'), may hold values from -6 to 6
- weight: bfloat16 [2, 12288, 12288], P('section', 'mp', 'dp'), may hold values from -1 to 1
- bias: float32 [2, 12288], P('section', 'dp'), may hold values from -3 to 3
- norm_gain: float32 [2, 12288], P('section', 'mp'), may hold values from 0.1 to 1.9
- norm_shift: float32 [2, 12288], P('section', 'mp'), may hold values from -3 to 3
Outputs:
- next_in: bfloat16 [2, 4, 4, 256, 3072], P('section', 'dp', 'mp')
- passed: bfloat16 [2, 4, 4, 256, 3072], P('section', 'dp', 'mp')
- weight_grad: float32 [2, 12288, 12288], P('section', 'mp', 'dp')
- bias_grad: float32 [2, 12288], P('section', 'dp')
- norm_grads: float32 [2, 2, 12288], P('section', None, 'mp')
All inputs are finite; a program needn't handle non-finite values.
Results may differ from a plain program's by a relative error of at most 0.018.
Values may be sent and summed in bfloat16 or wider, within the bound.
No kernel may reach another device: no remote copies, remote signals or barrier semaphores. Data moves between devices by JAX's collectives and lax.ppermute only.
A program may use at most 128 MiB of HBM per device.

v0:
```python
import jax
import jax.numpy as jnp
from jax import lax
from jax.sharding import PartitionSpec as P

eps = 1e-05


def from_partner(value, axis, stride):
    mask = 2**stride
    pairs = [(source, source ^ mask) for source in range(lax.axis_size(axis))]
    return lax.ppermute(value, axis, pairs)


def standardize(values, totals, squares, full_width):
    mean_val = totals / full_width
    spread = squares / full_width - mean_val * mean_val
    inv_std = lax.rsqrt(spread + eps)
    return ((values - mean_val[:, None]) * inv_std[:, None], inv_std)


def regroup(outgoing, groups):
    flat_buffer = outgoing.reshape((groups * groups,) + outgoing.shape[2:])
    moved_data = lax.all_to_all(flat_buffer, ("dp", "mp"), split_axis=0, concat_axis=0, tiled=True)
    return moved_data.reshape(outgoing.shape)


def shards(fwd_in, kept_in, cotangent, weight, bias, norm_gain, norm_shift):
    section_index = lax.axis_index("section")
    groups = lax.axis_size("dp")
    row_count = fwd_in.shape[3]
    col_count = fwd_in.shape[4]
    full_width = col_count * lax.axis_size("mp")
    piece_rows = row_count // groups
    piece_cols = col_count // groups
    weight_tile = weight.reshape(col_count, col_count)
    gain_cols = norm_gain.reshape(col_count)
    shift_cols = norm_shift.reshape(col_count)
    fresh_rows = fwd_in.reshape(row_count, col_count).astype(jnp.float32)
    kept_values = kept_in.reshape(row_count, col_count).astype(jnp.float32)
    upstream = cotangent.reshape(row_count, col_count)
    row_stats = lax.psum(
        (
            jnp.sum(fresh_rows, 1),
            jnp.sum(fresh_rows * fresh_rows, 1),
            jnp.sum(kept_values, 1),
            jnp.sum(kept_values * kept_values, 1),
        ),
        "mp",
    )
    fresh_hat, unused_scale = standardize(fresh_rows, row_stats[0], row_stats[1], full_width)
    kept_hat, kept_inv = standardize(kept_values, row_stats[2], row_stats[3], full_width)
    normed = (fresh_hat * gain_cols + shift_cols).astype(jnp.bfloat16)
    normed_kept = (kept_hat * gain_cols + shift_cols).astype(jnp.bfloat16)
    upstream_all = lax.all_gather(upstream, "mp", axis=0, tiled=True)
    gathered, gathered_kept = (
        lax.all_gather(normed, "dp", axis=0, tiled=True),
        lax.all_gather(normed_kept, "dp", axis=0, tiled=True),
    )
    weight_grad = lax.dot_general(
        gathered_kept, upstream_all, (((0,), (0,)), ((), ())), preferred_element_type=jnp.float32
    )
    segment = gathered
    summed = lax.psum_scatter(
        jnp.dot(segment, weight_tile, preferred_element_type=jnp.float32).astype(jnp.bfloat16),
        "mp",
        scatter_dimension=0,
        tiled=True,
    ).astype(jnp.float32)
    output = (summed + bias.reshape(col_count)).astype(jnp.bfloat16)
    bias_grad = jnp.sum(upstream_all, 0, dtype=jnp.float32)
    segment = upstream_all
    grad_rows = lax.psum_scatter(
        lax.dot_general(
            segment, weight_tile, (((1,), (1,)), ((), ())), preferred_element_type=jnp.float32
        ).astype(jnp.bfloat16),
        "dp",
        scatter_dimension=0,
        tiled=True,
    ).astype(jnp.float32)
    scaled = grad_rows * gain_cols
    column_grads = lax.psum((jnp.sum(grad_rows * kept_hat, 0), jnp.sum(grad_rows, 0)), "dp")
    row_terms = lax.psum((jnp.sum(scaled, 1), jnp.sum(scaled * kept_hat, 1)), "mp")
    input_grad = (
        kept_inv[:, None]
        * (
            scaled
            - row_terms[0][:, None] / full_width
            - kept_hat * (row_terms[1][:, None] / full_width)
        )
    ).astype(jnp.bfloat16)
    out_pack = output.reshape(groups, piece_rows, groups, piece_cols).transpose(0, 2, 1, 3)
    grad_pack = input_grad.reshape(groups, piece_rows, groups, piece_cols).transpose(2, 0, 1, 3)
    outgoing = jnp.where(section_index == 0, out_pack, grad_pack)
    arrived = from_partner(regroup(outgoing, groups), "section", 0)
    as_cotangent = arrived.transpose(0, 2, 1, 3).reshape(row_count, col_count)
    as_input = arrived.transpose(1, 2, 0, 3).reshape(row_count, col_count)
    next_in = jnp.where(section_index == 0, as_cotangent, as_input)
    passed = jnp.where(section_index == 0, input_grad, output)
    return (
        next_in.reshape(fwd_in.shape),
        passed.reshape(fwd_in.shape),
        weight_grad.reshape(1, col_count, col_count),
        bias_grad.reshape(1, col_count),
        jnp.stack([column_grads[0], column_grads[1]]).reshape(1, 2, col_count),
    )


def solution(mesh):
    placed = (
        P("section", "dp", "mp", None, None),
        P("section", "dp", "mp", None, None),
        P("section", "dp", "mp", None, None),
        P("section", "mp", "dp"),
        P("section", "dp"),
        P("section", "mp"),
        P("section", "mp"),
    )
    return jax.shard_map(
        shards,
        mesh=mesh,
        in_specs=placed,
        out_specs=(
            P("section", "dp", "mp", None, None),
            P("section", "dp", "mp", None, None),
            P("section", "mp", "dp"),
            P("section", "dp"),
            P("section", None, "mp"),
        ),
        check_vma=False,
    )
```

profile of v0, /device:TPU:0, one launch (start us, length us, event | category | flops | bytes accessed | tf_op | source)
XLA Modules:
  0.0 633.3 jit_solution(6474836863168188891)
XLA Ops:
  7.2 0.7 all-gather.9.cloned.1.call-update
  7.9 74.8 %all-gather.9.cloned.1.call-done = bf16[1,1,1,1024,3072]{4,3,2,1,0:T(8,128)(2,1)} async-done(((bf16[1,1,1,256,3072]{4,3,2,1,0:T(8,128)(2,1)}), bf16[1,1,1,1024,3072]{4,3,2,1,0:T(8,128)(2,1)}) %all-gather.9.cloned.1.call-update) | async-done | bytes 6291472 | tf_op jit(solution)/shard_map/all_gather | solution.py:55
  82.7 25.7 %fusion.9 = bf16[1024,3072]{1,0:T(8,128)(2,1)} fusion(bf16[1,3072,3072]{2,1,0:T(8,128)(2,1)} %param.10, bf16[1,1,1,1024,3072]{4,3,2,1,0:T(8,128)(2,1)} %all-gather.9.cloned.1.call-done), kind=kOutput, calls=%fused_computation.9 | convolution fusion | flops 19330498560 | bytes 31457280 | tf_op jit(solution)/shard_map/dot_general | solution.py:74
  108.5 0.0 all-gather.5.cloned.1.call-start
  108.5 1.3 copy-done
  109.8 0.3 convert_reduce_fusion.2
  110.1 0.4 fusion.26
  110.5 8.9 %all-reduce.1 = (f32[256]{0:T(256)S(1)}, f32[256]{0:T(256)S(1)}) all-reduce(f32[256]{0:T(256)S(1)} %convert_reduce_fusion.2, f32[256]{0:T(256)S(1)} %fusion.26), channel_id=1, replica_groups=mesh['section'=2,'dp'=4,'mp'=4] {'mp'}, use_global_device_ids=true, to_apply=%region_8.0 | all-reduce | flops 512 | bytes 4096 | tf_op jit(solution)/shard_map/psum | solution.py:42
  119.4 0.3 convert_reduce_fusion.3
  119.7 0.4 fusion.25
  120.1 99.2 %reduce-scatter.5.cloned.1.call-done = bf16[256,3072]{1,0:T(8,128)(2,1)} async-done(((bf16[1024,3072]{1,0:T(8,128)(2,1)}), bf16[256,3072]{1,0:T(8,128)(2,1)}) %reduce-scatter.5.cloned.1.call-update) | async-done | bytes 1572880 | tf_op jit(solution)/shard_map/reduce_scatter | solution.py:73
  219.3 4.3 fusion.36
  223.7 9.8 %all-reduce = (f32[256]{0:T(256)S(1)}, f32[256]{0:T(256)S(1)}, f32[256]{0:T(256)S(1)}, f32[256]{0:T(256)S(1)}) all-reduce(f32[256]{0:T(256)S(1)} %get-tuple-element.6, f32[256]{0:T(256)S(1)} %get-tuple-element.7, f32[256]{0:T(256)S(1)} %fusion.25, f32[256]{0:T(256)S(1)} %convert_reduce_fusion.3), channel_id=1, replica_groups=mesh['section'=2,'dp'=4,'mp'=4] {'mp'}, use_global_device_ids=true, to_apply=%region_13.0 | all-reduce | flops 1024 | bytes 8192 | tf_op jit(solution)/shard_map/psum | solution.py:83
  233.5 1.9 fusion.24
  235.4 0.2 reduce-scatter.3.cloned.1.call-start
  235.7 114.0 %all-gather.5.cloned.1.call-done = bf16[1024,3072]{1,0:T(8,128)(2,1)} async-done(((bf16[256,3072]{1,0:T(8,128)(2,1)}), bf16[1024,3072]{1,0:T(8,128)(2,1)}) %all-gather.5.cloned.1.call-update) | async-done | bytes 6291472 | tf_op jit(solution)/shard_map/all_gather | solution.py:57
  349.7 25.5 %fusion.6 = bf16[1024,3072]{1,0:T(8,128)(2,1)} fusion(bf16[1024,3072]{1,0:T(8,128)(2,1)} %all-gather.5.cloned.1.call-done, bf16[1,3072,3072]{2,1,0:T(8,128)(2,1)} %param.10), kind=kOutput, calls=%fused_computation.8 | convolution fusion | flops 19330498560 | bytes 31457280 | tf_op jit(solution)/shard_map/dot_general | solution.py:65
  375.3 0.5 all-gather.7.cloned.1.call-update
  375.8 68.0 %reduce-scatter.3.cloned.1.call-done = bf16[256,3072]{1,0:T(8,128)(2,1)} async-done(((bf16[1024,3072]{1,0:T(8,128)(2,1)}), bf16[256,3072]{1,0:T(8,128)(2,1)}) %reduce-scatter.3.cloned.1.call-update) | async-done | bytes 1572880 | tf_op jit(solution)/shard_map/reduce_scatter | solution.py:64
  443.8 5.2 select_bitcast_fusion
  449.0 3.4 reshape.77
  452.4 2.1 reshape.79
  454.5 3.1 bitcast_select_fusion.1
  457.6 5.7 all-to-all-start
  463.3 4.3 convert_reduce_fusion
  467.7 94.1 %all-reduce.2 = (f32[1,3072]{1,0:T(1,128)S(1)}, f32[1,3072]{1,0:T(1,128)S(1)}) all-reduce(f32[1,3072]{1,0:T(1,128)S(1)} %bitcast.97, f32[1,3072]{1,0:T(1,128)S(1)} %bitcast.96), channel_id=1, replica_groups=mesh['section'=2,'dp'=4,'mp'=4] {'dp'}, use_global_device_ids=true, to_apply=%region_18.0 | all-reduce | flops 6144 | bytes 49152 | tf_op jit(solution)/shard_map/psum | solution.py:82
  561.7 0.6 maximum_bitcast_fusion
  562.4 33.2 %all-gather.7.cloned.1.call-done = bf16[1024,3072]{1,0:T(8,128)(2,1)} async-done(((bf16[256,3072]{1,0:T(8,128)(2,1)}), bf16[1024,3072]{1,0:T(8,128)(2,1)}) %all-gather.7.cloned.1.call-update) | async-done | bytes 6291472 | tf_op jit(solution)/shard_map/all_gather | solution.py:58
  595.6 27.7 %convolution_bitcast_fusion = f32[1,3072,3072]{2,1,0:T(8,128)} fusion(bf16[1024,3072]{1,0:T(8,128)(2,1)} %all-gather.7.cloned.1.call-done, bf16[1,1,1,1024,3072]{4,3,2,1,0:T(8,128)(2,1)} %all-gather.9.cloned.1.call-done), kind=kOutput, calls=%fused_computation | convolution fusion | flops 19327352832 | bytes 50331648 | tf_op jit(solution)/shard_map/dot_general | solution.py:60
  623.3 0.1 bitcast_select_fusion
  623.5 1.2 copy.20
  624.7 2.1 select_n.36
  (25 shorter events, 0.2 us)
Async XLA Ops:
  7.2 75.6 %all-gather.9.cloned.1.call-start = ((), (), s32[]{:S(2)}) async-start(), calls=%async_computation.7 | async-start | bytes 7864320 | tf_op jit(solution)/shard_map/all_gather | solution.py:55
  7.9 211.4 %reduce-scatter.5.cloned.1.call-start = ((), (), s32[]{:S(2)}) async-start(), calls=%async_computation.5 | async-start | bytes 7864320 | tf_op jit(solution)/shard_map/reduce_scatter | solution.py:73
  108.4 1.4 copy-start
  108.4 11.0 %copy-start.1 = (bf16[1,1,1,256,3072]{4,3,2,1,0:T(8,128)(2,1)S(1)}, bf16[1,1,1,256,3072]{4,3,2,1,0:T(8,128)(2,1)}, u32[]{:S(2)}) copy-start(bf16[1,1,1,256,3072]{4,3,2,1,0:T(8,128)(2,1)} %param.7) | copy-start | bytes 4718596
  108.4 110.9 %copy-start.4 = (f32[1,3072]{1,0:T(1,128)S(1)}, f32[1,3072]{1,0:T(1,128)}, u32[]{:S(2)}) copy-start(f32[1,3072]{1,0:T(1,128)} %param.12) | copy-start | bytes 36868
  108.5 110.9 %copy-start.5 = (f32[1,3072]{1,0:T(1,128)S(1)}, f32[1,3072]{1,0:T(1,128)}, u32[]{:S(2)}) copy-start(f32[1,3072]{1,0:T(1,128)} %param.13) | copy-start | bytes 36868
  108.5 241.2 %all-gather.5.cloned.1.call-start = ((), (), s32[]{:S(2)}) async-start(), calls=%async_computation.3 | async-start | bytes 7864320 | tf_op jit(solution)/shard_map/all_gather | solution.py:57
  235.4 208.4 %reduce-scatter.3.cloned.1.call-start = ((), (), s32[]{:S(2)}) async-start(), calls=%async_computation.4 | async-start | bytes 7864320 | tf_op jit(solution)/shard_map/reduce_scatter | solution.py:64
  375.2 68.6 %copy-start.2 = (bf16[256,3072]{1,0:T(8,128)(2,1)S(1)}, bf16[256,3072]{1,0:T(8,128)(2,1)}, u32[]{:S(2)}) copy-start(bf16[256,3072]{1,0:T(8,128)(2,1)} %reduce-scatter.5.cloned.1.call-done) | copy-start | bytes 4718596
  375.2 68.6 %copy-start.6 = (f32[1,3072]{1,0:T(1,128)S(1)}, f32[1,3072]{1,0:T(1,128)}, u32[]{:S(2)}) copy-start(f32[1,3072]{1,0:T(1,128)} %param.11) | copy-start | bytes 36868
  375.2 220.3 %all-gather.7.cloned.1.call-start = ((), (), s32[]{:S(2)}) async-start(), calls=%async_computation.6 | async-start | bytes 7864320 | tf_op jit(solution)/shard_map/all_gather | solution.py:58
  449.0 3.4 copy-start.3
  457.6 104.7 %all-to-all-start = ((bf16[16,64,768]{2,1,0:T(8,128)(2,1)}), bf16[16,64,768]{2,1,0:T(8,128)(2,1)S(1)}, u32[]{:S(2)}, u32[]{:S(2)}) async-start(bf16[16,64,768]{2,1,0:T(8,128)(2,1)} %bitcast.9), calls=%async_computation.2 | async-start | bytes 3145728 | tf_op jit(solution)/shard_map/all_to_all | solution.py:24
  562.4 61.0 %collective-permute-start = (bf16[4,4,64,768]{3,2,1,0:T(8,128)(2,1)S(1)}, bf16[4,4,64,768]{3,2,1,0:T(8,128)(2,1)S(1)}, u32[]{:S(2)}, u32[]{:S(2)}) collective-permute-start(bf16[4,4,64,768]{3,2,1,0:T(8,128)(2,1)S(1)} %bitcast.90), channel_id=1, source_target_pairs={{0,16},{16,0},{1,17},{17,1},{2,18},{18,2},{3,19},{19,3},{4,20},{20... | collective-permute-start | bytes 4718600 | tf_op jit(solution)/shard_map/ppermute | solution.py:12
Sparse Core Ops, SparseCore 0:
  9.8 72.8 all-gather.8
  108.5 110.7 reduce-scatter.4
  235.6 114.0 all-gather.4
  375.4 68.4 reduce-scatter.2
  445.8 149.7 all-gather.6
where the time goes:
time: 634 us; the launch traced here: 633 us
  waiting for transfers between devices  390 us (62%)
  blocking collectives  113 us (18%)
  matrix products  79 us (12%)
  other arithmetic  21 us (3%)
  between operations  13.9 us (2%)
  local copies, waits for them, and re-layouts  10.1 us (2%)
    all_gather x1, waiting for transfers between devices, shards(): lax.all_gather(normed, 'dp', axis=0, tiled=True)  114 us
    reduce_scatter x1, waiting for transfers between devices, shards(): lax.psum_scatter(lax.dot_general(segment, weight_tile, (((1,), (1,)), (()...  99.2 us
    psum x1, blocking collectives, shards(): lax.psum((jnp.sum(grad_rows * kept_hat, 0), jnp.sum(grad_rows, 0)), 'dp')  94.1 us
    all_gather x1, waiting for transfers between devices, shards(): upstream_all = lax.all_gather(upstream, 'mp', axis=0, tiled=True)  74.8 us
    reduce_scatter x1, waiting for transfers between devices, shards(): lax.psum_scatter(jnp.dot(segment, weight_tile, preferred_element_type=jnp...  68 us
    all_gather x1, waiting for transfers between devices, shards(): lax.all_gather(normed_kept, 'dp', axis=0, tiled=True)  33.2 us
    dot_general x1, matrix products, shards(): lax.dot_general(gathered_kept, upstream_all, (((0,), (0,)), ((), ())), pr...  27.7 us
    dot_general x1, matrix products, shards(): lax.dot_general(segment, weight_tile, (((1,), (1,)), ((), ())), preferred...  25.7 us
  transfers between devices with their start and end apart: 7, of which 5 were waited for; matrix products, arithmetic and copies ran while one was open for 8% of the time, Pallas kernels for 0%

commit v1 on v0

--- a/solution.py
+++ b/solution.py
@@ -1,9 +1,168 @@
+import functools
+
 import jax
 import jax.numpy as jnp
 from jax import lax
+from jax.experimental import pallas as pl
+from jax.experimental.pallas import tpu as pltpu
 from jax.sharding import PartitionSpec as P
 
 eps = 1e-05
+V_CHUNKS = 4
+LIGHT = pl.CostEstimate(flops=1, bytes_accessed=1, transcendentals=0)
+
+
+def after(value, *others):
+    return lax.optimization_barrier((value,) + others)[0]
+
+
+def ring_total(value, axis):
+    n = lax.axis_size(axis)
+    parts = [
+        lax.ppermute(value, axis, [(s, (s + k) % n) for s in range(n)]) for k in range(1, n)
+    ]
+    total = value
+    for part in parts:
+        total = total + part
+    return total
+
+
+def flip(value, axis, mask):
+    n = lax.axis_size(axis)
+    return lax.ppermute(value, axis, [(s, s ^ mask) for s in range(n)])
+
+
+def pieces_of(matrix, groups, swapped):
+    rows, cols = matrix.shape[0] // groups, matrix.shape[1] // groups
+    cut = lambda r, c: matrix[r * rows:(r + 1) * rows, c * cols:(c + 1) * cols]
+    pairs = [(a, b) for a in range(groups) for b in range(groups)]
+    return jnp.stack([cut(b, a) if swapped else cut(a, b) for a, b in pairs])
+
+
+def matrix_of(pieces, groups, swapped):
+    at = lambda r, c: pieces[c * groups + r] if swapped else pieces[r * groups + c]
+    return jnp.concatenate(
+        [jnp.concatenate([at(r, c) for c in range(groups)], 1) for r in range(groups)], 0
+    )
+
+
+def grad_kernel(v_ref, c_ref, *rest):
+    out_ref, turned = rest[-2:]
+
+    @pl.when(pl.program_id(0) == 0)
+    def _():
+        turned[...] = v_ref[...].T
+
+    out_ref[...] = jnp.dot(turned[...], c_ref[...], preferred_element_type=jnp.float32)
+
+
+def grad_block(kept_block, upstream, filled, block, blocks):
+    tokens, width = kept_block.shape
+    cols = upstream.shape[1]
+    step = 768
+    specs = [
+        pl.BlockSpec((tokens, width), lambda j: (0, 0)),
+        pl.BlockSpec((tokens, step), lambda j: (0, j)),
+    ]
+    operands = [kept_block, upstream]
+    aliases = {}
+    if filled is not None:
+        specs.append(pl.BlockSpec(memory_space=pl.ANY))
+        operands.append(filled)
+        aliases = {2: 0}
+    return pl.pallas_call(
+        grad_kernel,
+        grid=(cols // step,),
+        in_specs=specs,
+        out_specs=pl.BlockSpec((width, step), lambda j: (block, j)),
+        out_shape=jax.ShapeDtypeStruct((width * blocks, cols), jnp.float32),
+        scratch_shapes=[pltpu.VMEM((width, tokens), jnp.bfloat16)],
+        input_output_aliases=aliases,
+        compiler_params=pltpu.CompilerParams(vmem_limit_bytes=32 * 2**20),
+        cost_estimate=LIGHT,
+    )(*operands)
+
+
+def share_kernel(count, turned, *refs):
+    w_ref, out_ref = refs[count], refs[-1]
+    dims = (((1,), (1 if turned else 0,)), ((), ()))
+    for k in range(count):
+        out_ref[k] = lax.dot_general(
+            refs[k][...], w_ref[...], dims, preferred_element_type=jnp.float32
+        ).astype(jnp.bfloat16)
+
+
+def shares(blocks, w, turned, filled, at, total):
+    count = len(blocks)
+    rows, depth = blocks[0].shape
+    cols = w.shape[0] if turned else w.shape[1]
+    step = 512
+    specs = [pl.BlockSpec((rows, depth), lambda j: (0, 0))] * count
+    if turned:
+        specs.append(pl.BlockSpec((step, depth), lambda j: (j, 0)))
+    else:
+        specs.append(pl.BlockSpec((depth, step), lambda j: (0, j)))
+    operands = list(blocks) + [w]
+    aliases = {}
+    if filled is not None:
+        specs.append(pl.BlockSpec(memory_space=pl.ANY))
+        operands.append(filled)
+        aliases = {count + 1: 0}
+    return pl.pallas_call(
+        functools.partial(share_kernel, count, turned),
+        grid=(cols // step,),
+        in_specs=specs,
+        out_specs=pl.BlockSpec((count, rows, step), lambda j: (at // count, 0, j)),
+        out_shape=jax.ShapeDtypeStruct((total, rows, cols), jnp.bfloat16),
+        input_output_aliases=aliases,
+        compiler_params=pltpu.CompilerParams(vmem_limit_bytes=32 * 2**20),
+        cost_estimate=LIGHT,
+    )(*operands)
+
+
+def boundary_kernel(g_ref, kept_ref, columns_ref, gain_ref, h_ref, h1_ref, h2_ref, bias_ref, section_ref, passed_ref, out_ref):
+    step = pl.program_id(0)
+    first = section_ref[0] == 0
+    groups = pl.num_programs(0)
+    width = out_ref.shape[2]
+    f32 = jnp.float32
+    columns = columns_ref[...]
+    mean, inverse, one, two = (columns[:, k:k + 1] for k in range(4))
+    for f in range(out_ref.shape[0] // 4):
+        cut = pl.ds(f * width, width)
+        hat = (kept_ref[:, cut].astype(f32) - mean) * inverse
+        grad = (inverse * (g_ref[:, cut] * gain_ref[:, cut] - one - hat * two)).astype(jnp.bfloat16)
+        summed = h_ref[:, cut].astype(f32) + h1_ref[:, cut].astype(f32) + h2_ref[:, cut].astype(f32)
+        output = (summed + bias_ref[:, cut]).astype(jnp.bfloat16)
+        passed_ref[:, cut] = jnp.where(first, grad, output)
+        out_ref[jnp.where(first, step * groups + f, f * groups + step)] = jnp.where(
+            first, output, grad
+        )
+
+
+def boundary(grad_rows, kept_rows, columns, gain, h0, h1, h2, bias, section):
+    rows, cols = grad_rows.shape
+    part = rows // 4
+    wide = pl.BlockSpec((part, cols), lambda j: (j, 0))
+    line = pl.BlockSpec((1, cols), lambda j: (0, 0))
+    return pl.pallas_call(
+        boundary_kernel,
+        grid=(4,),
+        in_specs=[
+            wide, wide, pl.BlockSpec((part, 4), lambda j: (j, 0)), line, wide, wide, wide, line,
+            pl.BlockSpec(memory_space=pltpu.SMEM),
+        ],
+        out_specs=[wide, pl.BlockSpec((16, part, cols // 4), lambda j: (0, 0, 0))],
+        out_shape=[
+            jax.ShapeDtypeStruct((rows, cols), jnp.bfloat16),
+            jax.ShapeDtypeStruct((16, part, cols // 4), jnp.bfloat16),
+        ],
+        compiler_params=pltpu.CompilerParams(vmem_limit_bytes=32 * 2**20),
+        cost_estimate=LIGHT,
+    )(
+        grad_rows, kept_rows, columns, gain.reshape(1, cols), h0, h1, h2, bias.reshape(1, cols),
+        section.reshape(1),
+    )
 
 
 def from_partner(value, axis, stride):
@@ -25,7 +184,7 @@
     return moved_data.reshape(outgoing.shape)
 
 
-def shards(fwd_in, kept_in, cotangent, weight, bias, norm_gain, norm_shift):
+def shards_of_any_size(fwd_in, kept_in, cotangent, weight, bias, norm_gain, norm_shift):
     section_index = lax.axis_index("section")
     groups = lax.axis_size("dp")
     row_count = fwd_in.shape[3]
@@ -106,6 +265,171 @@
     )
 
 
+PAIRS = [(0, 1), (1, 0), (2, 3), (3, 2)]
+MIDDLE = [(1, 2), (2, 1)]
+INWARD = [(0, 1), (3, 2)]
+OUTWARD = [(1, 0), (2, 3)]
+
+
+def shards_of_four(fwd_in, kept_in, cotangent, weight, bias, norm_gain, norm_shift):
+    f32, bf16 = jnp.float32, jnp.bfloat16
+    section = lax.axis_index("section")
+    dp, mp = lax.axis_index("dp"), lax.axis_index("mp")
+    inner = (dp == 1) | (dp == 2)
+    row_count, col_count = fwd_in.shape[3], fwd_in.shape[4]
+    full_width = col_count * 4
+    half = col_count // 2
+    w = weight.reshape(weight.shape[1], weight.shape[2])
+    gain = norm_gain.reshape(col_count)
+    shift = norm_shift.reshape(col_count)
+    fresh_rows = fwd_in.reshape(row_count, col_count)
+    kept_rows = kept_in.reshape(row_count, col_count)
+    upstream = cotangent.reshape(row_count, col_count)
+    along = lambda value, pairs: lax.ppermute(value, "dp", pairs)
+    pick = lambda stack, k: lax.dynamic_index_in_dim(stack, k, 0, keepdims=False)
+
+    def standardize(values, mean, square_mean):
+        inverse = lax.rsqrt(square_mean - mean * mean + eps)
+        return (values.astype(f32) - mean[:, None]) * inverse[:, None], inverse
+
+    def affine(hat):
+        return (hat * gain + shift).astype(bf16)
+
+    def added(one, two):
+        return (one.astype(f32) + two.astype(f32)).astype(bf16)
+
+    u1a, u1b = along(fresh_rows, PAIRS), along(fresh_rows, MIDDLE)
+    c1, c2 = flip(upstream, "mp", 1), flip(upstream, "mp", 2)
+    fresh, kept = fresh_rows.astype(f32), kept_rows.astype(f32)
+    sums = jnp.stack(
+        [jnp.sum(fresh, 1), jnp.sum(fresh * fresh, 1), jnp.sum(kept, 1), jnp.sum(kept * kept, 1)]
+    )
+    sums = sums + flip(sums, "mp", 1)
+    stats = (sums + flip(sums, "mp", 2)) / full_width
+    g_stack = shares([upstream], w, True, None, 2, 4)
+    u1a, u1b, c1, c2, stats, g_stack = lax.optimization_barrier(
+        (u1a, u1b, c1, c2, stats, g_stack)
+    )
+
+    u2in, u2out = along(u1a, MIDDLE), along(u1b, OUTWARD)
+    c3l, c3r = flip(c1[:, :half], "mp", 2), flip(c2[:, half:], "mp", 1)
+    kept_hat, kept_inv = standardize(kept_rows, stats[2], stats[3])
+    normed_kept = affine(kept_hat)
+    far1 = along(normed_kept, INWARD)
+    g_stack = shares([c1, c2], w, True, g_stack, 0, 4)
+    all_stats = lax.all_gather(stats[:2], "dp", axis=0)
+    c3 = jnp.concatenate([c3l, c3r], 1)
+    g_stack = shares([c3], w, True, g_stack, 3, 4)
+    u2in, u2out, far1, g_stack = lax.optimization_barrier((u2in, u2out, far1, g_stack))
+
+    def g_block(k):
+        apart = lax.bitwise_xor(lax.bitwise_xor(dp, mp), k)
+        return pick(g_stack, jnp.where(apart == 0, 2, jnp.where(apart == 3, 3, apart - 1)))
+
+    u3 = along(u2in, OUTWARD)
+    r1 = along(g_block(3), INWARD)
+    far2 = along(far1, MIDDLE)
+
+    def normed(rows, block):
+        row_stats = pick(all_stats, block)
+        hat, unused = standardize(rows, row_stats[0], row_stats[1])
+        return affine(hat)
+
+    n0 = normed(fresh_rows, dp)
+    n1 = normed(u1a, lax.bitwise_xor(dp, 1))
+    n2 = normed(jnp.where(inner, u1b, u2out), jnp.where(inner, dp ^ 3, dp ^ 2))
+    h_stack = shares([n0, n1, n2], w, False, None, 0, 4)
+    u3, r1, far2, h_stack = lax.optimization_barrier((u3, r1, far2, h_stack))
+
+    x2 = added(g_block(2), r1)
+    r2out, r2in = along(x2, INWARD), along(x2, MIDDLE)
+    far3 = along(far2, OUTWARD)
+    n3 = normed(jnp.where(inner, u2in, u3), jnp.where(inner, dp ^ 2, dp ^ 3))
+    h_stack = shares([n3], w, False, h_stack, 3, 4)
+
+    def h_block(k):
+        apart = lax.bitwise_xor(lax.bitwise_xor(dp, mp), k)
+        return pick(h_stack, jnp.where(inner & (apart >= 2), apart ^ 1, apart))
+
+    h_far = h_block(3)
+    left, right = flip(h_far[:, :half], "mp", 1), flip(h_far[:, half:], "mp", 2)
+    r2out, r2in, far3, h_stack = lax.optimization_barrier((r2out, r2in, far3, h_stack))
+
+    r3a = along(added(g_block(1), r2in), PAIRS)
+    r3b = along(added(g_block(3), r2out), MIDDLE)
+    h_two, h_one = h_block(2), h_block(1)
+    h_two = jnp.concatenate([added(h_two[:, :half], left), h_two[:, half:]], 1)
+    h_one = jnp.concatenate([h_one[:, :half], added(h_one[:, half:], right)], 1)
+    h_from_one, h_from_two = flip(h_one, "mp", 1), flip(h_two, "mp", 2)
+    c_stack = jnp.stack([upstream, c1, c2, c3])
+    block_sums = jnp.sum(c_stack, 1, dtype=f32)
+    in_order = [pick(block_sums, lax.bitwise_xor(mp, b)) for b in range(4)]
+    bias_grad = in_order[0] + in_order[1] + in_order[2] + in_order[3]
+    c_of = lambda k: pick(c_stack, lax.bitwise_xor(lax.bitwise_xor(dp, mp), k))
+    c_all = jnp.concatenate(
+        [c_of(0), c_of(1), c_of(jnp.where(inner, 3, 2)), c_of(jnp.where(inner, 2, 3))]
+    )
+    r3a, r3b, h_from_one, h_from_two, c_all, normed_kept = lax.optimization_barrier(
+        (r3a, r3b, h_from_one, h_from_two, c_all, normed_kept)
+    )
+
+    near1, near2 = along(normed_kept, MIDDLE), along(normed_kept, OUTWARD)
+    grad_rows = g_block(0).astype(f32) + r3a.astype(f32) + r3b.astype(f32)
+    scaled = grad_rows * gain
+    row_terms = ring_total(jnp.stack([jnp.sum(scaled, 1), jnp.sum(scaled * kept_hat, 1)]), "mp")
+    row_terms = row_terms / full_width
+    column_sums = jnp.stack([jnp.sum(grad_rows * kept_hat, 0), jnp.sum(grad_rows, 0)])
+    columns = jnp.stack([stats[2], kept_inv, row_terms[0], row_terms[1]], 1)
+    passed, outgoing = boundary(
+        grad_rows, kept_rows, columns, gain, h_block(0), h_from_one, h_from_two,
+        bias.reshape(col_count), section,
+    )
+    arrived = lax.all_to_all(outgoing, ("dp", "mp"), split_axis=0, concat_axis=0, tiled=True)
+
+    weight_grad = None
+    width = col_count // V_CHUNKS
+    cuts = lambda value: [value[:, k * width:(k + 1) * width] for k in range(V_CHUNKS)]
+    near3 = [along(part, OUTWARD) for part in lax.optimization_barrier(tuple(cuts(near1)))]
+    ready = lax.optimization_barrier(
+        (
+            tuple(cuts(normed_kept)),
+            tuple(cuts(jnp.where(inner, far1, near2))),
+            tuple(cuts(jnp.where(inner, far2, far3))),
+            tuple(cuts(near1)),
+        )
+    )
+    for k in range(V_CHUNKS):
+        last = near3[k]
+        if weight_grad is not None:
+            last, weight_grad = lax.optimization_barrier((last, weight_grad))
+        own, one, three, near = (part[k] for part in ready)
+        kept_all = jnp.concatenate([own, one, jnp.where(inner, near, last), three])
+        weight_grad = grad_block(kept_all, c_all, weight_grad, k, V_CHUNKS)
+        if k == V_CHUNKS // 2 - 1:
+            arrived, column_sums, weight_grad = lax.optimization_barrier(
+                (arrived, column_sums, weight_grad)
+            )
+
+    column_parts = lax.all_gather(column_sums, "dp", axis=0)
+    column_grads = column_parts[0] + column_parts[1] + column_parts[2] + column_parts[3]
+    arrived = flip(arrived, "section", 1)
+    next_in = jnp.where(section == 0, matrix_of(arrived, 4, False), matrix_of(arrived, 4, True))
+
+    return (
+        next_in.reshape(fwd_in.shape),
+        passed.reshape(fwd_in.shape),
+        weight_grad.reshape(weight.shape),
+        bias_grad.reshape(1, col_count),
+        column_grads.reshape(1, 2, col_count),
+    )
+
+
+def shards(*arrays):
+    if lax.axis_size("dp") == 4 and lax.axis_size("mp") == 4:
+        return shards_of_four(*arrays)
+    return shards_of_any_size(*arrays)
+
+
 def solution(mesh):
     placed = (
         P("section", "dp", "mp", None, None),

time: 634 us -> 374 us (0.59)
  waiting for transfers between devices: 390 us -> 111 us
  Pallas kernels: 0 us -> 96.8 us
  blocking collectives: 113 us -> 32.9 us
  matrix products: 79 us -> 0 us
  starting transfers between devices: 6.08 us -> 63.8 us
  other arithmetic: 21 us -> 39.2 us
  local copies, waits for them, and re-layouts: 10.1 us -> 28.1 us
  between operations: 13.9 us -> 1.4 us
    all_gather x3 -> x0, waiting for transfers between devices: 222 us -> none  [the longest x1 114 us: shards(): lax.all_gather(normed, 'dp', axis=0, tiled=True)]
    reduce_scatter x2 -> x0, waiting for transfers between devices: 167 us -> none  [the longest x1 99.2 us: shards(): lax.psum_scatter(lax.dot_general(segment, weight_tile, (((1,), (1,)), (()...]
    psum x3 -> x0, blocking collectives: 113 us -> none  [the longest x1 94.1 us: shards(): lax.psum((jnp.sum(grad_rows * kept_hat, 0), jnp.sum(grad_rows, 0)), 'dp')]
    ppermute x1 -> x33, waiting for transfers between devices: 0.01 us -> 111 us  [the longest x19 74.8 us: shards_of_four(): along = lambda value, pairs: lax.ppermute(value, 'dp', pairs)]
    pallas_call x0 -> x10, Pallas kernels: none -> 96.8 us  [the longest x5 62.1 us: shares(): pl.pallas_call(functools.partial(share_kernel, count, turned), grid=(cols...]
    dot_general x3 -> x0, matrix products: 79 us -> none  [the longest x1 27.7 us: shards(): lax.dot_general(gathered_kept, upstream_all, (((0,), (0,)), ((), ())), pr...]
    ppermute x1 -> x33, starting transfers between devices: 0.01 us -> 55.3 us  [the longest x19 41.5 us: shards_of_four(): along = lambda value, pairs: lax.ppermute(value, 'dp', pairs)]
    all_gather x0 -> x2, blocking collectives: none -> 32.9 us  [the longest x1 18.5 us: shards_of_four(): all_stats = lax.all_gather(stats[:2], 'dp', axis=0)]
  transfers between devices with their start and end apart: 7 -> 34, of which waited for: 5 -> 10; matrix products, arithmetic and copies ran while one was open for 8% -> 11% of each run, Pallas kernels for 0% -> 26%
where the time goes in v1:
time: 374 us; the launch traced here: 373 us
  waiting for transfers between devices  111 us (30%)
  Pallas kernels  96.8 us (26%)
  starting transfers between devices  63.8 us (17%)
  other arithmetic  39.2 us (10%)
  blocking collectives  32.9 us (9%)
  local copies, waits for them, and re-layouts  28.1 us (8%)
    ppermute x19, waiting for transfers between devices, shards_of_four(): along = lambda value, pairs: lax.ppermute(value, 'dp', pairs)  74.8 us
    pallas_call x5, Pallas kernels, shares(): pl.pallas_call(functools.partial(share_kernel, count, turned), grid=(cols...  62.1 us
    ppermute x19, starting transfers between devices, shards_of_four(): along = lambda value, pairs: lax.ppermute(value, 'dp', pairs)  41.5 us
    ppermute x11, waiting for transfers between devices, flip(): return lax.ppermute(value, axis, [(s, s ^ mask) for s in range(n)])  35.9 us
    pallas_call x4, Pallas kernels, grad_block(): pl.pallas_call(grad_kernel, grid=(cols // step,), in_specs=specs, out_spe...  31.7 us
    all_gather x1, blocking collectives, shards_of_four(): all_stats = lax.all_gather(stats[:2], 'dp', axis=0)  18.5 us
    unnamed x58, local copies, waits for them, and re-layouts  17.4 us
    all_gather x1, blocking collectives, shards_of_four(): column_parts = lax.all_gather(column_sums, 'dp', axis=0)  14.4 us
  transfers between devices with their start and end apart: 34, of which 10 were waited for; matrix products, arithmetic and copies ran while one was open for 11% of the time, Pallas kernels for 26%

profile of v1, /device:TPU:0, one launch (start us, length us, event | category | flops | bytes accessed | tf_op | source)
XLA Modules:
  0.0 372.8 jit_solution(3274807838643452742)
XLA Ops:
  0.6 3.1 collective-permute-start
  11.8 29.9 %collective-permute-done.4 = f32[4,256]{1,0:T(4,128)S(1)} collective-permute-done((f32[4,256]{1,0:T(4,128)S(1)}, f32[4,256]{1,0:T(4,128)S(1)}, u32[]{:S(2)}, u32[]{:S(2)}) %collective-permute-start.4) | collective-permute-done | bytes 4128 | tf_op jit(solution)/shard_map/ppermute | solution.py:32
  43.3 10.2 %shard_map.110.refs_3_ = bf16[4,256,3072]{2,1,0:T(8,128)(2,1)S(1)} custom-call(bf16[256,3072]{1,0:T(8,128)(2,1)S(1)} %bitcast.141, bf16[3072,3072]{1,0:T(8,128)(2,1)} %bitcast.148), custom_call_target="tpu_custom_call" | custom-call | flops 1 | bytes 1 | tf_op jit(solution)/shard_map/pallas_call | solution.py:111
  53.5 2.7 copy-done.1
  61.5 7.6 %collective-permute-start.8 = (bf16[256,3072]{1,0:T(8,128)(2,1)}, bf16[256,3072]{1,0:T(8,128)(2,1)}, u32[]{:S(2)}, u32[]{:S(2)}) collective-permute-start(bf16[256,3072]{1,0:T(8,128)(2,1)} %fusion.11), channel_id=1, source_target_pairs={{0,4},{12,8},{1,5},{13,9},{2,6},{14,10},{3,7},{15,11},{16,20},{28,... | collective-permute-start | bytes 4718600 | tf_op jit(solution)/shard_map/ppermute | solution.py:288
  73.0 2.8 copy-done.2
  77.2 13.1 %shard_map.111.refs_2_ = bf16[4,256,3072]{2,1,0:T(8,128)(2,1)S(1)} custom-call(bf16[256,3072]{1,0:T(8,128)(2,1)S(1)} %collective-permute-done.2.refs_0_, bf16[256,3072]{1,0:T(8,128)(2,1)S(1)} %copy-done.8, bf16[3072,3072]{1,0:T(8,128)(2,1)} %bitcast.149, bf16[4,256,3072]{2,1,0:T(8,128)(2,1)S(1)} %copy-done.2), custom_call_target="tpu_custom_call", output_to_operand_aliasing={{}: (3, {})} | custom-call | flops 1 | bytes 1 | tf_op jit(solution)/shard_map/pallas_call | solution.py:111
  90.3 18.5 %all-gather.2 = f32[4,2,256]{2,1,0:T(2,128)S(1)} all-gather(f32[1,2,256]{2,1,0:T(2,128)S(1)} %slice_bitcast_fusion.16), channel_id=2, replica_groups=mesh['section'=2,'dp'=4,'mp'=4] {'dp'}, dimensions={0}, use_global_device_ids=true | all-gather | bytes 10240 | tf_op jit(solution)/shard_map/all_gather | solution.py:320
  111.4 10.2 %shard_map.112 = bf16[4,256,3072]{2,1,0:T(8,128)(2,1)S(1)} custom-call(bf16[256,3072]{1,0:T(8,128)(2,1)S(1)} %constant_dynamic-update-slice_fusion.refs_0_, bf16[3072,3072]{1,0:T(8,128)(2,1)} %bitcast.150, bf16[4,256,3072]{2,1,0:T(8,128)(2,1)S(1)} %shard_map.111.refs_2_), custom_call_target="tpu_custom_call", output_to_operand_aliasing={{}: (2, {})} | custom-call | flops 1 | bytes 1 | tf_op jit(solution)/shard_map/pallas_call | solution.py:111
  123.3 4.7 %collective-permute-start.12 = (bf16[256,3072]{1,0:T(8,128)(2,1)S(1)}, bf16[256,3072]{1,0:T(8,128)(2,1)S(1)}, u32[]{:S(2)}, u32[]{:S(2)}) collective-permute-start(bf16[256,3072]{1,0:T(8,128)(2,1)S(1)} %dynamic-slice_bitcast_fusion.8), channel_id=1, source_target_pairs={{0,4},{12,8},{1,5},{13,9},{2,6},{14,10},{3,7},{15,11},{16,20},{28,... | collective-permute-start | bytes 4718600 | tf_op jit(solution)/shard_map/ppermute | solution.py:288
  128.8 4.2 %add_convert_fusion.2 = (bf16[256,3072]{1,0:T(8,128)(2,1)S(1)}, bf16[256,3072]{1,0:T(8,128)(2,1)S(1)}, bf16[256,3072]{1,0:T(8,128)(2,1)S(1)}) fusion(f32[256]{0:T(256)S(1)} %get-tuple-element.191, f32[256]{0:T(256)S(1)} %bitcast.181, bf16[256,3072]{1,0:T(8,128)(2,1)} %collective-permute-done.1, bf16[256,3072]{1,0:T(8,128)(2,1)} %collective-permute-done.7, ...), kind=kLoop, calls=%fused_computation.31 | loop fusion | flops 14942208 | bytes 11040769 | tf_op jit(solution)/shard_map/convert_element_type | solution.py:296
  133.1 18.6 %shard_map.113.refs_2_ = bf16[4,256,3072]{2,1,0:T(8,128)(2,1)S(1)} custom-call(bf16[256,3072]{1,0:T(8,128)(2,1)S(1)} %get-tuple-element.176.refs_0_, bf16[256,3072]{1,0:T(8,128)(2,1)S(1)} %get-tuple-element.177.refs_1_, bf16[256,3072]{1,0:T(8,128)(2,1)S(1)} %get-tuple-element.175.refs_2_, bf16[3072,3072]{1,0:T(8,128)(2,1)} %bitcast.151), custom_call_target="tpu_custom_call" | custom-call | flops 1 | bytes 1 | tf_op jit(solution)/shard_map/pallas_call | solution.py:111
  151.6 4.0 %collective-permute-done.11 = bf16[256,3072]{1,0:T(8,128)(2,1)S(1)} collective-permute-done((bf16[256,3072]{1,0:T(8,128)(2,1)}, bf16[256,3072]{1,0:T(8,128)(2,1)S(1)}, u32[]{:S(2)}, u32[]{:S(2)}) %collective-permute-start.11) | collective-permute-done | bytes 1572896 | tf_op jit(solution)/shard_map/ppermute | solution.py:288
  157.4 6.0 %collective-permute-start.14 = (bf16[256,3072]{1,0:T(8,128)(2,1)S(1)}, bf16[256,3072]{1,0:T(8,128)(2,1)S(1)}, u32[]{:S(2)}, u32[]{:S(2)}) collective-permute-start(bf16[256,3072]{1,0:T(8,128)(2,1)S(1)} %fusion.14), channel_id=1, source_target_pairs={{0,4},{12,8},{1,5},{13,9},{2,6},{14,10},{3,7},{15,11},{16,20},{28,... | collective-permute-start | bytes 4718600 | tf_op jit(solution)/shard_map/ppermute | solution.py:288
  168.0 10.0 %shard_map.114 = bf16[4,256,3072]{2,1,0:T(8,128)(2,1)S(1)} custom-call(bf16[256,3072]{1,0:T(8,128)(2,1)S(1)} %add_convert_fusion.1.refs_0_, bf16[3072,3072]{1,0:T(8,128)(2,1)} %bitcast.152, bf16[4,256,3072]{2,1,0:T(8,128)(2,1)S(1)} %shard_map.113.refs_2_), custom_call_target="tpu_custom_call", output_to_operand_aliasing={{}: (2, {})} | custom-call | flops 1 | bytes 1 | tf_op jit(solution)/shard_map/pallas_call | solution.py:111
  180.4 11.8 %collective-permute-done.14 = bf16[256,3072]{1,0:T(8,128)(2,1)S(1)} collective-permute-done((bf16[256,3072]{1,0:T(8,128)(2,1)S(1)}, bf16[256,3072]{1,0:T(8,128)(2,1)S(1)}, u32[]{:S(2)}, u32[]{:S(2)}) %collective-permute-start.14) | collective-permute-done | bytes 1572896 | tf_op jit(solution)/shard_map/ppermute | solution.py:288
  192.2 7.8 %collective-permute-done.16 = bf16[256,3072]{1,0:T(8,128)(2,1)S(1)} collective-permute-done((bf16[256,3072]{1,0:T(8,128)(2,1)S(1)}, bf16[256,3072]{1,0:T(8,128)(2,1)S(1)}, u32[]{:S(2)}, u32[]{:S(2)}) %collective-permute-start.16) | collective-permute-done | bytes 1572896 | tf_op jit(solution)/shard_map/ppermute | solution.py:288
  214.5 3.3 pad_maximum_fusion.1.c_ref
  217.8 12.2 %collective-permute-done.17 = bf16[256,3072]{1,0:T(8,128)(2,1)} collective-permute-done((bf16[256,3072]{1,0:T(8,128)(2,1)S(1)}, bf16[256,3072]{1,0:T(8,128)(2,1)}, u32[]{:S(2)}, u32[]{:S(2)}) %collective-permute-start.17) | collective-permute-done | bytes 1572896 | tf_op jit(solution)/shard_map/ppermute | solution.py:288
  230.0 3.1 collective-permute-done.20.h1_ref
  233.1 2.9 collective-permute-done.22.h2_ref
  236.0 5.9 %fusion.13 = (f32[3072]{0:T(1024)S(1)}, f32[256]{0:T(256)S(1)}, f32[256]{0:T(256)S(1)}, f32[3072]{0:T(1024)S(1)}, f32[256,3072]{1,0:T(8,128)}) fusion(f32[256]{0:T(256)S(1)} %add_rsqrt_fusion.4, f32[256]{0:T(256)S(1)} %bitcast.163, bf16[1,1,1,256,3072]{4,3,2,1,0:T(8,128)(2,1)S(1)} %copy-done.5, f32[3072]{0:T(1024)S(1)} %bitcast.146, ...), kind=kLoop, calls=%fused_computation.22 | loop fusion | flops 11789824 | bytes 9478148 | tf_op jit(solution)/shard_map/reduce_sum | solution.py:381
  254.0 3.1 shard_map.115
  258.2 8.5 %all-to-all-start = ((bf16[16,64,768]{2,1,0:T(8,128)(2,1)}), bf16[16,64,768]{2,1,0:T(8,128)(2,1)}, u32[]{:S(2)}, u32[]{:S(2)}) async-start(bf16[16,64,768]{2,1,0:T(8,128)(2,1)} %copy-done.13), calls=%async_computation | async-start | bytes 3145728 | tf_op jit(solution)/shard_map/all_to_all | solution.py:387
  272.8 32.2 %collective-permute-done.26 = bf16[256,3072]{1,0:T(8,128)(2,1)} collective-permute-done((bf16[256,3072]{1,0:T(8,128)(2,1)}, bf16[256,3072]{1,0:T(8,128)(2,1)}, u32[]{:S(2)}, u32[]{:S(2)}) %collective-permute-start.26) | collective-permute-done | bytes 1572896 | tf_op jit(solution)/shard_map/ppermute | solution.py:288
  310.3 5.6 %collective-permute-done.29 = bf16[256,768]{1,0:T(8,128)(2,1)S(1)} collective-permute-done((bf16[256,768]{1,0:T(8,128)(2,1)S(1)}, bf16[256,768]{1,0:T(8,128)(2,1)S(1)}, u32[]{:S(2)}, u32[]{:S(2)}) %collective-permute-start.29) | collective-permute-done | bytes 393248 | tf_op jit(solution)/shard_map/ppermute | solution.py:288
  316.0 7.9 %shard_map.116.rest_0_ = f32[3072,3072]{1,0:T(8,128)} custom-call(bf16[1024,768]{1,0:T(8,128)(2,1)S(1)} %pad_maximum_fusion.4.v_ref, bf16[1024,3072]{1,0:T(8,128)(2,1)S(1)} %bitcast.134), custom_call_target="tpu_custom_call" | custom-call | flops 1 | bytes 1 | tf_op jit(solution)/shard_map/pallas_call | solution.py:73
  324.1 7.9 %shard_map.117.rest_0_ = f32[3072,3072]{1,0:T(8,128)} custom-call(bf16[1024,768]{1,0:T(8,128)(2,1)S(1)} %pad_maximum_fusion.5.v_ref, bf16[1024,3072]{1,0:T(8,128)(2,1)S(1)} %bitcast.134, f32[3072,3072]{1,0:T(8,128)} %shard_map.116.rest_0_), custom_call_target="tpu_custom_call", output_to_operand_aliasing={{}: (2, {})} | custom-call | flops 1 | bytes 1 | tf_op jit(solution)/shard_map/pallas_call | solution.py:73
  337.1 2.8 copy-done
  339.9 7.9 %shard_map.118.rest_0_ = f32[3072,3072]{1,0:T(8,128)} custom-call(bf16[1024,768]{1,0:T(8,128)(2,1)S(1)} %pad_maximum_fusion.6.v_ref, bf16[1024,3072]{1,0:T(8,128)(2,1)S(1)} %copy-done, f32[3072,3072]{1,0:T(8,128)} %shard_map.117.rest_0_), custom_call_target="tpu_custom_call", output_to_operand_aliasing={{}: (2, {})} | custom-call | flops 1 | bytes 1 | tf_op jit(solution)/shard_map/pallas_call | solution.py:73
  348.0 7.9 %shard_map.119 = f32[3072,3072]{1,0:T(8,128)} custom-call(bf16[1024,768]{1,0:T(8,128)(2,1)S(1)} %pad_maximum_fusion.7.v_ref, bf16[1024,3072]{1,0:T(8,128)(2,1)S(1)} %copy-done, f32[3072,3072]{1,0:T(8,128)} %shard_map.118.rest_0_), custom_call_target="tpu_custom_call", output_to_operand_aliasing={{}: (2, {})} | custom-call | flops 1 | bytes 1 | tf_op jit(solution)/shard_map/pallas_call | solution.py:73
  355.9 14.4 %all-gather.3 = f32[4,2,3072]{2,1,0:T(2,128)S(1)} all-gather(f32[1,2,3072]{2,1,0:T(2,128)S(1)} %bitcast.158), channel_id=3, replica_groups=mesh['section'=2,'dp'=4,'mp'=4] {'dp'}, dimensions={0}, use_global_device_ids=true | all-gather | bytes 122880 | tf_op jit(solution)/shard_map/all_gather | solution.py:413
  (168 shorter events, 80.7 us)
Async XLA Ops:
  0.6 55.6 %collective-permute-start = (bf16[256,3072]{1,0:T(8,128)(2,1)}, bf16[256,3072]{1,0:T(8,128)(2,1)}, u32[]{:S(2)}, u32[]{:S(2)}) collective-permute-start(bf16[256,3072]{1,0:T(8,128)(2,1)} %bitcast.153), channel_id=1, source_target_pairs={{0,4},{4,0},{8,12},{12,8},{1,5},{5,1},{9,13},{13,9},{2,6},{6,2},{1... | collective-permute-start | bytes 4718600 | tf_op jit(solution)/shard_map/ppermute | solution.py:288
  3.7 52.5 %collective-permute-start.1 = (bf16[256,3072]{1,0:T(8,128)(2,1)}, bf16[256,3072]{1,0:T(8,128)(2,1)}, u32[]{:S(2)}, u32[]{:S(2)}) collective-permute-start(bf16[256,3072]{1,0:T(8,128)(2,1)} %bitcast.154), channel_id=1, source_target_pairs={{4,8},{8,4},{5,9},{9,5},{6,10},{10,6},{7,11},{11,7},{20,24},{24,20... | collective-permute-start | bytes 4718600 | tf_op jit(solution)/shard_map/ppermute | solution.py:288
  5.6 50.7 %collective-permute-start.2 = (bf16[256,3072]{1,0:T(8,128)(2,1)}, bf16[256,3072]{1,0:T(8,128)(2,1)S(1)}, u32[]{:S(2)}, u32[]{:S(2)}) collective-permute-start(bf16[256,3072]{1,0:T(8,128)(2,1)} %bitcast.139), channel_id=1, source_target_pairs={{0,1},{1,0},{2,3},{3,2},{4,5},{5,4},{6,7},{7,6},{8,9},{9,8},{10,11... | collective-permute-start | bytes 4718600 | tf_op jit(solution)/shard_map/ppermute | solution.py:32
  7.1 49.2 %collective-permute-start.3 = (bf16[256,3072]{1,0:T(8,128)(2,1)}, bf16[256,3072]{1,0:T(8,128)(2,1)S(1)}, u32[]{:S(2)}, u32[]{:S(2)}) collective-permute-start(bf16[256,3072]{1,0:T(8,128)(2,1)} %bitcast.140), channel_id=1, source_target_pairs={{0,2},{1,3},{2,0},{3,1},{4,6},{5,7},{6,4},{7,5},{8,10},{9,11},{10,... | collective-permute-start | bytes 4718600 | tf_op jit(solution)/shard_map/ppermute | solution.py:32
  11.2 30.5 %collective-permute-start.4 = (f32[4,256]{1,0:T(4,128)S(1)}, f32[4,256]{1,0:T(4,128)S(1)}, u32[]{:S(2)}, u32[]{:S(2)}) collective-permute-start(f32[4,256]{1,0:T(4,128)S(1)} %pad_maximum_fusion.17), channel_id=1, source_target_pairs={{0,1},{1,0},{2,3},{3,2},{4,5},{5,4},{6,7},{7,6},{8,9},{9,8},{10,11... | collective-permute-start | bytes 12296 | tf_op jit(solution)/shard_map/ppermute | solution.py:32
  41.7 14.5 %collective-permute-start.5 = (f32[4,256]{1,0:T(4,128)S(1)}, f32[4,256]{1,0:T(4,128)S(1)}, u32[]{:S(2)}, u32[]{:S(2)}) collective-permute-start(f32[4,256]{1,0:T(4,128)S(1)} %fusion.37), channel_id=1, source_target_pairs={{0,2},{1,3},{2,0},{3,1},{4,6},{5,7},{6,4},{7,5},{8,10},{9,11},{10,... | collective-permute-start | bytes 12296 | tf_op jit(solution)/shard_map/ppermute | solution.py:32
  56.3 65.2 %collective-permute-start.6 = (bf16[256,3072]{1,0:T(8,128)(2,1)}, bf16[256,3072]{1,0:T(8,128)(2,1)}, u32[]{:S(2)}, u32[]{:S(2)}) collective-permute-start(bf16[256,3072]{1,0:T(8,128)(2,1)} %collective-permute-done), channel_id=1, source_target_pairs={{4,8},{8,4},{5,9},{9,5},{6,10},{10,6},{7,11},{11,7},{20,24},{24,20... | collective-permute-start | bytes 4718600 | tf_op jit(solution)/shard_map/ppermute | solution.py:288
  58.2 63.4 %collective-permute-start.7 = (bf16[256,3072]{1,0:T(8,128)(2,1)}, bf16[256,3072]{1,0:T(8,128)(2,1)}, u32[]{:S(2)}, u32[]{:S(2)}) collective-permute-start(bf16[256,3072]{1,0:T(8,128)(2,1)} %collective-permute-done.1), channel_id=1, source_target_pairs={{4,0},{8,12},{5,1},{9,13},{6,2},{10,14},{7,3},{11,15},{20,16},{24,... | collective-permute-start | bytes 4718600 | tf_op jit(solution)/shard_map/ppermute | solution.py:288
  61.5 60.1 %collective-permute-start.8 = (bf16[256,3072]{1,0:T(8,128)(2,1)}, bf16[256,3072]{1,0:T(8,128)(2,1)}, u32[]{:S(2)}, u32[]{:S(2)}) collective-permute-start(bf16[256,3072]{1,0:T(8,128)(2,1)} %fusion.11), channel_id=1, source_target_pairs={{0,4},{12,8},{1,5},{13,9},{2,6},{14,10},{3,7},{15,11},{16,20},{28,... | collective-permute-start | bytes 4718600 | tf_op jit(solution)/shard_map/ppermute | solution.py:288
  70.1 38.8 %collective-permute-start.9 = (bf16[256,1536]{1,0:T(8,128)(2,1)}, bf16[256,1536]{1,0:T(8,128)(2,1)}, u32[]{:S(2)}, u32[]{:S(2)}) collective-permute-start(bf16[256,1536]{1,0:T(8,128)(2,1)} %slice.202), channel_id=1, source_target_pairs={{0,2},{1,3},{2,0},{3,1},{4,6},{5,7},{6,4},{7,5},{8,10},{9,11},{10,... | collective-permute-start | bytes 2359304 | tf_op jit(solution)/shard_map/ppermute | solution.py:32
  71.5 38.6 %collective-permute-start.10 = (bf16[256,1536]{1,0:T(8,128)(2,1)}, bf16[256,1536]{1,0:T(8,128)(2,1)}, u32[]{:S(2)}, u32[]{:S(2)}) collective-permute-start(bf16[256,1536]{1,0:T(8,128)(2,1)} %slice.203), channel_id=1, source_target_pairs={{0,1},{1,0},{2,3},{3,2},{4,5},{5,4},{6,7},{7,6},{8,9},{9,8},{10,11... | collective-permute-start | bytes 2359304 | tf_op jit(solution)/shard_map/ppermute | solution.py:32
  121.6 34.0 %collective-permute-start.11 = (bf16[256,3072]{1,0:T(8,128)(2,1)}, bf16[256,3072]{1,0:T(8,128)(2,1)S(1)}, u32[]{:S(2)}, u32[]{:S(2)}) collective-permute-start(bf16[256,3072]{1,0:T(8,128)(2,1)} %collective-permute-done.6), channel_id=1, source_target_pairs={{4,0},{8,12},{5,1},{9,13},{6,2},{10,14},{7,3},{11,15},{20,16},{24,... | collective-permute-start | bytes 4718600 | tf_op jit(solution)/shard_map/ppermute | solution.py:288
  123.3 33.5 %collective-permute-start.12 = (bf16[256,3072]{1,0:T(8,128)(2,1)S(1)}, bf16[256,3072]{1,0:T(8,128)(2,1)S(1)}, u32[]{:S(2)}, u32[]{:S(2)}) collective-permute-start(bf16[256,3072]{1,0:T(8,128)(2,1)S(1)} %dynamic-slice_bitcast_fusion.8), channel_id=1, source_target_pairs={{0,4},{12,8},{1,5},{13,9},{2,6},{14,10},{3,7},{15,11},{16,20},{28,... | collective-permute-start | bytes 4718600 | tf_op jit(solution)/shard_map/ppermute | solution.py:288
  128.0 28.8 %collective-permute-start.13 = (bf16[256,3072]{1,0:T(8,128)(2,1)}, bf16[256,3072]{1,0:T(8,128)(2,1)S(1)}, u32[]{:S(2)}, u32[]{:S(2)}) collective-permute-start(bf16[256,3072]{1,0:T(8,128)(2,1)} %collective-permute-done.8), channel_id=1, source_target_pairs={{4,8},{8,4},{5,9},{9,5},{6,10},{10,6},{7,11},{11,7},{20,24},{24,20... | collective-permute-start | bytes 4718600 | tf_op jit(solution)/shard_map/ppermute | solution.py:288
  157.4 34.8 %collective-permute-start.14 = (bf16[256,3072]{1,0:T(8,128)(2,1)S(1)}, bf16[256,3072]{1,0:T(8,128)(2,1)S(1)}, u32[]{:S(2)}, u32[]{:S(2)}) collective-permute-start(bf16[256,3072]{1,0:T(8,128)(2,1)S(1)} %fusion.14), channel_id=1, source_target_pairs={{0,4},{12,8},{1,5},{13,9},{2,6},{14,10},{3,7},{15,11},{16,20},{28,... | collective-permute-start | bytes 4718600 | tf_op jit(solution)/shard_map/ppermute | solution.py:288
  163.4 28.8 %collective-permute-start.15 = (bf16[256,3072]{1,0:T(8,128)(2,1)S(1)}, bf16[256,3072]{1,0:T(8,128)(2,1)S(1)}, u32[]{:S(2)}, u32[]{:S(2)}) collective-permute-start(bf16[256,3072]{1,0:T(8,128)(2,1)S(1)} %fusion.14), channel_id=1, source_target_pairs={{4,8},{8,4},{5,9},{9,5},{6,10},{10,6},{7,11},{11,7},{20,24},{24,20... | collective-permute-start | bytes 4718600 | tf_op jit(solution)/shard_map/ppermute | solution.py:288
  164.2 35.8 %collective-permute-start.16 = (bf16[256,3072]{1,0:T(8,128)(2,1)S(1)}, bf16[256,3072]{1,0:T(8,128)(2,1)S(1)}, u32[]{:S(2)}, u32[]{:S(2)}) collective-permute-start(bf16[256,3072]{1,0:T(8,128)(2,1)S(1)} %collective-permute-done.13), channel_id=1, source_target_pairs={{4,0},{8,12},{5,1},{9,13},{6,2},{10,14},{7,3},{11,15},{20,16},{24,... | collective-permute-start | bytes 4718600 | tf_op jit(solution)/shard_map/ppermute | solution.py:288
  178.3 27.5 %collective-permute-start.19 = (bf16[256,1536]{1,0:T(8,128)(2,1)S(1)}, bf16[256,1536]{1,0:T(8,128)(2,1)S(1)}, u32[]{:S(2)}, u32[]{:S(2)}) collective-permute-start(bf16[256,1536]{1,0:T(8,128)(2,1)S(1)} %get-tuple-element.166), channel_id=1, source_target_pairs={{0,2},{1,3},{2,0},{3,1},{4,6},{5,7},{6,4},{7,5},{8,10},{9,11},{10,... | collective-permute-start | bytes 2359304 | tf_op jit(solution)/shard_map/ppermute | solution.py:32
  178.9 30.0 %collective-permute-start.21 = (bf16[256,1536]{1,0:T(8,128)(2,1)S(1)}, bf16[256,1536]{1,0:T(8,128)(2,1)S(1)}, u32[]{:S(2)}, u32[]{:S(2)}) collective-permute-start(bf16[256,1536]{1,0:T(8,128)(2,1)S(1)} %get-tuple-element.165), channel_id=1, source_target_pairs={{0,1},{1,0},{2,3},{3,2},{4,5},{5,4},{6,7},{7,6},{8,9},{9,8},{10,11... | collective-permute-start | bytes 2359304 | tf_op jit(solution)/shard_map/ppermute | solution.py:32
  200.6 29.5 %collective-permute-start.17 = (bf16[256,3072]{1,0:T(8,128)(2,1)S(1)}, bf16[256,3072]{1,0:T(8,128)(2,1)}, u32[]{:S(2)}, u32[]{:S(2)}) collective-permute-start(bf16[256,3072]{1,0:T(8,128)(2,1)S(1)} %fusion.15), channel_id=1, source_target_pairs={{0,4},{4,0},{8,12},{12,8},{1,5},{5,1},{9,13},{13,9},{2,6},{6,2},{1... | collective-permute-start | bytes 4718600 | tf_op jit(solution)/shard_map/ppermute | solution.py:288
  202.4 27.7 %collective-permute-start.18 = (bf16[256,3072]{1,0:T(8,128)(2,1)}, bf16[256,3072]{1,0:T(8,128)(2,1)}, u32[]{:S(2)}, u32[]{:S(2)}) collective-permute-start(bf16[256,3072]{1,0:T(8,128)(2,1)} %add_convert_fusion), channel_id=1, source_target_pairs={{4,8},{8,4},{5,9},{9,5},{6,10},{10,6},{7,11},{11,7},{20,24},{24,20... | collective-permute-start | bytes 4718600 | tf_op jit(solution)/shard_map/ppermute | solution.py:288
  207.4 25.7 %collective-permute-start.20 = (bf16[256,3072]{1,0:T(8,128)(2,1)}, bf16[256,3072]{1,0:T(8,128)(2,1)S(1)}, u32[]{:S(2)}, u32[]{:S(2)}) collective-permute-start(bf16[256,3072]{1,0:T(8,128)(2,1)} %pad_maximum_fusion.2), channel_id=1, source_target_pairs={{0,1},{1,0},{2,3},{3,2},{4,5},{5,4},{6,7},{7,6},{8,9},{9,8},{10,11... | collective-permute-start | bytes 4718600 | tf_op jit(solution)/shard_map/ppermute | solution.py:32
  210.6 25.5 %collective-permute-start.22 = (bf16[256,3072]{1,0:T(8,128)(2,1)}, bf16[256,3072]{1,0:T(8,128)(2,1)S(1)}, u32[]{:S(2)}, u32[]{:S(2)}) collective-permute-start(bf16[256,3072]{1,0:T(8,128)(2,1)} %pad_maximum_fusion.3), channel_id=1, source_target_pairs={{0,2},{1,3},{2,0},{3,1},{4,6},{5,7},{6,4},{7,5},{8,10},{9,11},{10,... | collective-permute-start | bytes 4718600 | tf_op jit(solution)/shard_map/ppermute | solution.py:32
  242.0 7.0 %collective-permute-start.25 = (f32[2,256]{1,0:T(2,128)S(1)}, f32[2,256]{1,0:T(2,128)S(1)}, u32[]{:S(2)}, u32[]{:S(2)}) collective-permute-start(f32[2,256]{1,0:T(2,128)S(1)} %pad_maximum_fusion.19), channel_id=1, source_target_pairs={{0,3},{1,0},{2,1},{3,2},{4,7},{5,4},{6,5},{7,6},{8,11},{9,8},{10,9... | collective-permute-start | bytes 6152 | tf_op jit(solution)/shard_map/ppermute | solution.py:22
  244.6 24.3 %collective-permute-start.27 = (bf16[256,3072]{1,0:T(8,128)(2,1)}, bf16[256,3072]{1,0:T(8,128)(2,1)}, u32[]{:S(2)}, u32[]{:S(2)}) collective-permute-start(bf16[256,3072]{1,0:T(8,128)(2,1)} %fusion.11), channel_id=1, source_target_pairs={{4,8},{8,4},{5,9},{9,5},{6,10},{10,6},{7,11},{11,7},{20,24},{24,20... | collective-permute-start | bytes 4718600 | tf_op jit(solution)/shard_map/ppermute | solution.py:288
  247.7 57.4 %collective-permute-start.26 = (bf16[256,3072]{1,0:T(8,128)(2,1)}, bf16[256,3072]{1,0:T(8,128)(2,1)}, u32[]{:S(2)}, u32[]{:S(2)}) collective-permute-start(bf16[256,3072]{1,0:T(8,128)(2,1)} %fusion.11), channel_id=1, source_target_pairs={{4,0},{8,12},{5,1},{9,13},{6,2},{10,14},{7,3},{11,15},{20,16},{24,... | collective-permute-start | bytes 4718600 | tf_op jit(solution)/shard_map/ppermute | solution.py:288
  258.2 73.9 %all-to-all-start = ((bf16[16,64,768]{2,1,0:T(8,128)(2,1)}), bf16[16,64,768]{2,1,0:T(8,128)(2,1)}, u32[]{:S(2)}, u32[]{:S(2)}) async-start(bf16[16,64,768]{2,1,0:T(8,128)(2,1)} %copy-done.13), calls=%async_computation | async-start | bytes 3145728 | tf_op jit(solution)/shard_map/all_to_all | solution.py:387
  271.4 44.4 %collective-permute-start.29 = (bf16[256,768]{1,0:T(8,128)(2,1)S(1)}, bf16[256,768]{1,0:T(8,128)(2,1)S(1)}, u32[]{:S(2)}, u32[]{:S(2)}) collective-permute-start(bf16[256,768]{1,0:T(8,128)(2,1)S(1)} %get-tuple-element.91), channel_id=1, source_target_pairs={{4,0},{8,12},{5,1},{9,13},{6,2},{10,14},{7,3},{11,15},{20,16},{24,... | collective-permute-start | bytes 1179656 | tf_op jit(solution)/shard_map/ppermute | solution.py:288
  307.5 16.5 %collective-permute-start.28 = (bf16[256,768]{1,0:T(8,128)(2,1)S(1)}, bf16[256,768]{1,0:T(8,128)(2,1)S(1)}, u32[]{:S(2)}, u32[]{:S(2)}) collective-permute-start(bf16[256,768]{1,0:T(8,128)(2,1)S(1)} %get-tuple-element.87), channel_id=1, source_target_pairs={{4,0},{8,12},{5,1},{9,13},{6,2},{10,14},{7,3},{11,15},{20,16},{24,... | collective-permute-start | bytes 1179656 | tf_op jit(solution)/shard_map/ppermute | solution.py:288
  308.8 26.1 %collective-permute-start.32 = (bf16[256,768]{1,0:T(8,128)(2,1)}, bf16[256,768]{1,0:T(8,128)(2,1)}, u32[]{:S(2)}, u32[]{:S(2)}) collective-permute-start(bf16[256,768]{1,0:T(8,128)(2,1)} %get-tuple-element.106), channel_id=1, source_target_pairs={{4,0},{8,12},{5,1},{9,13},{6,2},{10,14},{7,3},{11,15},{20,16},{24,... | collective-permute-start | bytes 1179656 | tf_op jit(solution)/shard_map/ppermute | solution.py:288
  332.0 38.8 %collective-permute-start.30 = (bf16[16,64,768]{2,1,0:T(8,128)(2,1)}, bf16[16,64,768]{2,1,0:T(8,128)(2,1)S(1)}, u32[]{:S(2)}, u32[]{:S(2)}) collective-permute-start(bf16[16,64,768]{2,1,0:T(8,128)(2,1)} %all-to-all-done), channel_id=1, source_target_pairs={{0,16},{16,0},{1,17},{17,1},{2,18},{18,2},{3,19},{19,3},{4,20},{20... | collective-permute-start | bytes 4718600 | tf_op jit(solution)/shard_map/ppermute | solution.py:32
  333.6 14.2 %collective-permute-start.31 = (bf16[256,768]{1,0:T(8,128)(2,1)}, bf16[256,768]{1,0:T(8,128)(2,1)S(1)}, u32[]{:S(2)}, u32[]{:S(2)}) collective-permute-start(bf16[256,768]{1,0:T(8,128)(2,1)} %get-tuple-element.102), channel_id=1, source_target_pairs={{4,0},{8,12},{5,1},{9,13},{6,2},{10,14},{7,3},{11,15},{20,16},{24,... | collective-permute-start | bytes 1179656 | tf_op jit(solution)/shard_map/ppermute | solution.py:288
  (30 other events, 321.4 us)

commit v2 on v1

--- a/solution.py
+++ b/solution.py
@@ -8,42 +8,12 @@
 from jax.sharding import PartitionSpec as P
 
 eps = 1e-05
-V_CHUNKS = 4
 LIGHT = pl.CostEstimate(flops=1, bytes_accessed=1, transcendentals=0)
-
-
-def after(value, *others):
-    return lax.optimization_barrier((value,) + others)[0]
-
-
-def ring_total(value, axis):
-    n = lax.axis_size(axis)
-    parts = [
-        lax.ppermute(value, axis, [(s, (s + k) % n) for s in range(n)]) for k in range(1, n)
-    ]
-    total = value
-    for part in parts:
-        total = total + part
-    return total
 
 
 def flip(value, axis, mask):
     n = lax.axis_size(axis)
     return lax.ppermute(value, axis, [(s, s ^ mask) for s in range(n)])
-
-
-def pieces_of(matrix, groups, swapped):
-    rows, cols = matrix.shape[0] // groups, matrix.shape[1] // groups
-    cut = lambda r, c: matrix[r * rows:(r + 1) * rows, c * cols:(c + 1) * cols]
-    pairs = [(a, b) for a in range(groups) for b in range(groups)]
-    return jnp.stack([cut(b, a) if swapped else cut(a, b) for a, b in pairs])
-
-
-def matrix_of(pieces, groups, swapped):
-    at = lambda r, c: pieces[c * groups + r] if swapped else pieces[r * groups + c]
-    return jnp.concatenate(
-        [jnp.concatenate([at(r, c) for c in range(groups)], 1) for r in range(groups)], 0
-    )
 
 
 def grad_kernel(v_ref, c_ref, *rest):
@@ -84,30 +54,45 @@
 
 
 def share_kernel(count, turned, *refs):
-    w_ref, out_ref = refs[count], refs[-1]
-    dims = (((1,), (1 if turned else 0,)), ((), ()))
+    w_ref, out_ref = refs[2 * count], refs[-1]
+    half = refs[0].shape[1]
     for k in range(count):
-        out_ref[k] = lax.dot_general(
-            refs[k][...], w_ref[...], dims, preferred_element_type=jnp.float32
-        ).astype(jnp.bfloat16)
+        total = None
+        for side in range(2):
+            cut = pl.ds(side * half, half)
+            part = lax.dot_general(
+                refs[2 * k + side][...],
+                w_ref[:, cut] if turned else w_ref[cut, :],
+                (((1,), (1 if turned else 0,)), ((), ())),
+                preferred_element_type=jnp.float32,
+            )
+            total = part if total is None else total + part
+        out_ref[k] = total.astype(jnp.bfloat16)
 
 
 def shares(blocks, w, turned, filled, at, total):
     count = len(blocks)
-    rows, depth = blocks[0].shape
+    halves = []
+    for block in blocks:
+        halves += list(block) if isinstance(block, tuple) else [(block, 0), (block, 1)]
+    rows = halves[0][0].shape[0]
+    depth = w.shape[1] if turned else w.shape[0]
     cols = w.shape[0] if turned else w.shape[1]
     step = 512
-    specs = [pl.BlockSpec((rows, depth), lambda j: (0, 0))] * count
+    specs = [
+        pl.BlockSpec((rows, depth // 2), functools.partial(lambda side, j: (0, side), side))
+        for array, side in halves
+    ]
     if turned:
         specs.append(pl.BlockSpec((step, depth), lambda j: (j, 0)))
     else:
         specs.append(pl.BlockSpec((depth, step), lambda j: (0, j)))
-    operands = list(blocks) + [w]
+    operands = [array for array, side in halves] + [w]
     aliases = {}
     if filled is not None:
         specs.append(pl.BlockSpec(memory_space=pl.ANY))
         operands.append(filled)
-        aliases = {count + 1: 0}
+        aliases = {2 * count + 1: 0}
     return pl.pallas_call(
         functools.partial(share_kernel, count, turned),
         grid=(cols // step,),
@@ -120,7 +105,7 @@
     )(*operands)
 
 
-def boundary_kernel(g_ref, kept_ref, columns_ref, gain_ref, h_ref, h1_ref, h2_ref, bias_ref, section_ref, passed_ref, out_ref):
+def boundary_kernel(upper_ref, lower_ref, kept_ref, columns_ref, gain_ref, h_ref, bias_ref, section_ref, passed_ref, out_ref):
     step = pl.program_id(0)
     first = section_ref[0] == 0
     groups = pl.num_programs(0)
@@ -131,17 +116,17 @@
     for f in range(out_ref.shape[0] // 4):
         cut = pl.ds(f * width, width)
         hat = (kept_ref[:, cut].astype(f32) - mean) * inverse
-        grad = (inverse * (g_ref[:, cut] * gain_ref[:, cut] - one - hat * two)).astype(jnp.bfloat16)
-        summed = h_ref[:, cut].astype(f32) + h1_ref[:, cut].astype(f32) + h2_ref[:, cut].astype(f32)
-        output = (summed + bias_ref[:, cut]).astype(jnp.bfloat16)
+        rows = jnp.where(step < 2, upper_ref[:, cut], lower_ref[:, cut])
+        grad = (inverse * (rows * gain_ref[:, cut] - one - hat * two)).astype(jnp.bfloat16)
+        output = (h_ref[:, cut].astype(f32) + bias_ref[:, cut]).astype(jnp.bfloat16)
         passed_ref[:, cut] = jnp.where(first, grad, output)
         out_ref[jnp.where(first, step * groups + f, f * groups + step)] = jnp.where(
             first, output, grad
         )
 
 
-def boundary(grad_rows, kept_rows, columns, gain, h0, h1, h2, bias, section):
-    rows, cols = grad_rows.shape
+def boundary(upper, lower, kept_rows, columns, gain, summed, bias, section):
+    rows, cols = kept_rows.shape
     part = rows // 4
     wide = pl.BlockSpec((part, cols), lambda j: (j, 0))
     line = pl.BlockSpec((1, cols), lambda j: (0, 0))
@@ -149,7 +134,9 @@
         boundary_kernel,
         grid=(4,),
         in_specs=[
-            wide, wide, pl.BlockSpec((part, 4), lambda j: (j, 0)), line, wide, wide, wide, line,
+            pl.BlockSpec((part, cols), lambda j: (jnp.minimum(j, 1), 0)),
+            pl.BlockSpec((part, cols), lambda j: (jnp.maximum(j - 2, 0), 0)),
+            wide, pl.BlockSpec((part, 4), lambda j: (j, 0)), line, wide, line,
             pl.BlockSpec(memory_space=pltpu.SMEM),
         ],
         out_specs=[wide, pl.BlockSpec((16, part, cols // 4), lambda j: (0, 0, 0))],
@@ -160,9 +147,33 @@
         compiler_params=pltpu.CompilerParams(vmem_limit_bytes=32 * 2**20),
         cost_estimate=LIGHT,
     )(
-        grad_rows, kept_rows, columns, gain.reshape(1, cols), h0, h1, h2, bias.reshape(1, cols),
+        upper, lower, kept_rows, columns, gain.reshape(1, cols), summed, bias.reshape(1, cols),
         section.reshape(1),
     )
+
+
+def joined_kernel(pieces_ref, section_ref, out_ref):
+    step = pl.program_id(0)
+    width = pieces_ref.shape[2]
+    for c in range(4):
+        piece = jnp.where(section_ref[0] == 0, step * 4 + c, c * 4 + step)
+        out_ref[:, pl.ds(c * width, width)] = pieces_ref[piece]
+
+
+def joined(pieces, section):
+    count, part, width = pieces.shape
+    return pl.pallas_call(
+        joined_kernel,
+        grid=(4,),
+        in_specs=[
+            pl.BlockSpec((count, part, width), lambda j: (0, 0, 0)),
+            pl.BlockSpec(memory_space=pltpu.SMEM),
+        ],
+        out_specs=pl.BlockSpec((part, 4 * width), lambda j: (j, 0)),
+        out_shape=jax.ShapeDtypeStruct((4 * part, 4 * width), pieces.dtype),
+        compiler_params=pltpu.CompilerParams(vmem_limit_bytes=32 * 2**20),
+        cost_estimate=LIGHT,
+    )(pieces, section.reshape(1))
 
 
 def from_partner(value, axis, stride):
@@ -298,70 +309,101 @@
     def added(one, two):
         return (one.astype(f32) + two.astype(f32)).astype(bf16)
 
+    seq = lambda *values: lax.optimization_barrier(values)
+
     u1a, u1b = along(fresh_rows, PAIRS), along(fresh_rows, MIDDLE)
-    c1, c2 = flip(upstream, "mp", 1), flip(upstream, "mp", 2)
+    c_left, c_right = upstream[:, :half], upstream[:, half:]
+    c1_left, c2_right = flip(c_left, "mp", 1), flip(c_right, "mp", 2)
     fresh, kept = fresh_rows.astype(f32), kept_rows.astype(f32)
     sums = jnp.stack(
         [jnp.sum(fresh, 1), jnp.sum(fresh * fresh, 1), jnp.sum(kept, 1), jnp.sum(kept * kept, 1)]
     )
-    sums = sums + flip(sums, "mp", 1)
+    other = flip(sums, "mp", 1)
+    g_stack = shares([upstream], w, True, None, 3, 4)
+    c1_left, c2_right, sums, other, g_stack = seq(c1_left, c2_right, sums, other, g_stack)
+    c_from_one = flip(jnp.concatenate([c_right, c2_right], 1), "mp", 1)
+    c_from_two = flip(jnp.concatenate([c_left, c1_left], 1), "mp", 2)
+    sums = sums + other
     stats = (sums + flip(sums, "mp", 2)) / full_width
-    g_stack = shares([upstream], w, True, None, 2, 4)
-    u1a, u1b, c1, c2, stats, g_stack = lax.optimization_barrier(
-        (u1a, u1b, c1, c2, stats, g_stack)
-    )
-
-    u2in, u2out = along(u1a, MIDDLE), along(u1b, OUTWARD)
-    c3l, c3r = flip(c1[:, :half], "mp", 2), flip(c2[:, half:], "mp", 1)
     kept_hat, kept_inv = standardize(kept_rows, stats[2], stats[3])
     normed_kept = affine(kept_hat)
-    far1 = along(normed_kept, INWARD)
-    g_stack = shares([c1, c2], w, True, g_stack, 0, 4)
-    all_stats = lax.all_gather(stats[:2], "dp", axis=0)
-    c3 = jnp.concatenate([c3l, c3r], 1)
-    g_stack = shares([c3], w, True, g_stack, 3, 4)
-    u2in, u2out, far1, g_stack = lax.optimization_barrier((u2in, u2out, far1, g_stack))
-
-    def g_block(k):
-        apart = lax.bitwise_xor(lax.bitwise_xor(dp, mp), k)
-        return pick(g_stack, jnp.where(apart == 0, 2, jnp.where(apart == 3, 3, apart - 1)))
-
-    u3 = along(u2in, OUTWARD)
-    r1 = along(g_block(3), INWARD)
-    far2 = along(far1, MIDDLE)
-
-    def normed(rows, block):
-        row_stats = pick(all_stats, block)
+
+    def normed(rows, row_stats):
         hat, unused = standardize(rows, row_stats[0], row_stats[1])
         return affine(hat)
 
-    n0 = normed(fresh_rows, dp)
-    n1 = normed(u1a, lax.bitwise_xor(dp, 1))
-    n2 = normed(jnp.where(inner, u1b, u2out), jnp.where(inner, dp ^ 3, dp ^ 2))
-    h_stack = shares([n0, n1, n2], w, False, None, 0, 4)
-    u3, r1, far2, h_stack = lax.optimization_barrier((u3, r1, far2, h_stack))
-
-    x2 = added(g_block(2), r1)
-    r2out, r2in = along(x2, INWARD), along(x2, MIDDLE)
-    far3 = along(far2, OUTWARD)
-    n3 = normed(jnp.where(inner, u2in, u3), jnp.where(inner, dp ^ 2, dp ^ 3))
-    h_stack = shares([n3], w, False, h_stack, 3, 4)
-
-    def h_block(k):
+    pair_stats = jnp.stack([stats[:2], along(stats[:2], PAIRS)])
+    h_stack = shares([normed(fresh_rows, stats)], w, False, None, 0, 4)
+    u1a, u1b, normed_kept, h_stack = seq(u1a, u1b, normed_kept, h_stack)
+
+    sides = [slice(0, row_count // 2), slice(row_count // 2, row_count)]
+    either = lambda from_inner, from_outer: jnp.where(inner, from_inner, from_outer)
+    a1, b1, a2, b2, a3, b3, a4, b4, a5, b5, x2 = ([None, None] for unused in range(11))
+
+    for k in range(2):
+        a1[k] = along(either(u1b[sides[k]], normed_kept[sides[k]]), PAIRS)
+        b1[k] = along(u1a[sides[k]], MIDDLE)
+    h_stack = shares([normed(u1a, pair_stats[1])], w, False, h_stack, 1, 4)
+
+    a1[0], b1[0], h_stack, c1_left, c2_right = seq(a1[0], b1[0], h_stack, c1_left, c2_right)
+    a2[0], b2[0] = along(b1[0], OUTWARD), along(a1[0], MIDDLE)
+    g_stack = shares(
+        [((c1_left, 0), (c_from_one, 0)), ((c_from_two, 0), (c2_right, 0))], w, True, g_stack, 0, 4
+    )
+    a1[1], b1[1], g_stack = seq(a1[1], b1[1], g_stack)
+    a2[1], b2[1] = along(b1[1], OUTWARD), along(a1[1], MIDDLE)
+    pair_stats = seq(pair_stats, b1[1])[0]
+    all_stats = jnp.concatenate([pair_stats, along(pair_stats, [(s, s ^ 2) for s in range(4)])])
+    g_stack = shares([((c_from_two, 1), (c_from_one, 1))], w, True, g_stack, 2, 4)
+
+    def g_block(k, side):
         apart = lax.bitwise_xor(lax.bitwise_xor(dp, mp), k)
+        at = jnp.where(apart == 0, 3, apart - 1)
+        return lax.dynamic_slice(
+            g_stack, (at, side.start, 0), (1, side.stop - side.start, col_count)
+        )[0]
+
+    a2[0], b2[0], g_stack, normed_kept = seq(a2[0], b2[0], g_stack, normed_kept)
+    sent, h_stack = seq(either(b2[0], g_block(3, sides[0])), h_stack)
+    a3[0] = along(sent, PAIRS)
+    b3[0] = along(normed_kept[sides[0]], MIDDLE)
+    all_stats, h_stack = seq(all_stats, h_stack)
+    u2 = jnp.where(inner, u1b, jnp.concatenate(a1))
+    h_stack = shares([normed(u2, pick(all_stats, jnp.where(inner, 3, 2)))], w, False, h_stack, 2, 4)
+    a2[1], b2[1], h_stack, normed_kept = seq(a2[1], b2[1], h_stack, normed_kept)
+    sent, h_stack = seq(either(b2[1], g_block(3, sides[1])), h_stack)
+    a3[1] = along(sent, PAIRS)
+    b3[1] = along(normed_kept[sides[1]], MIDDLE)
+    u3 = jnp.where(inner, jnp.concatenate(b1), jnp.concatenate(a2))
+    h_stack = shares([normed(u3, pick(all_stats, jnp.where(inner, 2, 3)))], w, False, h_stack, 3, 4)
+
+    nothing = jnp.zeros((row_count // 2, col_count), bf16)
+
+    def fourth(k, chain):
+        x2[k] = added(g_block(2, sides[k]), jnp.where(inner, a3[k], nothing))
+        sent, x2[k], chain = seq(either(normed_kept[sides[k]], x2[k]), x2[k], chain)
+        a4[k], b4[k] = along(sent, PAIRS), along(x2[k], MIDDLE)
+        return chain
+
+    a3[0], b3[0], h_stack = seq(a3[0], b3[0], h_stack)
+    h_stack = fourth(0, h_stack)
+
+    def h_block(b):
+        apart = lax.bitwise_xor(dp, b)
         return pick(h_stack, jnp.where(inner & (apart >= 2), apart ^ 1, apart))
 
-    h_far = h_block(3)
-    left, right = flip(h_far[:, :half], "mp", 1), flip(h_far[:, half:], "mp", 2)
-    r2out, r2in, far3, h_stack = lax.optimization_barrier((r2out, r2in, far3, h_stack))
-
-    r3a = along(added(g_block(1), r2in), PAIRS)
-    r3b = along(added(g_block(3), r2out), MIDDLE)
-    h_two, h_one = h_block(2), h_block(1)
-    h_two = jnp.concatenate([added(h_two[:, :half], left), h_two[:, half:]], 1)
-    h_one = jnp.concatenate([h_one[:, :half], added(h_one[:, half:], right)], 1)
-    h_from_one, h_from_two = flip(h_one, "mp", 1), flip(h_two, "mp", 2)
-    c_stack = jnp.stack([upstream, c1, c2, c3])
+    h_all = jnp.concatenate([h_block(b) for b in range(4)])
+    a3[1], b3[1], h_all = seq(a3[1], b3[1], h_all)
+    summed = lax.psum_scatter(h_all, "mp", scatter_dimension=0, tiled=True)
+    own_block = fourth(1, upstream)
+    c_stack = jnp.stack(
+        [
+            own_block,
+            jnp.concatenate([c1_left, c_from_one[:, :half]], 1),
+            jnp.concatenate([c_from_two[:, :half], c2_right], 1),
+            jnp.concatenate([c_from_two[:, half:], c_from_one[:, half:]], 1),
+        ]
+    )
     block_sums = jnp.sum(c_stack, 1, dtype=f32)
     in_order = [pick(block_sums, lax.bitwise_xor(mp, b)) for b in range(4)]
     bias_grad = in_order[0] + in_order[1] + in_order[2] + in_order[3]
@@ -369,51 +411,69 @@
     c_all = jnp.concatenate(
         [c_of(0), c_of(1), c_of(jnp.where(inner, 3, 2)), c_of(jnp.where(inner, 2, 3))]
     )
-    r3a, r3b, h_from_one, h_from_two, c_all, normed_kept = lax.optimization_barrier(
-        (r3a, r3b, h_from_one, h_from_two, c_all, normed_kept)
-    )
-
-    near1, near2 = along(normed_kept, MIDDLE), along(normed_kept, OUTWARD)
-    grad_rows = g_block(0).astype(f32) + r3a.astype(f32) + r3b.astype(f32)
-    scaled = grad_rows * gain
-    row_terms = ring_total(jnp.stack([jnp.sum(scaled, 1), jnp.sum(scaled * kept_hat, 1)]), "mp")
-    row_terms = row_terms / full_width
-    column_sums = jnp.stack([jnp.sum(grad_rows * kept_hat, 0), jnp.sum(grad_rows, 0)])
+
+    def fifth(k, chain):
+        one, two, chain = seq(
+            added(g_block(1, sides[k]), b4[k]), added(g_block(3, sides[k]), a4[k]), chain
+        )
+        a5[k], b5[k] = along(one, PAIRS), along(two, MIDDLE)
+        return chain
+
+    a4[0], b4[0], c_all = seq(a4[0], b4[0], c_all)
+    c_all = fifth(0, c_all)
+    a4[1], b4[1], c_all = seq(a4[1], b4[1], c_all)
+    c_all = fifth(1, c_all)
+
+    def gradient(k):
+        rows = g_block(0, sides[k]).astype(f32) + a5[k].astype(f32) + b5[k].astype(f32)
+        scaled, hat = rows * gain, kept_hat[sides[k]]
+        return (
+            rows,
+            jnp.stack([jnp.sum(scaled, 1), jnp.sum(scaled * hat, 1)]),
+            jnp.stack([jnp.sum(rows * hat, 0), jnp.sum(rows, 0)]),
+        )
+
+    near1 = jnp.concatenate(b3)
+    a5[0], b5[0], near1, c_all = seq(a5[0], b5[0], near1, c_all)
+    near3 = [along(near1[:, :half], OUTWARD), along(near1[:, half:], OUTWARD)]
+    upper, upper_terms, upper_sums = gradient(0)
+    a5[1], b5[1], upper_terms, upper_sums = seq(a5[1], b5[1], upper_terms, upper_sums)
+    lower, lower_terms, lower_sums = gradient(1)
+    row_terms = jnp.concatenate([upper_terms, lower_terms], 1)
+    row_terms = row_terms + flip(row_terms, "mp", 1)
+    row_terms = (row_terms + flip(row_terms, "mp", 2)) / full_width
     columns = jnp.stack([stats[2], kept_inv, row_terms[0], row_terms[1]], 1)
     passed, outgoing = boundary(
-        grad_rows, kept_rows, columns, gain, h_block(0), h_from_one, h_from_two,
-        bias.reshape(col_count), section,
+        upper, lower, kept_rows, columns, gain, summed, bias.reshape(col_count), section
     )
     arrived = lax.all_to_all(outgoing, ("dp", "mp"), split_axis=0, concat_axis=0, tiled=True)
 
+    column_sums, c_all, outgoing = seq(upper_sums + lower_sums, c_all, outgoing)
+    column_sums = column_sums + along(column_sums, PAIRS)
+    column_grads = column_sums + along(column_sums, [(s, s ^ 2) for s in range(4)])
+    width = half // 2
+    early = [
+        normed_kept,
+        jnp.where(inner, jnp.concatenate(a1), jnp.concatenate(a4)),
+        jnp.where(inner, jnp.concatenate(b2), jnp.concatenate(a3)),
+    ]
     weight_grad = None
-    width = col_count // V_CHUNKS
-    cuts = lambda value: [value[:, k * width:(k + 1) * width] for k in range(V_CHUNKS)]
-    near3 = [along(part, OUTWARD) for part in lax.optimization_barrier(tuple(cuts(near1)))]
-    ready = lax.optimization_barrier(
-        (
-            tuple(cuts(normed_kept)),
-            tuple(cuts(jnp.where(inner, far1, near2))),
-            tuple(cuts(jnp.where(inner, far2, far3))),
-            tuple(cuts(near1)),
+    for k in range(4):
+        last = near3[k // 2]
+        if weight_grad is None:
+            last, c_all = seq(last, c_all)
+        else:
+            last, weight_grad = seq(last, weight_grad)
+        cut = lambda value: value[:, k * width:(k + 1) * width]
+        own, one, three = (cut(value) for value in early)
+        two = jnp.where(inner, cut(near1), last[:, (k % 2) * width:(k % 2 + 1) * width])
+        weight_grad = grad_block(
+            jnp.concatenate([own, one, two, three]), c_all, weight_grad, k, 4
         )
-    )
-    for k in range(V_CHUNKS):
-        last = near3[k]
-        if weight_grad is not None:
-            last, weight_grad = lax.optimization_barrier((last, weight_grad))
-        own, one, three, near = (part[k] for part in ready)
-        kept_all = jnp.concatenate([own, one, jnp.where(inner, near, last), three])
-        weight_grad = grad_block(kept_all, c_all, weight_grad, k, V_CHUNKS)
-        if k == V_CHUNKS // 2 - 1:
-            arrived, column_sums, weight_grad = lax.optimization_barrier(
-                (arrived, column_sums, weight_grad)
-            )
-
-    column_parts = lax.all_gather(column_sums, "dp", axis=0)
-    column_grads = column_parts[0] + column_parts[1] + column_parts[2] + column_parts[3]
-    arrived = flip(arrived, "section", 1)
-    next_in = jnp.where(section == 0, matrix_of(arrived, 4, False), matrix_of(arrived, 4, True))
+        if k == 2:
+            arrived, column_grads, weight_grad = seq(arrived, column_grads, weight_grad)
+            arrived = flip(arrived, "section", 1)
+    next_in = joined(arrived, section)
 
     return (
         next_in.reshape(fwd_in.shape),

time: 374 us -> 356 us (0.952)
  waiting for transfers between devices: 111 us -> 66.6 us
  blocking collectives: 32.9 us -> 0 us
  starting transfers between devices: 63.8 us -> 94.4 us
  Pallas kernels: 96.8 us -> 112 us
  between operations: 1.4 us -> 15.3 us
  local copies, waits for them, and re-layouts: 28.1 us -> 23.7 us
    ppermute x19 -> x28, starting transfers between devices: 41.5 us -> 76.6 us  [shards_of_four(): along = lambda value, pairs: lax.ppermute(value, 'dp', pairs)]
    ppermute x11 -> x9, waiting for transfers between devices: 35.9 us -> 2.5 us  [flip(): return lax.ppermute(value, axis, [(s, s ^ mask) for s in range(n)])]
    all_gather x2 -> x0, blocking collectives: 32.9 us -> none  [the longest x1 18.5 us: shards_of_four(): all_stats = lax.all_gather(stats[:2], 'dp', axis=0)]
    pallas_call x5 -> x7, Pallas kernels: 62.1 us -> 75.7 us  [shares(): pl.pallas_call(functools.partial(share_kernel, count, turned), grid=(cols...]
    ppermute x19 -> x28, waiting for transfers between devices: 74.8 us -> 64.1 us  [shards_of_four(): along = lambda value, pairs: lax.ppermute(value, 'dp', pairs)]
    concatenate x8 -> x10, other arithmetic: 4.5 us -> 9.83 us  [the longest x1 3.15 us: shards_of_four(): h_all = jnp.concatenate([h_block(b) for b in range(4)])]
    unnamed x58 -> x109, local copies, waits for them, and re-layouts: 17.4 us -> 13.3 us
    select_n x7 -> x11, other arithmetic: 5.55 us -> 8.48 us  [the longest x5 5.01 us: shards_of_four(): jnp.where(inner, from_inner, from_outer)]
  transfers between devices with their start and end apart: 34 -> 39, of which waited for: 10 -> 8; matrix products, arithmetic and copies ran while one was open for 11% -> 14% of each run, Pallas kernels for 26% -> 30%
where the time goes in v2:
time: 356 us; the launch traced here: 354 us
  Pallas kernels  112 us (31%)
  starting transfers between devices  94.4 us (27%)
  waiting for transfers between devices  66.6 us (19%)
  other arithmetic  42.5 us (12%)
  local copies, waits for them, and re-layouts  23.7 us (7%)
  between operations  15.3 us (4%)
    ppermute x28, starting transfers between devices, shards_of_four(): along = lambda value, pairs: lax.ppermute(value, 'dp', pairs)  76.6 us
    pallas_call x7, Pallas kernels, shares(): pl.pallas_call(functools.partial(share_kernel, count, turned), grid=(cols...  75.7 us
    ppermute x28, waiting for transfers between devices, shards_of_four(): along = lambda value, pairs: lax.ppermute(value, 'dp', pairs)  64.1 us
    pallas_call x4, Pallas kernels, grad_block(): pl.pallas_call(grad_kernel, grid=(cols // step,), in_specs=specs, out_spe...  31.7 us
    unnamed x109, local copies, waits for them, and re-layouts  13.3 us
    ppermute x9, starting transfers between devices, flip(): return lax.ppermute(value, axis, [(s, s ^ mask) for s in range(n)])  10.6 us
    convert_element_type x4, other arithmetic, affine(): return (hat * gain + shift).astype(bf16)  9.24 us
    all_to_all x1, starting transfers between devices, shards_of_four(): lax.all_to_all(outgoing, ('dp', 'mp'), split_axis=0, concat_axis=0, tiled...  7.16 us
  transfers between devices with their start and end apart: 39, of which 8 were waited for; matrix products, arithmetic and copies ran while one was open for 14% of the time, Pallas kernels for 30%

profile of v2, /device:TPU:0, one launch (start us, length us, event | category | flops | bytes accessed | tf_op | source)
XLA Modules:
  0.0 354.3 jit_solution(5334402240979542818)
XLA Ops:
  9.8 3.0 collective-permute-start.3
  19.3 3.3 collective-permute-start
  22.7 10.2 %shard_map.110.refs_5_ = bf16[4,256,3072]{2,1,0:T(8,128)(2,1)S(1)} custom-call(bf16[256,3072]{1,0:T(8,128)(2,1)S(1)} %bitcast.115, bf16[256,3072]{1,0:T(8,128)(2,1)S(1)} %bitcast.116, bf16[3072,3072]{1,0:T(8,128)(2,1)} %bitcast.125), custom_call_target="tpu_custom_call" | custom-call | flops 1 | bytes 1 | tf_op jit(solution)/shard_map/pallas_call | solution.py:96
  42.3 4.8 %add_convert_fusion.3 = (bf16[256,3072]{1,0:T(8,128)(2,1)S(1)}, f32[256,3072]{1,0:T(8,128)}, bf16[256,3072]{1,0:T(8,128)(2,1)S(1)}) fusion(f32[3072]{0:T(1024)S(1)} %bitcast.134, f32[3072]{0:T(1024)S(1)} %bitcast.119, f32[256]{0:T(256)S(1)} %get-tuple-element.239, f32[256]{0:T(256)S(1)} %bitcast.152, bf16[1,1,1,256,3072]{4,3,2,1,0:T(8,128)(2,1)S(1)} %copy-done.6, ...), kind=kLoop, calls=%fused_computation.20 | loop fusion | flops 9437184 | bytes 9465856 | tf_op jit(solution)/shard_map/convert_element_type | solution.py:307
  47.1 10.6 %shard_map.111.refs_3_ = bf16[4,256,3072]{2,1,0:T(8,128)(2,1)S(1)} custom-call(bf16[256,3072]{1,0:T(8,128)(2,1)S(1)} %get-tuple-element.222.refs_0_.refs_1_, bf16[256,3072]{1,0:T(8,128)(2,1)S(1)} %get-tuple-element.222.refs_0_.refs_1_, bf16[3072,3072]{1,0:T(8,128)(2,1)} %bitcast.126), custom_call_target="tpu_custom_call" | custom-call | flops 1 | bytes 1 | tf_op jit(solution)/shard_map/pallas_call | solution.py:96
  62.2 6.5 %collective-permute-start.6 = (bf16[128,3072]{1,0:T(8,128)(2,1)S(1)}, bf16[128,3072]{1,0:T(8,128)(2,1)S(1)}, u32[]{:S(2)}, u32[]{:S(2)}) collective-permute-start(bf16[128,3072]{1,0:T(8,128)(2,1)S(1)} %get-tuple-element.195), channel_id=1, source_target_pairs={{0,4},{4,0},{8,12},{12,8},{1,5},{5,1},{9,13},{13,9},{2,6},{6,2},{1... | collective-permute-start | bytes 2359304 | tf_op jit(solution)/shard_map/ppermute | solution.py:299
  68.7 14.9 %collective-permute-start.13 = (bf16[128,3072]{1,0:T(8,128)(2,1)S(1)}, bf16[128,3072]{1,0:T(8,128)(2,1)S(1)}, u32[]{:S(2)}, u32[]{:S(2)}) collective-permute-start(bf16[128,3072]{1,0:T(8,128)(2,1)S(1)} %get-tuple-element.196), channel_id=1, source_target_pairs={{0,4},{4,0},{8,12},{12,8},{1,5},{5,1},{9,13},{13,9},{2,6},{6,2},{1... | collective-permute-start | bytes 2359304 | tf_op jit(solution)/shard_map/ppermute | solution.py:299
  86.0 10.2 %shard_map.112.refs_3_ = bf16[4,256,3072]{2,1,0:T(8,128)(2,1)S(1)} custom-call(bf16[256,3072]{1,0:T(8,128)(2,1)S(1)} %add_convert_fusion.2.refs_0_.refs_1_, bf16[256,3072]{1,0:T(8,128)(2,1)S(1)} %add_convert_fusion.2.refs_0_.refs_1_, bf16[3072,3072]{1,0:T(8,128)(2,1)} %bitcast.127, ...), custom_call_target="tpu_custom_call", output_to_operand_aliasing={{}: (3, {})} | custom-call | flops 1 | bytes 1 | tf_op jit(solution)/shard_map/pallas_call | solution.py:96
  98.3 13.8 %shard_map.113.refs_3_ = bf16[4,256,3072]{2,1,0:T(8,128)(2,1)S(1)} custom-call(bf16[256,1536]{1,0:T(8,128)(2,1)S(1)} %copy-done.9, bf16[256,3072]{1,0:T(8,128)(2,1)S(1)} %collective-permute-done.12.refs_1_, bf16[256,3072]{1,0:T(8,128)(2,1)S(1)} %collective-permute-done.11.refs_2_.refs_0_, ...), custom_call_target="tpu_custom_call", output_to_operand_aliasing={{}: (5, {})} | custom-call | flops 1 | bytes 1 | tf_op jit(solution)/shard_map/pallas_call | solution.py:96
  113.4 5.5 %collective-permute-start.17 = (f32[2,2,256]{2,1,0:T(2,128)S(1)}, f32[2,2,256]{2,1,0:T(2,128)S(1)}, u32[]{:S(2)}, u32[]{:S(2)}) collective-permute-start(f32[2,2,256]{2,1,0:T(2,128)S(1)} %pad_maximum_fusion.13), channel_id=1, source_target_pairs={{0,8},{4,12},{8,0},{12,4},{1,9},{5,13},{9,1},{13,5},{2,10},{6,14},... | collective-permute-start | bytes 12296 | tf_op jit(solution)/shard_map/ppermute | solution.py:299
  119.9 10.8 %shard_map.114 = bf16[4,256,3072]{2,1,0:T(8,128)(2,1)S(1)} custom-call(bf16[256,3072]{1,0:T(8,128)(2,1)S(1)} %collective-permute-done.11.refs_2_.refs_0_, bf16[256,3072]{1,0:T(8,128)(2,1)S(1)} %collective-permute-done.12.refs_1_, bf16[3072,3072]{1,0:T(8,128)(2,1)} %bitcast.129, ...), custom_call_target="tpu_custom_call", output_to_operand_aliasing={{}: (3, {})} | custom-call | flops 1 | bytes 1 | tf_op jit(solution)/shard_map/pallas_call | solution.py:96
  131.6 3.5 collective-permute-start.18
  136.2 10.1 %shard_map.115.refs_3_ = bf16[4,256,3072]{2,1,0:T(8,128)(2,1)S(1)} custom-call(bf16[256,3072]{1,0:T(8,128)(2,1)S(1)} %add_convert_fusion.1.refs_0_.refs_1_, bf16[256,3072]{1,0:T(8,128)(2,1)S(1)} %add_convert_fusion.1.refs_0_.refs_1_, bf16[3072,3072]{1,0:T(8,128)(2,1)} %bitcast.130, ...), custom_call_target="tpu_custom_call", output_to_operand_aliasing={{}: (3, {})} | custom-call | flops 1 | bytes 1 | tf_op jit(solution)/shard_map/pallas_call | solution.py:96
  149.9 10.1 %shard_map.116 = bf16[4,256,3072]{2,1,0:T(8,128)(2,1)S(1)} custom-call(bf16[256,3072]{1,0:T(8,128)(2,1)S(1)} %add_convert_fusion.refs_0_.refs_1_, bf16[256,3072]{1,0:T(8,128)(2,1)S(1)} %add_convert_fusion.refs_0_.refs_1_, bf16[3072,3072]{1,0:T(8,128)(2,1)} %bitcast.131, bf16[4,256,3072]{2,1,0:T(8,128)(2,1)S(1)} %shard_map.115.refs_3_), custom_call_target="tpu_custom_call", output_to_operand_aliasing={{}: (3, {})} | custom-call | flops 1 | bytes 1 | tf_op jit(solution)/shard_map/pallas_call | solution.py:96
  163.9 3.2 pad_maximum_fusion
  174.1 9.2 %collective-permute-start.20 = (bf16[128,3072]{1,0:T(8,128)(2,1)S(1)}, bf16[128,3072]{1,0:T(8,128)(2,1)S(1)}, u32[]{:S(2)}, u32[]{:S(2)}) collective-permute-start(bf16[128,3072]{1,0:T(8,128)(2,1)S(1)} %copy-done.46), channel_id=1, source_target_pairs={{0,4},{4,0},{8,12},{12,8},{1,5},{5,1},{9,13},{13,9},{2,6},{6,2},{1... | collective-permute-start | bytes 2359304 | tf_op jit(solution)/shard_map/ppermute | solution.py:299
  184.5 4.4 %collective-permute-start.26 = (bf16[128,3072]{1,0:T(8,128)(2,1)S(1)}, bf16[128,3072]{1,0:T(8,128)(2,1)S(1)}, u32[]{:S(2)}, u32[]{:S(2)}) collective-permute-start(bf16[128,3072]{1,0:T(8,128)(2,1)S(1)} %get-tuple-element.130), channel_id=1, source_target_pairs={{0,4},{4,0},{8,12},{12,8},{1,5},{5,1},{9,13},{13,9},{2,6},{6,2},{1... | collective-permute-start | bytes 2359304 | tf_op jit(solution)/shard_map/ppermute | solution.py:299
  192.4 3.2 pad_maximum_fusion.2.c_ref
  195.7 6.1 %collective-permute-done.20 = bf16[128,3072]{1,0:T(8,128)(2,1)S(1)} collective-permute-done((bf16[128,3072]{1,0:T(8,128)(2,1)S(1)}, bf16[128,3072]{1,0:T(8,128)(2,1)S(1)}, u32[]{:S(2)}, u32[]{:S(2)}) %collective-permute-start.20) | collective-permute-done | bytes 786464 | tf_op jit(solution)/shard_map/ppermute | solution.py:299
  202.7 4.1 %collective-permute-start.24 = (bf16[128,3072]{1,0:T(8,128)(2,1)S(1)}, bf16[128,3072]{1,0:T(8,128)(2,1)S(1)}, u32[]{:S(2)}, u32[]{:S(2)}) collective-permute-start(bf16[128,3072]{1,0:T(8,128)(2,1)S(1)} %get-tuple-element.126), channel_id=1, source_target_pairs={{0,4},{4,0},{8,12},{12,8},{1,5},{5,1},{9,13},{13,9},{2,6},{6,2},{1... | collective-permute-start | bytes 2359304 | tf_op jit(solution)/shard_map/ppermute | solution.py:299
  209.9 8.7 %collective-permute-done.26 = bf16[128,3072]{1,0:T(8,128)(2,1)S(1)} collective-permute-done((bf16[128,3072]{1,0:T(8,128)(2,1)S(1)}, bf16[128,3072]{1,0:T(8,128)(2,1)S(1)}, u32[]{:S(2)}, u32[]{:S(2)}) %collective-permute-start.26) | collective-permute-done | bytes 786464 | tf_op jit(solution)/shard_map/ppermute | solution.py:299
  219.5 4.1 %collective-permute-start.28 = (bf16[128,3072]{1,0:T(8,128)(2,1)S(1)}, bf16[128,3072]{1,0:T(8,128)(2,1)S(1)}, u32[]{:S(2)}, u32[]{:S(2)}) collective-permute-start(bf16[128,3072]{1,0:T(8,128)(2,1)S(1)} %get-tuple-element.139), channel_id=1, source_target_pairs={{0,4},{4,0},{8,12},{12,8},{1,5},{5,1},{9,13},{13,9},{2,6},{6,2},{1... | collective-permute-start | bytes 2359304 | tf_op jit(solution)/shard_map/ppermute | solution.py:299
  224.6 8.0 %collective-permute-done.24 = bf16[128,3072]{1,0:T(8,128)(2,1)S(1)} collective-permute-done((bf16[128,3072]{1,0:T(8,128)(2,1)S(1)}, bf16[128,3072]{1,0:T(8,128)(2,1)S(1)}, u32[]{:S(2)}, u32[]{:S(2)}) %collective-permute-start.24) | collective-permute-done | bytes 786464 | tf_op jit(solution)/shard_map/ppermute | solution.py:299
  233.5 7.4 %collective-permute-done.28 = bf16[128,3072]{1,0:T(8,128)(2,1)S(1)} collective-permute-done((bf16[128,3072]{1,0:T(8,128)(2,1)S(1)}, bf16[128,3072]{1,0:T(8,128)(2,1)S(1)}, u32[]{:S(2)}, u32[]{:S(2)}) %collective-permute-start.28) | collective-permute-done | bytes 786464 | tf_op jit(solution)/shard_map/ppermute | solution.py:299
  253.0 2.8 shard_map.117
  256.9 7.2 %all-to-all-start = ((bf16[16,64,768]{2,1,0:T(8,128)(2,1)}), bf16[16,64,768]{2,1,0:T(8,128)(2,1)}, u32[]{:S(2)}, u32[]{:S(2)}) async-start(bf16[16,64,768]{2,1,0:T(8,128)(2,1)} %copy-done.15), calls=%async_computation.1 | async-start | bytes 3145728 | tf_op jit(solution)/shard_map/all_to_all | solution.py:449
  271.7 33.3 %collective-permute-done.35 = bf16[256,1536]{1,0:T(8,128)(2,1)S(1)} collective-permute-done((bf16[256,1536]{1,0:T(8,128)(2,1)S(1)}, bf16[256,1536]{1,0:T(8,128)(2,1)S(1)}, u32[]{:S(2)}, u32[]{:S(2)}) %collective-permute-start.35) | collective-permute-done | bytes 786464 | tf_op jit(solution)/shard_map/ppermute | solution.py:299
  305.2 7.9 %shard_map.118.rest_0_ = f32[3072,3072]{1,0:T(8,128)} custom-call(bf16[1024,768]{1,0:T(8,128)(2,1)S(1)} %pad_maximum_fusion.6.v_ref, bf16[1024,3072]{1,0:T(8,128)(2,1)S(1)} %bitcast.109), custom_call_target="tpu_custom_call" | custom-call | flops 1 | bytes 1 | tf_op jit(solution)/shard_map/pallas_call | solution.py:43
  313.3 7.9 %shard_map.119.rest_0_ = f32[3072,3072]{1,0:T(8,128)} custom-call(bf16[1024,768]{1,0:T(8,128)(2,1)S(1)} %pad_maximum_fusion.7.v_ref, bf16[1024,3072]{1,0:T(8,128)(2,1)S(1)} %bitcast.109, f32[3072,3072]{1,0:T(8,128)} %shard_map.118.rest_0_), custom_call_target="tpu_custom_call", output_to_operand_aliasing={{}: (2, {})} | custom-call | flops 1 | bytes 1 | tf_op jit(solution)/shard_map/pallas_call | solution.py:43
  322.7 7.9 %shard_map.120.rest_0_ = f32[3072,3072]{1,0:T(8,128)} custom-call(bf16[1024,768]{1,0:T(8,128)(2,1)S(1)} %pad_maximum_fusion.8.v_ref, bf16[1024,3072]{1,0:T(8,128)(2,1)S(1)} %bitcast.109, f32[3072,3072]{1,0:T(8,128)} %shard_map.119.rest_0_), custom_call_target="tpu_custom_call", output_to_operand_aliasing={{}: (2, {})} | custom-call | flops 1 | bytes 1 | tf_op jit(solution)/shard_map/pallas_call | solution.py:43
  335.1 2.8 copy-done
  337.9 7.9 %shard_map.122 = f32[3072,3072]{1,0:T(8,128)} custom-call(bf16[1024,768]{1,0:T(8,128)(2,1)S(1)} %pad_maximum_fusion.9.v_ref, bf16[1024,3072]{1,0:T(8,128)(2,1)S(1)} %copy-done, f32[3072,3072]{1,0:T(8,128)} %shard_map.120.rest_0_), custom_call_target="tpu_custom_call", output_to_operand_aliasing={{}: (2, {})} | custom-call | flops 1 | bytes 1 | tf_op jit(solution)/shard_map/pallas_call | solution.py:43
  (244 shorter events, 85.8 us)
Async XLA Ops:
  7.2 243.0 %reduce-scatter.2.cloned.1.call-start = ((), (), s32[]{:S(2)}) async-start(), calls=%async_computation.2 | async-start | bytes 7864320 | tf_op jit(solution)/shard_map/reduce_scatter | solution.py:397
  9.8 25.8 %collective-permute-start.3 = (bf16[256,1536]{1,0:T(8,128)(2,1)}, bf16[256,1536]{1,0:T(8,128)(2,1)S(1)}, u32[]{:S(2)}, u32[]{:S(2)}) collective-permute-start(bf16[256,1536]{1,0:T(8,128)(2,1)} %get-tuple-element.220), channel_id=1, source_target_pairs={{0,2},{1,3},{2,0},{3,1},{4,6},{5,7},{6,4},{7,5},{8,10},{9,11},{10,... | collective-permute-start | bytes 2359304 | tf_op jit(solution)/shard_map/ppermute | solution.py:16
  12.8 22.8 %collective-permute-start.2 = (bf16[256,1536]{1,0:T(8,128)(2,1)}, bf16[256,1536]{1,0:T(8,128)(2,1)S(1)}, u32[]{:S(2)}, u32[]{:S(2)}) collective-permute-start(bf16[256,1536]{1,0:T(8,128)(2,1)} %get-tuple-element.221), channel_id=1, source_target_pairs={{0,1},{1,0},{2,3},{3,2},{4,5},{5,4},{6,7},{7,6},{8,9},{9,8},{10,11... | collective-permute-start | bytes 2359304 | tf_op jit(solution)/shard_map/ppermute | solution.py:16
  16.9 18.6 %collective-permute-start.4 = (f32[4,256]{1,0:T(4,128)S(1)}, f32[4,256]{1,0:T(4,128)S(1)}, u32[]{:S(2)}, u32[]{:S(2)}) collective-permute-start(f32[4,256]{1,0:T(4,128)S(1)} %pad_maximum_fusion.12), channel_id=1, source_target_pairs={{0,1},{1,0},{2,3},{3,2},{4,5},{5,4},{6,7},{7,6},{8,9},{9,8},{10,11... | collective-permute-start | bytes 12296 | tf_op jit(solution)/shard_map/ppermute | solution.py:16
  17.5 40.2 %collective-permute-start.1 = (bf16[256,3072]{1,0:T(8,128)(2,1)}, bf16[256,3072]{1,0:T(8,128)(2,1)}, u32[]{:S(2)}, u32[]{:S(2)}) collective-permute-start(bf16[256,3072]{1,0:T(8,128)(2,1)} %bitcast), channel_id=1, source_target_pairs={{4,8},{8,4},{5,9},{9,5},{6,10},{10,6},{7,11},{11,7},{20,24},{24,20... | collective-permute-start | bytes 4718600 | tf_op jit(solution)/shard_map/ppermute | solution.py:299
  19.3 38.4 %collective-permute-start = (bf16[256,3072]{1,0:T(8,128)(2,1)}, bf16[256,3072]{1,0:T(8,128)(2,1)}, u32[]{:S(2)}, u32[]{:S(2)}) collective-permute-start(bf16[256,3072]{1,0:T(8,128)(2,1)} %bitcast), channel_id=1, source_target_pairs={{0,4},{4,0},{8,12},{12,8},{1,5},{5,1},{9,13},{13,9},{2,6},{6,2},{1... | collective-permute-start | bytes 4718600 | tf_op jit(solution)/shard_map/ppermute | solution.py:299
  39.0 58.5 %collective-permute-start.12 = (bf16[256,3072]{1,0:T(8,128)(2,1)S(1)}, bf16[256,3072]{1,0:T(8,128)(2,1)S(1)}, u32[]{:S(2)}, u32[]{:S(2)}) collective-permute-start(bf16[256,3072]{1,0:T(8,128)(2,1)S(1)} %pad_maximum_fusion.4), channel_id=1, source_target_pairs={{0,1},{1,0},{2,3},{3,2},{4,5},{5,4},{6,7},{7,6},{8,9},{9,8},{10,11... | collective-permute-start | bytes 4718600 | tf_op jit(solution)/shard_map/ppermute | solution.py:16
  40.6 57.7 %collective-permute-start.11 = (bf16[256,3072]{1,0:T(8,128)(2,1)S(1)}, bf16[256,3072]{1,0:T(8,128)(2,1)S(1)}, u32[]{:S(2)}, u32[]{:S(2)}) collective-permute-start(bf16[256,3072]{1,0:T(8,128)(2,1)S(1)} %pad_maximum_fusion.3), channel_id=1, source_target_pairs={{0,2},{1,3},{2,0},{3,1},{4,6},{5,7},{6,4},{7,5},{8,10},{9,11},{10,... | collective-permute-start | bytes 4718600 | tf_op jit(solution)/shard_map/ppermute | solution.py:16
  42.1 15.6 %collective-permute-start.8 = (f32[2,256]{1,0:T(2,128)S(1)}, f32[2,256]{1,0:T(2,128)S(1)}, u32[]{:S(2)}, u32[]{:S(2)}) collective-permute-start(f32[2,256]{1,0:T(2,128)S(1)} %get-tuple-element.233), channel_id=1, source_target_pairs={{0,4},{4,0},{8,12},{12,8},{1,5},{5,1},{9,13},{13,9},{2,6},{6,2},{1... | collective-permute-start | bytes 6152 | tf_op jit(solution)/shard_map/ppermute | solution.py:299
  60.0 52.1 %collective-permute-start.14 = (bf16[128,3072]{1,0:T(8,128)(2,1)S(1)}, bf16[128,3072]{1,0:T(8,128)(2,1)S(1)}, u32[]{:S(2)}, u32[]{:S(2)}) collective-permute-start(bf16[128,3072]{1,0:T(8,128)(2,1)S(1)} %get-tuple-element.219), channel_id=1, source_target_pairs={{4,8},{8,4},{5,9},{9,5},{6,10},{10,6},{7,11},{11,7},{20,24},{24,20... | collective-permute-start | bytes 2359304 | tf_op jit(solution)/shard_map/ppermute | solution.py:299
  62.2 34.0 %collective-permute-start.6 = (bf16[128,3072]{1,0:T(8,128)(2,1)S(1)}, bf16[128,3072]{1,0:T(8,128)(2,1)S(1)}, u32[]{:S(2)}, u32[]{:S(2)}) collective-permute-start(bf16[128,3072]{1,0:T(8,128)(2,1)S(1)} %get-tuple-element.195), channel_id=1, source_target_pairs={{0,4},{4,0},{8,12},{12,8},{1,5},{5,1},{9,13},{13,9},{2,6},{6,2},{1... | collective-permute-start | bytes 2359304 | tf_op jit(solution)/shard_map/ppermute | solution.py:299
  68.7 43.4 %collective-permute-start.13 = (bf16[128,3072]{1,0:T(8,128)(2,1)S(1)}, bf16[128,3072]{1,0:T(8,128)(2,1)S(1)}, u32[]{:S(2)}, u32[]{:S(2)}) collective-permute-start(bf16[128,3072]{1,0:T(8,128)(2,1)S(1)} %get-tuple-element.196), channel_id=1, source_target_pairs={{0,4},{4,0},{8,12},{12,8},{1,5},{5,1},{9,13},{13,9},{2,6},{6,2},{1... | collective-permute-start | bytes 2359304 | tf_op jit(solution)/shard_map/ppermute | solution.py:299
  96.2 34.5 %collective-permute-start.9 = (bf16[128,3072]{1,0:T(8,128)(2,1)S(1)}, bf16[128,3072]{1,0:T(8,128)(2,1)S(1)}, u32[]{:S(2)}, u32[]{:S(2)}) collective-permute-start(bf16[128,3072]{1,0:T(8,128)(2,1)S(1)} %collective-permute-done.7), channel_id=1, source_target_pairs={{4,0},{8,12},{5,1},{9,13},{6,2},{10,14},{7,3},{11,15},{20,16},{24,... | collective-permute-start | bytes 2359304 | tf_op jit(solution)/shard_map/ppermute | solution.py:299
  97.6 33.2 %collective-permute-start.10 = (bf16[128,3072]{1,0:T(8,128)(2,1)S(1)}, bf16[128,3072]{1,0:T(8,128)(2,1)S(1)}, u32[]{:S(2)}, u32[]{:S(2)}) collective-permute-start(bf16[128,3072]{1,0:T(8,128)(2,1)S(1)} %collective-permute-done.6), channel_id=1, source_target_pairs={{4,8},{8,4},{5,9},{9,5},{6,10},{10,6},{7,11},{11,7},{20,24},{24,20... | collective-permute-start | bytes 2359304 | tf_op jit(solution)/shard_map/ppermute | solution.py:299
  112.1 34.1 %collective-permute-start.15 = (bf16[128,3072]{1,0:T(8,128)(2,1)S(1)}, bf16[128,3072]{1,0:T(8,128)(2,1)S(1)}, u32[]{:S(2)}, u32[]{:S(2)}) collective-permute-start(bf16[128,3072]{1,0:T(8,128)(2,1)S(1)} %collective-permute-done.14), channel_id=1, source_target_pairs={{4,0},{8,12},{5,1},{9,13},{6,2},{10,14},{7,3},{11,15},{20,16},{24,... | collective-permute-start | bytes 2359304 | tf_op jit(solution)/shard_map/ppermute | solution.py:299
  113.4 17.3 %collective-permute-start.17 = (f32[2,2,256]{2,1,0:T(2,128)S(1)}, f32[2,2,256]{2,1,0:T(2,128)S(1)}, u32[]{:S(2)}, u32[]{:S(2)}) collective-permute-start(f32[2,2,256]{2,1,0:T(2,128)S(1)} %pad_maximum_fusion.13), channel_id=1, source_target_pairs={{0,8},{4,12},{8,0},{12,4},{1,9},{5,13},{9,1},{13,5},{2,10},{6,14},... | collective-permute-start | bytes 12296 | tf_op jit(solution)/shard_map/ppermute | solution.py:299
  118.9 27.4 %collective-permute-start.16 = (bf16[128,3072]{1,0:T(8,128)(2,1)S(1)}, bf16[128,3072]{1,0:T(8,128)(2,1)S(1)}, u32[]{:S(2)}, u32[]{:S(2)}) collective-permute-start(bf16[128,3072]{1,0:T(8,128)(2,1)S(1)} %collective-permute-done.13), channel_id=1, source_target_pairs={{4,8},{8,4},{5,9},{9,5},{6,10},{10,6},{7,11},{11,7},{20,24},{24,20... | collective-permute-start | bytes 2359304 | tf_op jit(solution)/shard_map/ppermute | solution.py:299
  130.9 29.1 %collective-permute-start.19 = (bf16[128,3072]{1,0:T(8,128)(2,1)S(1)}, bf16[128,3072]{1,0:T(8,128)(2,1)S(1)}, u32[]{:S(2)}, u32[]{:S(2)}) collective-permute-start(bf16[128,3072]{1,0:T(8,128)(2,1)S(1)} %slice.181), channel_id=1, source_target_pairs={{4,8},{8,4},{5,9},{9,5},{6,10},{10,6},{7,11},{11,7},{20,24},{24,20... | collective-permute-start | bytes 2359304 | tf_op jit(solution)/shard_map/ppermute | solution.py:299
  131.6 28.4 %collective-permute-start.18 = (bf16[128,3072]{1,0:T(8,128)(2,1)S(1)}, bf16[128,3072]{1,0:T(8,128)(2,1)S(1)}, u32[]{:S(2)}, u32[]{:S(2)}) collective-permute-start(bf16[128,3072]{1,0:T(8,128)(2,1)S(1)} %bitcast_select_fusion.1), channel_id=1, source_target_pairs={{0,4},{4,0},{8,12},{12,8},{1,5},{5,1},{9,13},{13,9},{2,6},{6,2},{1... | collective-permute-start | bytes 2359304 | tf_op jit(solution)/shard_map/ppermute | solution.py:299
  147.3 20.3 %collective-permute-start.22 = (bf16[128,3072]{1,0:T(8,128)(2,1)}, bf16[128,3072]{1,0:T(8,128)(2,1)}, u32[]{:S(2)}, u32[]{:S(2)}) collective-permute-start(bf16[128,3072]{1,0:T(8,128)(2,1)} %bitcast_select_fusion), channel_id=1, source_target_pairs={{0,4},{4,0},{8,12},{12,8},{1,5},{5,1},{9,13},{13,9},{2,6},{6,2},{1... | collective-permute-start | bytes 2359304 | tf_op jit(solution)/shard_map/ppermute | solution.py:299
  174.1 27.7 %collective-permute-start.20 = (bf16[128,3072]{1,0:T(8,128)(2,1)S(1)}, bf16[128,3072]{1,0:T(8,128)(2,1)S(1)}, u32[]{:S(2)}, u32[]{:S(2)}) collective-permute-start(bf16[128,3072]{1,0:T(8,128)(2,1)S(1)} %copy-done.46), channel_id=1, source_target_pairs={{0,4},{4,0},{8,12},{12,8},{1,5},{5,1},{9,13},{13,9},{2,6},{6,2},{1... | collective-permute-start | bytes 2359304 | tf_op jit(solution)/shard_map/ppermute | solution.py:299
  183.3 18.5 %collective-permute-start.21 = (bf16[128,3072]{1,0:T(8,128)(2,1)S(1)}, bf16[128,3072]{1,0:T(8,128)(2,1)S(1)}, u32[]{:S(2)}, u32[]{:S(2)}) collective-permute-start(bf16[128,3072]{1,0:T(8,128)(2,1)S(1)} %copy-done.45), channel_id=1, source_target_pairs={{4,8},{8,4},{5,9},{9,5},{6,10},{10,6},{7,11},{11,7},{20,24},{24,20... | collective-permute-start | bytes 2359304 | tf_op jit(solution)/shard_map/ppermute | solution.py:299
  184.5 34.1 %collective-permute-start.26 = (bf16[128,3072]{1,0:T(8,128)(2,1)S(1)}, bf16[128,3072]{1,0:T(8,128)(2,1)S(1)}, u32[]{:S(2)}, u32[]{:S(2)}) collective-permute-start(bf16[128,3072]{1,0:T(8,128)(2,1)S(1)} %get-tuple-element.130), channel_id=1, source_target_pairs={{0,4},{4,0},{8,12},{12,8},{1,5},{5,1},{9,13},{13,9},{2,6},{6,2},{1... | collective-permute-start | bytes 2359304 | tf_op jit(solution)/shard_map/ppermute | solution.py:299
  188.9 29.7 %collective-permute-start.27 = (bf16[128,3072]{1,0:T(8,128)(2,1)S(1)}, bf16[128,3072]{1,0:T(8,128)(2,1)S(1)}, u32[]{:S(2)}, u32[]{:S(2)}) collective-permute-start(bf16[128,3072]{1,0:T(8,128)(2,1)S(1)} %get-tuple-element.131), channel_id=1, source_target_pairs={{4,8},{8,4},{5,9},{9,5},{6,10},{10,6},{7,11},{11,7},{20,24},{24,20... | collective-permute-start | bytes 2359304 | tf_op jit(solution)/shard_map/ppermute | solution.py:299
  202.7 29.8 %collective-permute-start.24 = (bf16[128,3072]{1,0:T(8,128)(2,1)S(1)}, bf16[128,3072]{1,0:T(8,128)(2,1)S(1)}, u32[]{:S(2)}, u32[]{:S(2)}) collective-permute-start(bf16[128,3072]{1,0:T(8,128)(2,1)S(1)} %get-tuple-element.126), channel_id=1, source_target_pairs={{0,4},{4,0},{8,12},{12,8},{1,5},{5,1},{9,13},{13,9},{2,6},{6,2},{1... | collective-permute-start | bytes 2359304 | tf_op jit(solution)/shard_map/ppermute | solution.py:299
  206.8 25.7 %collective-permute-start.25 = (bf16[128,3072]{1,0:T(8,128)(2,1)S(1)}, bf16[128,3072]{1,0:T(8,128)(2,1)S(1)}, u32[]{:S(2)}, u32[]{:S(2)}) collective-permute-start(bf16[128,3072]{1,0:T(8,128)(2,1)S(1)} %get-tuple-element.127), channel_id=1, source_target_pairs={{4,8},{8,4},{5,9},{9,5},{6,10},{10,6},{7,11},{11,7},{20,24},{24,20... | collective-permute-start | bytes 2359304 | tf_op jit(solution)/shard_map/ppermute | solution.py:299
  219.5 21.5 %collective-permute-start.28 = (bf16[128,3072]{1,0:T(8,128)(2,1)S(1)}, bf16[128,3072]{1,0:T(8,128)(2,1)S(1)}, u32[]{:S(2)}, u32[]{:S(2)}) collective-permute-start(bf16[128,3072]{1,0:T(8,128)(2,1)S(1)} %get-tuple-element.139), channel_id=1, source_target_pairs={{0,4},{4,0},{8,12},{12,8},{1,5},{5,1},{9,13},{13,9},{2,6},{6,2},{1... | collective-permute-start | bytes 2359304 | tf_op jit(solution)/shard_map/ppermute | solution.py:299
  223.6 17.3 %collective-permute-start.29 = (bf16[128,3072]{1,0:T(8,128)(2,1)S(1)}, bf16[128,3072]{1,0:T(8,128)(2,1)S(1)}, u32[]{:S(2)}, u32[]{:S(2)}) collective-permute-start(bf16[128,3072]{1,0:T(8,128)(2,1)S(1)} %get-tuple-element.140), channel_id=1, source_target_pairs={{4,8},{8,4},{5,9},{9,5},{6,10},{10,6},{7,11},{11,7},{20,24},{24,20... | collective-permute-start | bytes 2359304 | tf_op jit(solution)/shard_map/ppermute | solution.py:299
  256.9 74.3 %all-to-all-start = ((bf16[16,64,768]{2,1,0:T(8,128)(2,1)}), bf16[16,64,768]{2,1,0:T(8,128)(2,1)}, u32[]{:S(2)}, u32[]{:S(2)}) async-start(bf16[16,64,768]{2,1,0:T(8,128)(2,1)} %copy-done.15), calls=%async_computation.1 | async-start | bytes 3145728 | tf_op jit(solution)/shard_map/all_to_all | solution.py:449
  264.3 40.7 %collective-permute-start.35 = (bf16[256,1536]{1,0:T(8,128)(2,1)S(1)}, bf16[256,1536]{1,0:T(8,128)(2,1)S(1)}, u32[]{:S(2)}, u32[]{:S(2)}) collective-permute-start(bf16[256,1536]{1,0:T(8,128)(2,1)S(1)} %get-tuple-element.211), channel_id=1, source_target_pairs={{4,0},{8,12},{5,1},{9,13},{6,2},{10,14},{7,3},{11,15},{20,16},{24,... | collective-permute-start | bytes 2359304 | tf_op jit(solution)/shard_map/ppermute | solution.py:299
  267.5 53.8 %collective-permute-start.34 = (bf16[256,1536]{1,0:T(8,128)(2,1)S(1)}, bf16[256,1536]{1,0:T(8,128)(2,1)S(1)}, u32[]{:S(2)}, u32[]{:S(2)}) collective-permute-start(bf16[256,1536]{1,0:T(8,128)(2,1)S(1)} %get-tuple-element.212), channel_id=1, source_target_pairs={{4,0},{8,12},{5,1},{9,13},{6,2},{10,14},{7,3},{11,15},{20,16},{24,... | collective-permute-start | bytes 2359304 | tf_op jit(solution)/shard_map/ppermute | solution.py:299
  268.9 52.3 %collective-permute-start.32 = (f32[2,3072]{1,0:T(2,128)S(1)}, f32[2,3072]{1,0:T(2,128)S(1)}, u32[]{:S(2)}, u32[]{:S(2)}) collective-permute-start(f32[2,3072]{1,0:T(2,128)S(1)} %maximum_add_fusion), channel_id=1, source_target_pairs={{0,4},{4,0},{8,12},{12,8},{1,5},{5,1},{9,13},{13,9},{2,6},{6,2},{1... | collective-permute-start | bytes 73736 | tf_op jit(solution)/shard_map/ppermute | solution.py:299
  (61 other events, 675.0 us)
Sparse Core Ops, SparseCore 0:
  167.8 76.0 reduce-scatter.1

commit v3 on v2

--- a/solution.py
+++ b/solution.py
@@ -70,24 +70,24 @@
         out_ref[k] = total.astype(jnp.bfloat16)
 
 
-def shares(blocks, w, turned, filled, at, total):
+def shares(blocks, w, turned, filled, place, total, total_rows):
     count = len(blocks)
     halves = []
     for block in blocks:
-        halves += list(block) if isinstance(block, tuple) else [(block, 0), (block, 1)]
-    rows = halves[0][0].shape[0]
+        halves += list(block) if isinstance(block, tuple) else [(block, 0, 0), (block, 1, 0)]
+    rows = total_rows // total
     depth = w.shape[1] if turned else w.shape[0]
     cols = w.shape[0] if turned else w.shape[1]
     step = 512
     specs = [
-        pl.BlockSpec((rows, depth // 2), functools.partial(lambda side, j: (0, side), side))
-        for array, side in halves
+        pl.BlockSpec((rows, depth // 2), functools.partial(lambda side, at, j: (at, side), side, at))
+        for array, side, at in halves
     ]
     if turned:
         specs.append(pl.BlockSpec((step, depth), lambda j: (j, 0)))
     else:
         specs.append(pl.BlockSpec((depth, step), lambda j: (0, j)))
-    operands = [array for array, side in halves] + [w]
+    operands = [array for array, side, at in halves] + [w]
     aliases = {}
     if filled is not None:
         specs.append(pl.BlockSpec(memory_space=pl.ANY))
@@ -97,12 +97,57 @@
         functools.partial(share_kernel, count, turned),
         grid=(cols // step,),
         in_specs=specs,
-        out_specs=pl.BlockSpec((count, rows, step), lambda j: (at // count, 0, j)),
+        out_specs=pl.BlockSpec((count, rows, step), lambda j: (place // count, 0, j)),
         out_shape=jax.ShapeDtypeStruct((total, rows, cols), jnp.bfloat16),
         input_output_aliases=aliases,
         compiler_params=pltpu.CompilerParams(vmem_limit_bytes=32 * 2**20),
         cost_estimate=LIGHT,
     )(*operands)
+
+
+def normed_kernel(rows_ref, stats_ref, gain_ref, shift_ref, out_ref):
+    stats = stats_ref[...]
+    hat = (rows_ref[...].astype(jnp.float32) - stats[:, 0:1]) * stats[:, 1:2]
+    out_ref[...] = (hat * gain_ref[...] + shift_ref[...]).astype(jnp.bfloat16)
+
+
+def normed(rows, row_stats, gain, shift):
+    mean, square_mean = row_stats[0], row_stats[1]
+    stats = jnp.stack([mean, lax.rsqrt(square_mean - mean * mean + eps)], 1)
+    count, cols = rows.shape
+    part = 64
+    line = pl.BlockSpec((1, cols), lambda j: (0, 0))
+    wide = pl.BlockSpec((part, cols), lambda j: (j, 0))
+    return pl.pallas_call(
+        normed_kernel,
+        grid=(count // part,),
+        in_specs=[wide, pl.BlockSpec((part, 2), lambda j: (j, 0)), line, line],
+        out_specs=wide,
+        out_shape=jax.ShapeDtypeStruct((count, cols), jnp.bfloat16),
+        compiler_params=pltpu.CompilerParams(vmem_limit_bytes=32 * 2**20),
+        cost_estimate=LIGHT,
+    )(rows, stats, gain.reshape(1, cols), shift.reshape(1, cols))
+
+
+def reorder_kernel(order_ref, stack_ref, out_ref):
+    out_ref[...] = stack_ref[...]
+
+
+def reorder(stack, order):
+    count, rows, cols = stack.shape
+    out = pl.pallas_call(
+        reorder_kernel,
+        grid_spec=pltpu.PrefetchScalarGridSpec(
+            num_scalar_prefetch=1,
+            grid=(count,),
+            in_specs=[pl.BlockSpec((1, rows, cols), lambda j, order: (order[j], 0, 0))],
+            out_specs=pl.BlockSpec((1, rows, cols), lambda j, order: (j, 0, 0)),
+        ),
+        out_shape=jax.ShapeDtypeStruct(stack.shape, stack.dtype),
+        compiler_params=pltpu.CompilerParams(vmem_limit_bytes=32 * 2**20),
+        cost_estimate=LIGHT,
+    )(jnp.stack(order).astype(jnp.int32), stack)
+    return out.reshape(count * rows, cols)
 
 
 def boundary_kernel(upper_ref, lower_ref, kept_ref, columns_ref, gain_ref, h_ref, bias_ref, section_ref, passed_ref, out_ref):
@@ -303,79 +348,77 @@
         inverse = lax.rsqrt(square_mean - mean * mean + eps)
         return (values.astype(f32) - mean[:, None]) * inverse[:, None], inverse
 
-    def affine(hat):
-        return (hat * gain + shift).astype(bf16)
-
     def added(one, two):
         return (one.astype(f32) + two.astype(f32)).astype(bf16)
 
     seq = lambda *values: lax.optimization_barrier(values)
 
-    u1a, u1b = along(fresh_rows, PAIRS), along(fresh_rows, MIDDLE)
-    c_left, c_right = upstream[:, :half], upstream[:, half:]
-    c1_left, c2_right = flip(c_left, "mp", 1), flip(c_right, "mp", 2)
+    sides = [slice(0, row_count // 2), slice(row_count // 2, row_count)]
+    either = lambda from_inner, from_outer: jnp.where(inner, from_inner, from_outer)
+    u1a, u1b, a1, b1, a2, b2, a3, b3, a4, b4, a5, b5, x2 = (
+        [None, None] for unused in range(13)
+    )
+
+    c_all = lax.all_gather(upstream, "mp", axis=0, tiled=True)
+    for k in range(2):
+        u1a[k] = along(fresh_rows[sides[k]], PAIRS)
+        u1b[k] = along(fresh_rows[sides[k]], MIDDLE)
     fresh, kept = fresh_rows.astype(f32), kept_rows.astype(f32)
     sums = jnp.stack(
         [jnp.sum(fresh, 1), jnp.sum(fresh * fresh, 1), jnp.sum(kept, 1), jnp.sum(kept * kept, 1)]
     )
-    other = flip(sums, "mp", 1)
-    g_stack = shares([upstream], w, True, None, 3, 4)
-    c1_left, c2_right, sums, other, g_stack = seq(c1_left, c2_right, sums, other, g_stack)
-    c_from_one = flip(jnp.concatenate([c_right, c2_right], 1), "mp", 1)
-    c_from_two = flip(jnp.concatenate([c_left, c1_left], 1), "mp", 2)
-    sums = sums + other
+    u1a[0], u1b[0], sums = seq(u1a[0], u1b[0], sums)
+    sums = sums + flip(sums, "mp", 1)
     stats = (sums + flip(sums, "mp", 2)) / full_width
     kept_hat, kept_inv = standardize(kept_rows, stats[2], stats[3])
-    normed_kept = affine(kept_hat)
-
-    def normed(rows, row_stats):
-        hat, unused = standardize(rows, row_stats[0], row_stats[1])
-        return affine(hat)
-
+    normed_kept = normed(kept_rows, stats[2:], gain, shift)
+
+    u1a[0], u1b[0], normed_kept, stats = seq(u1a[0], u1b[0], normed_kept, stats)
     pair_stats = jnp.stack([stats[:2], along(stats[:2], PAIRS)])
-    h_stack = shares([normed(fresh_rows, stats)], w, False, None, 0, 4)
-    u1a, u1b, normed_kept, h_stack = seq(u1a, u1b, normed_kept, h_stack)
-
-    sides = [slice(0, row_count // 2), slice(row_count // 2, row_count)]
-    either = lambda from_inner, from_outer: jnp.where(inner, from_inner, from_outer)
-    a1, b1, a2, b2, a3, b3, a4, b4, a5, b5, x2 = ([None, None] for unused in range(11))
-
-    for k in range(2):
-        a1[k] = along(either(u1b[sides[k]], normed_kept[sides[k]]), PAIRS)
-        b1[k] = along(u1a[sides[k]], MIDDLE)
-    h_stack = shares([normed(u1a, pair_stats[1])], w, False, h_stack, 1, 4)
-
-    a1[0], b1[0], h_stack, c1_left, c2_right = seq(a1[0], b1[0], h_stack, c1_left, c2_right)
+    sent, stats = seq(either(u1b[0], normed_kept[sides[0]]), stats)
+    a1[0], b1[0] = along(sent, PAIRS), along(u1a[0], MIDDLE)
+    u1a[1], u1b[1], normed_kept, stats = seq(u1a[1], u1b[1], normed_kept, stats)
+    sent, stats = seq(either(u1b[1], normed_kept[sides[1]]), stats)
+    a1[1], b1[1] = along(sent, PAIRS), along(u1a[1], MIDDLE)
+    pair_stats, stats, u1a[1] = seq(pair_stats, stats, u1a[1])
+    h_stack = shares(
+        [
+            normed(fresh_rows, stats, gain, shift),
+            normed(jnp.concatenate(u1a), pair_stats[1], gain, shift),
+        ],
+        w, False, None, 0, 4, 4 * row_count,
+    )
+
+    a1[0], b1[0], h_stack, pair_stats = seq(a1[0], b1[0], h_stack, pair_stats)
     a2[0], b2[0] = along(b1[0], OUTWARD), along(a1[0], MIDDLE)
-    g_stack = shares(
-        [((c1_left, 0), (c_from_one, 0)), ((c_from_two, 0), (c2_right, 0))], w, True, g_stack, 0, 4
-    )
-    a1[1], b1[1], g_stack = seq(a1[1], b1[1], g_stack)
+    all_stats = jnp.concatenate([pair_stats, along(pair_stats, [(s, s ^ 2) for s in range(4)])])
+    a1[1], b1[1], h_stack, all_stats, c_all = seq(a1[1], b1[1], h_stack, all_stats, c_all)
     a2[1], b2[1] = along(b1[1], OUTWARD), along(a1[1], MIDDLE)
-    pair_stats = seq(pair_stats, b1[1])[0]
-    all_stats = jnp.concatenate([pair_stats, along(pair_stats, [(s, s ^ 2) for s in range(4)])])
-    g_stack = shares([((c_from_two, 1), (c_from_one, 1))], w, True, g_stack, 2, 4)
+    g_stack = None
+    for first in (0, 2):
+        blocks = [((c_all, 0, b), (c_all, 1, b)) for b in (first, first + 1)]
+        g_stack = shares(blocks, w, True, g_stack, first, 4, 4 * row_count)
 
     def g_block(k, side):
-        apart = lax.bitwise_xor(lax.bitwise_xor(dp, mp), k)
-        at = jnp.where(apart == 0, 3, apart - 1)
         return lax.dynamic_slice(
-            g_stack, (at, side.start, 0), (1, side.stop - side.start, col_count)
+            g_stack, (dp ^ k, side.start, 0), (1, side.stop - side.start, col_count)
         )[0]
 
     a2[0], b2[0], g_stack, normed_kept = seq(a2[0], b2[0], g_stack, normed_kept)
-    sent, h_stack = seq(either(b2[0], g_block(3, sides[0])), h_stack)
-    a3[0] = along(sent, PAIRS)
-    b3[0] = along(normed_kept[sides[0]], MIDDLE)
-    all_stats, h_stack = seq(all_stats, h_stack)
-    u2 = jnp.where(inner, u1b, jnp.concatenate(a1))
-    h_stack = shares([normed(u2, pick(all_stats, jnp.where(inner, 3, 2)))], w, False, h_stack, 2, 4)
-    a2[1], b2[1], h_stack, normed_kept = seq(a2[1], b2[1], h_stack, normed_kept)
+    sent, g_stack = seq(either(b2[0], g_block(3, sides[0])), g_stack)
+    a3[0], b3[0] = along(sent, PAIRS), along(normed_kept[sides[0]], MIDDLE)
+    a2[1], b2[1], g_stack, normed_kept = seq(a2[1], b2[1], g_stack, normed_kept)
     sent, h_stack = seq(either(b2[1], g_block(3, sides[1])), h_stack)
-    a3[1] = along(sent, PAIRS)
-    b3[1] = along(normed_kept[sides[1]], MIDDLE)
+    a3[1], b3[1] = along(sent, PAIRS), along(normed_kept[sides[1]], MIDDLE)
+    u2 = jnp.where(inner, jnp.concatenate(u1b), jnp.concatenate(a1))
     u3 = jnp.where(inner, jnp.concatenate(b1), jnp.concatenate(a2))
-    h_stack = shares([normed(u3, pick(all_stats, jnp.where(inner, 2, 3)))], w, False, h_stack, 3, 4)
+    h_stack = shares(
+        [
+            normed(u2, pick(all_stats, jnp.where(inner, 3, 2)), gain, shift),
+            normed(u3, pick(all_stats, jnp.where(inner, 2, 3)), gain, shift),
+        ],
+        w, False, h_stack, 2, 4, 4 * row_count,
+    )
 
     nothing = jnp.zeros((row_count // 2, col_count), bf16)
 
@@ -388,28 +431,16 @@
     a3[0], b3[0], h_stack = seq(a3[0], b3[0], h_stack)
     h_stack = fourth(0, h_stack)
 
-    def h_block(b):
-        apart = lax.bitwise_xor(dp, b)
-        return pick(h_stack, jnp.where(inner & (apart >= 2), apart ^ 1, apart))
-
-    h_all = jnp.concatenate([h_block(b) for b in range(4)])
+    places = [lax.bitwise_xor(dp, b) for b in range(4)]
+    places = [jnp.where(inner & (at >= 2), at ^ 1, at) for at in places]
+    h_all = reorder(h_stack, places)
     a3[1], b3[1], h_all = seq(a3[1], b3[1], h_all)
     summed = lax.psum_scatter(h_all, "mp", scatter_dimension=0, tiled=True)
-    own_block = fourth(1, upstream)
-    c_stack = jnp.stack(
-        [
-            own_block,
-            jnp.concatenate([c1_left, c_from_one[:, :half]], 1),
-            jnp.concatenate([c_from_two[:, :half], c2_right], 1),
-            jnp.concatenate([c_from_two[:, half:], c_from_one[:, half:]], 1),
-        ]
-    )
-    block_sums = jnp.sum(c_stack, 1, dtype=f32)
-    in_order = [pick(block_sums, lax.bitwise_xor(mp, b)) for b in range(4)]
-    bias_grad = in_order[0] + in_order[1] + in_order[2] + in_order[3]
-    c_of = lambda k: pick(c_stack, lax.bitwise_xor(lax.bitwise_xor(dp, mp), k))
-    c_all = jnp.concatenate(
-        [c_of(0), c_of(1), c_of(jnp.where(inner, 3, 2)), c_of(jnp.where(inner, 2, 3))]
+    c_all = fourth(1, c_all)
+    bias_grad = jnp.sum(c_all, 0, dtype=f32)
+    c_all = reorder(
+        c_all.reshape(4, row_count, col_count),
+        [dp, dp ^ 1, jnp.where(inner, dp ^ 3, dp ^ 2), jnp.where(inner, dp ^ 2, dp ^ 3)],
     )
 
     def fifth(k, chain):
@@ -419,7 +450,7 @@
         a5[k], b5[k] = along(one, PAIRS), along(two, MIDDLE)
         return chain
 
-    a4[0], b4[0], c_all = seq(a4[0], b4[0], c_all)
+    a4[0], b4[0], c_all, bias_grad = seq(a4[0], b4[0], c_all, bias_grad)
     c_all = fifth(0, c_all)
     a4[1], b4[1], c_all = seq(a4[1], b4[1], c_all)
     c_all = fifth(1, c_all)
@@ -435,17 +466,21 @@
 
     near1 = jnp.concatenate(b3)
     a5[0], b5[0], near1, c_all = seq(a5[0], b5[0], near1, c_all)
-    near3 = [along(near1[:, :half], OUTWARD), along(near1[:, half:], OUTWARD)]
+    near3 = [along(near1[:, :half], OUTWARD), None]
     upper, upper_terms, upper_sums = gradient(0)
     a5[1], b5[1], upper_terms, upper_sums = seq(a5[1], b5[1], upper_terms, upper_sums)
     lower, lower_terms, lower_sums = gradient(1)
     row_terms = jnp.concatenate([upper_terms, lower_terms], 1)
     row_terms = row_terms + flip(row_terms, "mp", 1)
+    sent, row_terms = seq(near1[:, half:], row_terms)
+    near3[1] = along(sent, OUTWARD)
     row_terms = (row_terms + flip(row_terms, "mp", 2)) / full_width
     columns = jnp.stack([stats[2], kept_inv, row_terms[0], row_terms[1]], 1)
+    near3[0], columns = seq(near3[0], columns)
     passed, outgoing = boundary(
         upper, lower, kept_rows, columns, gain, summed, bias.reshape(col_count), section
     )
+    outgoing = flip(outgoing, "section", 1)
     arrived = lax.all_to_all(outgoing, ("dp", "mp"), split_axis=0, concat_axis=0, tiled=True)
 
     column_sums, c_all, outgoing = seq(upper_sums + lower_sums, c_all, outgoing)
@@ -472,7 +507,6 @@
         )
         if k == 2:
             arrived, column_grads, weight_grad = seq(arrived, column_grads, weight_grad)
-            arrived = flip(arrived, "section", 1)
     next_in = joined(arrived, section)
 
     return (

time: 356 us -> 369 us (1.037)
  waiting for transfers between devices: 66.6 us -> 108 us
  Pallas kernels: 112 us -> 95.3 us
  starting transfers between devices: 94.4 us -> 79.5 us
  local copies, waits for them, and re-layouts: 23.7 us -> 36.6 us
  other arithmetic: 42.5 us -> 32.4 us
    ppermute x28 -> x30, waiting for transfers between devices: 64.1 us -> 102 us  [shards_of_four(): along = lambda value, pairs: lax.ppermute(value, 'dp', pairs)]
    pallas_call x7 -> x4, Pallas kernels: 75.7 us -> 52.4 us  [shares(): pl.pallas_call(functools.partial(share_kernel, count, turned), grid=(cols...]
    unnamed x109 -> x111, local copies, waits for them, and re-layouts: 13.3 us -> 28.9 us
    convert_element_type x4 -> x0, other arithmetic: 9.24 us -> none  [affine(): return (hat * gain + shift).astype(bf16)]
    concatenate x4 -> x1, other arithmetic: 9.13 us -> 1.59 us  [shards_of_four(): jnp.concatenate(u1a)]
    pallas_call x0 -> x7, Pallas kernels: none -> 6.74 us  [the longest x5 4.69 us: normed(): pl.pallas_call(normed_kernel, grid=(count // part,), in_specs=[wide, pl.B...]
    ppermute x28 -> x30, starting transfers between devices: 76.6 us -> 70.3 us  [shards_of_four(): along = lambda value, pairs: lax.ppermute(value, 'dp', pairs)]
    ppermute x9 -> x5, starting transfers between devices: 10.6 us -> 5.14 us  [flip(): return lax.ppermute(value, axis, [(s, s ^ mask) for s in range(n)])]
  transfers between devices with their start and end apart: 39 -> 38, of which waited for: 8 -> 12; matrix products, arithmetic and copies ran while one was open for 14% -> 11% of each run, Pallas kernels for 30% -> 23%
where the time goes in v3:
time: 369 us; the launch traced here: 367 us
  waiting for transfers between devices  108 us (29%)
  Pallas kernels  95.3 us (26%)
  starting transfers between devices  79.5 us (22%)
  local copies, waits for them, and re-layouts  36.6 us (10%)
  other arithmetic  32.4 us (9%)
  between operations  15.2 us (4%)
    ppermute x30, waiting for transfers between devices, shards_of_four(): along = lambda value, pairs: lax.ppermute(value, 'dp', pairs)  102 us
    ppermute x30, starting transfers between devices, shards_of_four(): along = lambda value, pairs: lax.ppermute(value, 'dp', pairs)  70.3 us
    pallas_call x4, Pallas kernels, shares(): pl.pallas_call(functools.partial(share_kernel, count, turned), grid=(cols...  52.4 us
    pallas_call x4, Pallas kernels, grad_block(): pl.pallas_call(grad_kernel, grid=(cols // step,), in_specs=specs, out_spe...  31.7 us
    unnamed x111, local copies, waits for them, and re-layouts  28.9 us
    select_n x6, other arithmetic, shards_of_four(): jnp.where(inner, from_inner, from_outer)  10.3 us
  transfers between devices with their start and end apart: 38, of which 12 were waited for; matrix products, arithmetic and copies ran while one was open for 11% of the time, Pallas kernels for 23%

profile of v3, /device:TPU:0, one launch (start us, length us, event | category | flops | bytes accessed | tf_op | source)
XLA Modules:
  0.0 366.8 jit_solution(15689553600010594833)
XLA Ops:
  11.2 5.0 %collective-permute-start.2 = (bf16[128,3072]{1,0:T(8,128)(2,1)S(1)}, bf16[128,3072]{1,0:T(8,128)(2,1)}, u32[]{:S(2)}, u32[]{:S(2)}) collective-permute-start(bf16[128,3072]{1,0:T(8,128)(2,1)S(1)} %get-tuple-element.229), channel_id=1, source_target_pairs={{0,4},{4,0},{8,12},{12,8},{1,5},{5,1},{9,13},{13,9},{2,6},{6,2},{1... | collective-permute-start | bytes 2359304 | tf_op jit(solution)/shard_map/ppermute | solution.py:344
  17.5 16.1 %collective-permute-done.2 = bf16[128,3072]{1,0:T(8,128)(2,1)} collective-permute-done((bf16[128,3072]{1,0:T(8,128)(2,1)S(1)}, bf16[128,3072]{1,0:T(8,128)(2,1)}, u32[]{:S(2)}, u32[]{:S(2)}) %collective-permute-start.2) | collective-permute-done | bytes 786464 | tf_op jit(solution)/shard_map/ppermute | solution.py:344
  44.4 14.0 %collective-permute-done = bf16[128,3072]{1,0:T(8,128)(2,1)} collective-permute-done((bf16[128,3072]{1,0:T(8,128)(2,1)}, bf16[128,3072]{1,0:T(8,128)(2,1)}, u32[]{:S(2)}, u32[]{:S(2)}) %collective-permute-start) | collective-permute-done | bytes 786464 | tf_op jit(solution)/shard_map/ppermute | solution.py:344
  59.4 2.9 collective-permute-start.6
  71.4 13.0 %shard_map.113.refs_5_ = bf16[4,256,3072]{2,1,0:T(8,128)(2,1)S(1)} custom-call(bf16[256,3072]{1,0:T(8,128)(2,1)S(1)} %shard_map.111.refs_0_.refs_1_, bf16[256,3072]{1,0:T(8,128)(2,1)S(1)} %shard_map.111.refs_0_.refs_1_, bf16[256,3072]{1,0:T(8,128)(2,1)S(1)} %shard_map.112.refs_2_.refs_3_, bf16[256,3072]{1,0:T(8,128)(2,1)S(1)} %shard_map.112.refs_2_.refs_3_, ...), custom_call_target="tpu_custom_call" | custom-call | flops 1 | bytes 1 | tf_op jit(solution)/shard_map/pallas_call | solution.py:96
  87.2 6.4 %collective-permute-done.8 = bf16[128,3072]{1,0:T(8,128)(2,1)} collective-permute-done((bf16[128,3072]{1,0:T(8,128)(2,1)S(1)}, bf16[128,3072]{1,0:T(8,128)(2,1)}, u32[]{:S(2)}, u32[]{:S(2)}) %collective-permute-start.8) | collective-permute-done | bytes 786464 | tf_op jit(solution)/shard_map/ppermute | solution.py:344
  93.6 4.6 %collective-permute-start.11 = (f32[2,2,256]{2,1,0:T(2,128)S(1)}, f32[2,2,256]{2,1,0:T(2,128)S(1)}, u32[]{:S(2)}, u32[]{:S(2)}) collective-permute-start(f32[2,2,256]{2,1,0:T(2,128)S(1)} %pad_maximum_fusion.9), channel_id=1, source_target_pairs={{0,8},{4,12},{8,0},{12,4},{1,9},{5,13},{9,1},{13,5},{2,10},{6,14},... | collective-permute-start | bytes 12296 | tf_op jit(solution)/shard_map/ppermute | solution.py:344
  103.6 2.8 copy-done
  106.4 13.1 %shard_map.114.refs_5_ = bf16[4,256,3072]{2,1,0:T(8,128)(2,1)S(1)} custom-call(bf16[1024,3072]{1,0:T(8,128)(2,1)S(1)} %bitcast.135, bf16[1024,3072]{1,0:T(8,128)(2,1)S(1)} %bitcast.136, bf16[1024,3072]{1,0:T(8,128)(2,1)S(1)} %bitcast.137, bf16[1024,3072]{1,0:T(8,128)(2,1)S(1)} %bitcast.138, bf16[3072,3072]{1,0:T(8,128)(2,1)} %bitcast.165), custom_call_target="tpu_custom_call" | custom-call | flops 1 | bytes 1 | tf_op jit(solution)/shard_map/pallas_call | solution.py:96
  121.1 13.1 %shard_map.115 = bf16[4,256,3072]{2,1,0:T(8,128)(2,1)S(1)} custom-call(bf16[1024,3072]{1,0:T(8,128)(2,1)S(1)} %bitcast.139, bf16[1024,3072]{1,0:T(8,128)(2,1)S(1)} %bitcast.140, bf16[1024,3072]{1,0:T(8,128)(2,1)S(1)} %bitcast.141, bf16[1024,3072]{1,0:T(8,128)(2,1)S(1)} %bitcast.142, bf16[3072,3072]{1,0:T(8,128)(2,1)} %bitcast.166, ...), custom_call_target="tpu_custom_call", output_to_operand_aliasing={{}: (5, {})} | custom-call | flops 1 | bytes 1 | tf_op jit(solution)/shard_map/pallas_call | solution.py:96
  141.6 10.0 %collective-permute-start.16 = (bf16[128,3072]{1,0:T(8,128)(2,1)S(1)}, bf16[128,3072]{1,0:T(8,128)(2,1)S(1)}, u32[]{:S(2)}, u32[]{:S(2)}) collective-permute-start(bf16[128,3072]{1,0:T(8,128)(2,1)S(1)} %copy-done.44), channel_id=1, source_target_pairs={{0,4},{4,0},{8,12},{12,8},{1,5},{5,1},{9,13},{13,9},{2,6},{6,2},{1... | collective-permute-start | bytes 2359304 | tf_op jit(solution)/shard_map/ppermute | solution.py:344
  158.9 13.0 %shard_map.118.stack_ref = bf16[4,256,3072]{2,1,0:T(8,128)(2,1)S(1)} custom-call(bf16[256,3072]{1,0:T(8,128)(2,1)S(1)} %shard_map.116.refs_0_.refs_1_, bf16[256,3072]{1,0:T(8,128)(2,1)S(1)} %shard_map.116.refs_0_.refs_1_, bf16[256,3072]{1,0:T(8,128)(2,1)S(1)} %shard_map.117.refs_2_.refs_3_, ...), custom_call_target="tpu_custom_call", output_to_operand_aliasing={{}: (5, {})} | custom-call | flops 1 | bytes 1 | tf_op jit(solution)/shard_map/pallas_call | solution.py:96
  174.7 3.5 slice_select_fusion
  179.1 2.8 copy-done.6
  188.9 9.3 %collective-permute-start.18 = (bf16[128,3072]{1,0:T(8,128)(2,1)}, bf16[128,3072]{1,0:T(8,128)(2,1)S(1)}, u32[]{:S(2)}, u32[]{:S(2)}) collective-permute-start(bf16[128,3072]{1,0:T(8,128)(2,1)} %get-tuple-element.136), channel_id=1, source_target_pairs={{0,4},{4,0},{8,12},{12,8},{1,5},{5,1},{9,13},{13,9},{2,6},{6,2},{1... | collective-permute-start | bytes 2359304 | tf_op jit(solution)/shard_map/ppermute | solution.py:344
  201.3 3.2 collective-permute-start.24
  210.4 6.4 %collective-permute-done.18 = bf16[128,3072]{1,0:T(8,128)(2,1)S(1)} collective-permute-done((bf16[128,3072]{1,0:T(8,128)(2,1)}, bf16[128,3072]{1,0:T(8,128)(2,1)S(1)}, u32[]{:S(2)}, u32[]{:S(2)}) %collective-permute-start.18) | collective-permute-done | bytes 786464 | tf_op jit(solution)/shard_map/ppermute | solution.py:344
  217.8 3.9 %collective-permute-start.22 = (bf16[128,3072]{1,0:T(8,128)(2,1)S(1)}, bf16[128,3072]{1,0:T(8,128)(2,1)S(1)}, u32[]{:S(2)}, u32[]{:S(2)}) collective-permute-start(bf16[128,3072]{1,0:T(8,128)(2,1)S(1)} %get-tuple-element.145), channel_id=1, source_target_pairs={{0,4},{4,0},{8,12},{12,8},{1,5},{5,1},{9,13},{13,9},{2,6},{6,2},{1... | collective-permute-start | bytes 2359304 | tf_op jit(solution)/shard_map/ppermute | solution.py:344
  222.5 11.2 %collective-permute-done.24 = bf16[128,3072]{1,0:T(8,128)(2,1)S(1)} collective-permute-done((bf16[128,3072]{1,0:T(8,128)(2,1)S(1)}, bf16[128,3072]{1,0:T(8,128)(2,1)S(1)}, u32[]{:S(2)}, u32[]{:S(2)}) %collective-permute-start.24) | collective-permute-done | bytes 786464 | tf_op jit(solution)/shard_map/ppermute | solution.py:344
  234.6 3.8 %collective-permute-start.26 = (bf16[128,3072]{1,0:T(8,128)(2,1)S(1)}, bf16[128,3072]{1,0:T(8,128)(2,1)S(1)}, u32[]{:S(2)}, u32[]{:S(2)}) collective-permute-start(bf16[128,3072]{1,0:T(8,128)(2,1)S(1)} %get-tuple-element.158), channel_id=1, source_target_pairs={{0,4},{4,0},{8,12},{12,8},{1,5},{5,1},{9,13},{13,9},{2,6},{6,2},{1... | collective-permute-start | bytes 2359304 | tf_op jit(solution)/shard_map/ppermute | solution.py:344
  239.2 11.4 %collective-permute-done.22 = bf16[128,3072]{1,0:T(8,128)(2,1)S(1)} collective-permute-done((bf16[128,3072]{1,0:T(8,128)(2,1)S(1)}, bf16[128,3072]{1,0:T(8,128)(2,1)S(1)}, u32[]{:S(2)}, u32[]{:S(2)}) %collective-permute-start.22) | collective-permute-done | bytes 786464 | tf_op jit(solution)/shard_map/ppermute | solution.py:344
  252.1 7.1 %collective-permute-done.26 = bf16[128,3072]{1,0:T(8,128)(2,1)S(1)} collective-permute-done((bf16[128,3072]{1,0:T(8,128)(2,1)S(1)}, bf16[128,3072]{1,0:T(8,128)(2,1)S(1)}, u32[]{:S(2)}, u32[]{:S(2)}) %collective-permute-start.26) | collective-permute-done | bytes 786464 | tf_op jit(solution)/shard_map/ppermute | solution.py:344
  266.2 3.1 collective-permute-done.30
  269.3 10.3 %collective-permute-done.28 = bf16[256,1536]{1,0:T(8,128)(2,1)} collective-permute-done((bf16[256,1536]{1,0:T(8,128)(2,1)}, bf16[256,1536]{1,0:T(8,128)(2,1)}, u32[]{:S(2)}, u32[]{:S(2)}) %collective-permute-start.28) | collective-permute-done | bytes 786464 | tf_op jit(solution)/shard_map/ppermute | solution.py:344
  282.6 2.8 shard_map.121
  289.2 3.9 %all-to-all-start = ((bf16[16,64,768]{2,1,0:T(8,128)(2,1)}), bf16[16,64,768]{2,1,0:T(8,128)(2,1)S(1)}, u32[]{:S(2)}, u32[]{:S(2)}) async-start(bf16[16,64,768]{2,1,0:T(8,128)(2,1)} %collective-permute-done.31), calls=%async_computation.1 | async-start | bytes 3145728 | tf_op jit(solution)/shard_map/all_to_all | solution.py:484
  302.2 7.9 %shard_map.122.rest_0_ = f32[3072,3072]{1,0:T(8,128)} custom-call(bf16[1024,768]{1,0:T(8,128)(2,1)S(1)} %pad_maximum_fusion.2.v_ref, bf16[1024,3072]{1,0:T(8,128)(2,1)S(1)} %bitcast.149), custom_call_target="tpu_custom_call" | custom-call | flops 1 | bytes 1 | tf_op jit(solution)/shard_map/pallas_call | solution.py:43
  311.3 7.9 %shard_map.123.rest_0_ = f32[3072,3072]{1,0:T(8,128)} custom-call(bf16[1024,768]{1,0:T(8,128)(2,1)S(1)} %pad_maximum_fusion.3.v_ref, bf16[1024,3072]{1,0:T(8,128)(2,1)S(1)} %bitcast.150, f32[3072,3072]{1,0:T(8,128)} %shard_map.122.rest_0_), custom_call_target="tpu_custom_call", output_to_operand_aliasing={{}: (2, {})} | custom-call | flops 1 | bytes 1 | tf_op jit(solution)/shard_map/pallas_call | solution.py:43
  319.2 18.6 %collective-permute-done.34 = bf16[256,1536]{1,0:T(8,128)(2,1)S(1)} collective-permute-done((bf16[256,1536]{1,0:T(8,128)(2,1)S(1)}, bf16[256,1536]{1,0:T(8,128)(2,1)S(1)}, u32[]{:S(2)}, u32[]{:S(2)}) %collective-permute-start.34) | collective-permute-done | bytes 786464 | tf_op jit(solution)/shard_map/ppermute | solution.py:344
  338.8 7.9 %shard_map.124.rest_0_ = f32[3072,3072]{1,0:T(8,128)} custom-call(bf16[1024,768]{1,0:T(8,128)(2,1)S(1)} %pad_maximum_fusion.4.v_ref, bf16[1024,3072]{1,0:T(8,128)(2,1)S(1)} %bitcast.151, f32[3072,3072]{1,0:T(8,128)} %shard_map.123.rest_0_), custom_call_target="tpu_custom_call", output_to_operand_aliasing={{}: (2, {})} | custom-call | flops 1 | bytes 1 | tf_op jit(solution)/shard_map/pallas_call | solution.py:43
  349.3 2.8 copy-done.2
  352.0 7.9 %shard_map.126 = f32[3072,3072]{1,0:T(8,128)} custom-call(bf16[1024,768]{1,0:T(8,128)(2,1)S(1)} %pad_maximum_fusion.5.v_ref, bf16[1024,3072]{1,0:T(8,128)(2,1)S(1)} %bitcast.152, f32[3072,3072]{1,0:T(8,128)} %shard_map.124.rest_0_), custom_call_target="tpu_custom_call", output_to_operand_aliasing={{}: (2, {})} | custom-call | flops 1 | bytes 1 | tf_op jit(solution)/shard_map/pallas_call | solution.py:43
  (248 shorter events, 101.5 us)
Async XLA Ops:
  7.2 95.1 %all-gather.3.cloned.1.call-start = ((), (), s32[]{:S(2)}) async-start(), calls=%async_computation.3 | async-start | bytes 7864320 | tf_op jit(solution)/shard_map/all_gather | solution.py:362
  7.9 271.9 %reduce-scatter.2.cloned.1.call-start = ((), (), s32[]{:S(2)}) async-start(), calls=%async_computation.2 | async-start | bytes 7864320 | tf_op jit(solution)/shard_map/reduce_scatter | solution.py:438
  9.6 8.0 %collective-permute-start.3 = (bf16[128,3072]{1,0:T(8,128)(2,1)S(1)}, bf16[128,3072]{1,0:T(8,128)(2,1)}, u32[]{:S(2)}, u32[]{:S(2)}) collective-permute-start(bf16[128,3072]{1,0:T(8,128)(2,1)S(1)} %get-tuple-element.229), channel_id=1, source_target_pairs={{4,8},{8,4},{5,9},{9,5},{6,10},{10,6},{7,11},{11,7},{20,24},{24,20... | collective-permute-start | bytes 2359304 | tf_op jit(solution)/shard_map/ppermute | solution.py:344
  11.2 22.4 %collective-permute-start.2 = (bf16[128,3072]{1,0:T(8,128)(2,1)S(1)}, bf16[128,3072]{1,0:T(8,128)(2,1)}, u32[]{:S(2)}, u32[]{:S(2)}) collective-permute-start(bf16[128,3072]{1,0:T(8,128)(2,1)S(1)} %get-tuple-element.229), channel_id=1, source_target_pairs={{0,4},{4,0},{8,12},{12,8},{1,5},{5,1},{9,13},{13,9},{2,6},{6,2},{1... | collective-permute-start | bytes 2359304 | tf_op jit(solution)/shard_map/ppermute | solution.py:344
  40.4 18.1 %collective-permute-start = (bf16[128,3072]{1,0:T(8,128)(2,1)}, bf16[128,3072]{1,0:T(8,128)(2,1)}, u32[]{:S(2)}, u32[]{:S(2)}) collective-permute-start(bf16[128,3072]{1,0:T(8,128)(2,1)} %get-tuple-element.228), channel_id=1, source_target_pairs={{0,4},{4,0},{8,12},{12,8},{1,5},{5,1},{9,13},{13,9},{2,6},{6,2},{1... | collective-permute-start | bytes 2359304 | tf_op jit(solution)/shard_map/ppermute | solution.py:344
  44.2 23.1 %collective-permute-start.10 = (f32[2,256]{1,0:T(2,128)S(1)}, f32[2,256]{1,0:T(2,128)S(1)}, u32[]{:S(2)}, u32[]{:S(2)}) collective-permute-start(f32[2,256]{1,0:T(2,128)S(1)} %get-tuple-element.235), channel_id=1, source_target_pairs={{0,4},{4,0},{8,12},{12,8},{1,5},{5,1},{9,13},{13,9},{2,6},{6,2},{1... | collective-permute-start | bytes 6152 | tf_op jit(solution)/shard_map/ppermute | solution.py:344
  59.4 42.8 %collective-permute-start.6 = (bf16[128,3072]{1,0:T(8,128)(2,1)}, bf16[128,3072]{1,0:T(8,128)(2,1)}, u32[]{:S(2)}, u32[]{:S(2)}) collective-permute-start(bf16[128,3072]{1,0:T(8,128)(2,1)} %slice_select_fusion.1), channel_id=1, source_target_pairs={{0,4},{4,0},{8,12},{12,8},{1,5},{5,1},{9,13},{13,9},{2,6},{6,2},{1... | collective-permute-start | bytes 2359304 | tf_op jit(solution)/shard_map/ppermute | solution.py:344
  62.3 40.0 %collective-permute-start.7 = (bf16[128,3072]{1,0:T(8,128)(2,1)}, bf16[128,3072]{1,0:T(8,128)(2,1)}, u32[]{:S(2)}, u32[]{:S(2)}) collective-permute-start(bf16[128,3072]{1,0:T(8,128)(2,1)} %collective-permute-done), channel_id=1, source_target_pairs={{4,8},{8,4},{5,9},{9,5},{6,10},{10,6},{7,11},{11,7},{20,24},{24,20... | collective-permute-start | bytes 2359304 | tf_op jit(solution)/shard_map/ppermute | solution.py:344
  63.8 29.8 %collective-permute-start.8 = (bf16[128,3072]{1,0:T(8,128)(2,1)S(1)}, bf16[128,3072]{1,0:T(8,128)(2,1)}, u32[]{:S(2)}, u32[]{:S(2)}) collective-permute-start(bf16[128,3072]{1,0:T(8,128)(2,1)S(1)} %slice_select_fusion.2), channel_id=1, source_target_pairs={{0,4},{4,0},{8,12},{12,8},{1,5},{5,1},{9,13},{13,9},{2,6},{6,2},{1... | collective-permute-start | bytes 2359304 | tf_op jit(solution)/shard_map/ppermute | solution.py:344
  65.8 27.8 %collective-permute-start.9 = (bf16[128,3072]{1,0:T(8,128)(2,1)}, bf16[128,3072]{1,0:T(8,128)(2,1)}, u32[]{:S(2)}, u32[]{:S(2)}) collective-permute-start(bf16[128,3072]{1,0:T(8,128)(2,1)} %collective-permute-done.2), channel_id=1, source_target_pairs={{4,8},{8,4},{5,9},{9,5},{6,10},{10,6},{7,11},{11,7},{20,24},{24,20... | collective-permute-start | bytes 2359304 | tf_op jit(solution)/shard_map/ppermute | solution.py:344
  93.6 8.6 %collective-permute-start.11 = (f32[2,2,256]{2,1,0:T(2,128)S(1)}, f32[2,2,256]{2,1,0:T(2,128)S(1)}, u32[]{:S(2)}, u32[]{:S(2)}) collective-permute-start(f32[2,2,256]{2,1,0:T(2,128)S(1)} %pad_maximum_fusion.9), channel_id=1, source_target_pairs={{0,8},{4,12},{8,0},{12,4},{1,9},{5,13},{9,1},{13,5},{2,10},{6,14},... | collective-permute-start | bytes 12296 | tf_op jit(solution)/shard_map/ppermute | solution.py:344
  98.2 37.9 %collective-permute-start.14 = (bf16[128,3072]{1,0:T(8,128)(2,1)}, bf16[128,3072]{1,0:T(8,128)(2,1)}, u32[]{:S(2)}, u32[]{:S(2)}) collective-permute-start(bf16[128,3072]{1,0:T(8,128)(2,1)} %collective-permute-done.9), channel_id=1, source_target_pairs={{4,0},{8,12},{5,1},{9,13},{6,2},{10,14},{7,3},{11,15},{20,16},{24,... | collective-permute-start | bytes 2359304 | tf_op jit(solution)/shard_map/ppermute | solution.py:344
  99.5 36.6 %collective-permute-start.15 = (bf16[128,3072]{1,0:T(8,128)(2,1)}, bf16[128,3072]{1,0:T(8,128)(2,1)}, u32[]{:S(2)}, u32[]{:S(2)}) collective-permute-start(bf16[128,3072]{1,0:T(8,128)(2,1)} %collective-permute-done.8), channel_id=1, source_target_pairs={{4,8},{8,4},{5,9},{9,5},{6,10},{10,6},{7,11},{11,7},{20,24},{24,20... | collective-permute-start | bytes 2359304 | tf_op jit(solution)/shard_map/ppermute | solution.py:344
  102.3 50.3 %collective-permute-start.12 = (bf16[128,3072]{1,0:T(8,128)(2,1)}, bf16[128,3072]{1,0:T(8,128)(2,1)}, u32[]{:S(2)}, u32[]{:S(2)}) collective-permute-start(bf16[128,3072]{1,0:T(8,128)(2,1)} %collective-permute-done.7), channel_id=1, source_target_pairs={{4,0},{8,12},{5,1},{9,13},{6,2},{10,14},{7,3},{11,15},{20,16},{24,... | collective-permute-start | bytes 2359304 | tf_op jit(solution)/shard_map/ppermute | solution.py:344
  119.5 33.1 %collective-permute-start.13 = (bf16[128,3072]{1,0:T(8,128)(2,1)}, bf16[128,3072]{1,0:T(8,128)(2,1)}, u32[]{:S(2)}, u32[]{:S(2)}) collective-permute-start(bf16[128,3072]{1,0:T(8,128)(2,1)} %collective-permute-done.6), channel_id=1, source_target_pairs={{4,8},{8,4},{5,9},{9,5},{6,10},{10,6},{7,11},{11,7},{20,24},{24,20... | collective-permute-start | bytes 2359304 | tf_op jit(solution)/shard_map/ppermute | solution.py:344
  138.3 36.3 %collective-permute-start.17 = (bf16[128,3072]{1,0:T(8,128)(2,1)S(1)}, bf16[128,3072]{1,0:T(8,128)(2,1)S(1)}, u32[]{:S(2)}, u32[]{:S(2)}) collective-permute-start(bf16[128,3072]{1,0:T(8,128)(2,1)S(1)} %slice.173), channel_id=1, source_target_pairs={{4,8},{8,4},{5,9},{9,5},{6,10},{10,6},{7,11},{11,7},{20,24},{24,20... | collective-permute-start | bytes 2359304 | tf_op jit(solution)/shard_map/ppermute | solution.py:344
  141.6 33.0 %collective-permute-start.16 = (bf16[128,3072]{1,0:T(8,128)(2,1)S(1)}, bf16[128,3072]{1,0:T(8,128)(2,1)S(1)}, u32[]{:S(2)}, u32[]{:S(2)}) collective-permute-start(bf16[128,3072]{1,0:T(8,128)(2,1)S(1)} %copy-done.44), channel_id=1, source_target_pairs={{0,4},{4,0},{8,12},{12,8},{1,5},{5,1},{9,13},{13,9},{2,6},{6,2},{1... | collective-permute-start | bytes 2359304 | tf_op jit(solution)/shard_map/ppermute | solution.py:344
  157.6 28.0 %collective-permute-start.20 = (bf16[128,3072]{1,0:T(8,128)(2,1)}, bf16[128,3072]{1,0:T(8,128)(2,1)S(1)}, u32[]{:S(2)}, u32[]{:S(2)}) collective-permute-start(bf16[128,3072]{1,0:T(8,128)(2,1)} %bitcast_select_fusion), channel_id=1, source_target_pairs={{0,4},{4,0},{8,12},{12,8},{1,5},{5,1},{9,13},{13,9},{2,6},{6,2},{1... | collective-permute-start | bytes 2359304 | tf_op jit(solution)/shard_map/ppermute | solution.py:344
  178.2 7.4 %collective-permute-start.21 = (bf16[128,3072]{1,0:T(8,128)(2,1)}, bf16[128,3072]{1,0:T(8,128)(2,1)S(1)}, u32[]{:S(2)}, u32[]{:S(2)}) collective-permute-start(bf16[128,3072]{1,0:T(8,128)(2,1)} %get-tuple-element.227), channel_id=1, source_target_pairs={{4,8},{8,4},{5,9},{9,5},{6,10},{10,6},{7,11},{11,7},{20,24},{24,20... | collective-permute-start | bytes 2359304 | tf_op jit(solution)/shard_map/ppermute | solution.py:344
  188.9 27.9 %collective-permute-start.18 = (bf16[128,3072]{1,0:T(8,128)(2,1)}, bf16[128,3072]{1,0:T(8,128)(2,1)S(1)}, u32[]{:S(2)}, u32[]{:S(2)}) collective-permute-start(bf16[128,3072]{1,0:T(8,128)(2,1)} %get-tuple-element.136), channel_id=1, source_target_pairs={{0,4},{4,0},{8,12},{12,8},{1,5},{5,1},{9,13},{13,9},{2,6},{6,2},{1... | collective-permute-start | bytes 2359304 | tf_op jit(solution)/shard_map/ppermute | solution.py:344
  198.2 18.7 %collective-permute-start.19 = (bf16[128,3072]{1,0:T(8,128)(2,1)}, bf16[128,3072]{1,0:T(8,128)(2,1)S(1)}, u32[]{:S(2)}, u32[]{:S(2)}) collective-permute-start(bf16[128,3072]{1,0:T(8,128)(2,1)} %get-tuple-element.137), channel_id=1, source_target_pairs={{4,8},{8,4},{5,9},{9,5},{6,10},{10,6},{7,11},{11,7},{20,24},{24,20... | collective-permute-start | bytes 2359304 | tf_op jit(solution)/shard_map/ppermute | solution.py:344
  201.3 32.4 %collective-permute-start.24 = (bf16[128,3072]{1,0:T(8,128)(2,1)S(1)}, bf16[128,3072]{1,0:T(8,128)(2,1)S(1)}, u32[]{:S(2)}, u32[]{:S(2)}) collective-permute-start(bf16[128,3072]{1,0:T(8,128)(2,1)S(1)} %get-tuple-element.149), channel_id=1, source_target_pairs={{0,4},{4,0},{8,12},{12,8},{1,5},{5,1},{9,13},{13,9},{2,6},{6,2},{1... | collective-permute-start | bytes 2359304 | tf_op jit(solution)/shard_map/ppermute | solution.py:344
  204.5 29.2 %collective-permute-start.25 = (bf16[128,3072]{1,0:T(8,128)(2,1)S(1)}, bf16[128,3072]{1,0:T(8,128)(2,1)S(1)}, u32[]{:S(2)}, u32[]{:S(2)}) collective-permute-start(bf16[128,3072]{1,0:T(8,128)(2,1)S(1)} %get-tuple-element.150), channel_id=1, source_target_pairs={{4,8},{8,4},{5,9},{9,5},{6,10},{10,6},{7,11},{11,7},{20,24},{24,20... | collective-permute-start | bytes 2359304 | tf_op jit(solution)/shard_map/ppermute | solution.py:344
  217.8 32.8 %collective-permute-start.22 = (bf16[128,3072]{1,0:T(8,128)(2,1)S(1)}, bf16[128,3072]{1,0:T(8,128)(2,1)S(1)}, u32[]{:S(2)}, u32[]{:S(2)}) collective-permute-start(bf16[128,3072]{1,0:T(8,128)(2,1)S(1)} %get-tuple-element.145), channel_id=1, source_target_pairs={{0,4},{4,0},{8,12},{12,8},{1,5},{5,1},{9,13},{13,9},{2,6},{6,2},{1... | collective-permute-start | bytes 2359304 | tf_op jit(solution)/shard_map/ppermute | solution.py:344
  221.6 29.0 %collective-permute-start.23 = (bf16[128,3072]{1,0:T(8,128)(2,1)S(1)}, bf16[128,3072]{1,0:T(8,128)(2,1)S(1)}, u32[]{:S(2)}, u32[]{:S(2)}) collective-permute-start(bf16[128,3072]{1,0:T(8,128)(2,1)S(1)} %get-tuple-element.146), channel_id=1, source_target_pairs={{4,8},{8,4},{5,9},{9,5},{6,10},{10,6},{7,11},{11,7},{20,24},{24,20... | collective-permute-start | bytes 2359304 | tf_op jit(solution)/shard_map/ppermute | solution.py:344
  234.6 24.6 %collective-permute-start.26 = (bf16[128,3072]{1,0:T(8,128)(2,1)S(1)}, bf16[128,3072]{1,0:T(8,128)(2,1)S(1)}, u32[]{:S(2)}, u32[]{:S(2)}) collective-permute-start(bf16[128,3072]{1,0:T(8,128)(2,1)S(1)} %get-tuple-element.158), channel_id=1, source_target_pairs={{0,4},{4,0},{8,12},{12,8},{1,5},{5,1},{9,13},{13,9},{2,6},{6,2},{1... | collective-permute-start | bytes 2359304 | tf_op jit(solution)/shard_map/ppermute | solution.py:344
  238.4 20.8 %collective-permute-start.27 = (bf16[128,3072]{1,0:T(8,128)(2,1)S(1)}, bf16[128,3072]{1,0:T(8,128)(2,1)S(1)}, u32[]{:S(2)}, u32[]{:S(2)}) collective-permute-start(bf16[128,3072]{1,0:T(8,128)(2,1)S(1)} %get-tuple-element.159), channel_id=1, source_target_pairs={{4,8},{8,4},{5,9},{9,5},{6,10},{10,6},{7,11},{11,7},{20,24},{24,20... | collective-permute-start | bytes 2359304 | tf_op jit(solution)/shard_map/ppermute | solution.py:344
  264.3 15.3 %collective-permute-start.28 = (bf16[256,1536]{1,0:T(8,128)(2,1)}, bf16[256,1536]{1,0:T(8,128)(2,1)}, u32[]{:S(2)}, u32[]{:S(2)}) collective-permute-start(bf16[256,1536]{1,0:T(8,128)(2,1)} %get-tuple-element.226), channel_id=1, source_target_pairs={{4,0},{8,12},{5,1},{9,13},{6,2},{10,14},{7,3},{11,15},{20,16},{24,... | collective-permute-start | bytes 2359304 | tf_op jit(solution)/shard_map/ppermute | solution.py:344
  289.2 58.1 %all-to-all-start = ((bf16[16,64,768]{2,1,0:T(8,128)(2,1)}), bf16[16,64,768]{2,1,0:T(8,128)(2,1)S(1)}, u32[]{:S(2)}, u32[]{:S(2)}) async-start(bf16[16,64,768]{2,1,0:T(8,128)(2,1)} %collective-permute-done.31), calls=%async_computation.1 | async-start | bytes 3145728 | tf_op jit(solution)/shard_map/all_to_all | solution.py:484
  296.7 41.1 %collective-permute-start.34 = (bf16[256,1536]{1,0:T(8,128)(2,1)S(1)}, bf16[256,1536]{1,0:T(8,128)(2,1)S(1)}, u32[]{:S(2)}, u32[]{:S(2)}) collective-permute-start(bf16[256,1536]{1,0:T(8,128)(2,1)S(1)} %copy-done.39), channel_id=1, source_target_pairs={{4,0},{8,12},{5,1},{9,13},{6,2},{10,14},{7,3},{11,15},{20,16},{24,... | collective-permute-start | bytes 2359304 | tf_op jit(solution)/shard_map/ppermute | solution.py:344
  298.3 39.8 %collective-permute-start.32 = (f32[2,3072]{1,0:T(2,128)S(1)}, f32[2,3072]{1,0:T(2,128)S(1)}, u32[]{:S(2)}, u32[]{:S(2)}) collective-permute-start(f32[2,3072]{1,0:T(2,128)S(1)} %maximum_add_fusion), channel_id=1, source_target_pairs={{0,4},{4,0},{8,12},{12,8},{1,5},{5,1},{9,13},{13,9},{2,6},{6,2},{1... | collective-permute-start | bytes 73736 | tf_op jit(solution)/shard_map/ppermute | solution.py:344
  338.1 8.6 %collective-permute-start.33 = (f32[2,3072]{1,0:T(2,128)S(1)}, f32[2,3072]{1,0:T(2,128)S(1)}, u32[]{:S(2)}, u32[]{:S(2)}) collective-permute-start(f32[2,3072]{1,0:T(2,128)S(1)} %add.154), channel_id=1, source_target_pairs={{0,8},{4,12},{8,0},{12,4},{1,9},{5,13},{9,1},{13,5},{2,10},{6,14},... | collective-permute-start | bytes 73736 | tf_op jit(solution)/shard_map/ppermute | solution.py:344
  (61 other events, 527.2 us)
Sparse Core Ops, SparseCore 0:
  9.9 72.9 all-gather.2
  186.7 77.1 reduce-scatter.1

commit v4 on v3

--- a/solution.py
+++ b/solution.py
@@ -150,7 +150,7 @@
     return out.reshape(count * rows, cols)
 
 
-def boundary_kernel(upper_ref, lower_ref, kept_ref, columns_ref, gain_ref, h_ref, bias_ref, section_ref, passed_ref, out_ref):
+def boundary_kernel(g_ref, kept_ref, columns_ref, gain_ref, h_ref, bias_ref, section_ref, passed_ref, out_ref):
     step = pl.program_id(0)
     first = section_ref[0] == 0
     groups = pl.num_programs(0)
@@ -161,8 +161,7 @@
     for f in range(out_ref.shape[0] // 4):
         cut = pl.ds(f * width, width)
         hat = (kept_ref[:, cut].astype(f32) - mean) * inverse
-        rows = jnp.where(step < 2, upper_ref[:, cut], lower_ref[:, cut])
-        grad = (inverse * (rows * gain_ref[:, cut] - one - hat * two)).astype(jnp.bfloat16)
+        grad = (inverse * (g_ref[:, cut] * gain_ref[:, cut] - one - hat * two)).astype(jnp.bfloat16)
         output = (h_ref[:, cut].astype(f32) + bias_ref[:, cut]).astype(jnp.bfloat16)
         passed_ref[:, cut] = jnp.where(first, grad, output)
         out_ref[jnp.where(first, step * groups + f, f * groups + step)] = jnp.where(
@@ -170,7 +169,7 @@
         )
 
 
-def boundary(upper, lower, kept_rows, columns, gain, summed, bias, section):
+def boundary(grad_rows, kept_rows, columns, gain, summed, bias, section):
     rows, cols = kept_rows.shape
     part = rows // 4
     wide = pl.BlockSpec((part, cols), lambda j: (j, 0))
@@ -179,9 +178,7 @@
         boundary_kernel,
         grid=(4,),
         in_specs=[
-            pl.BlockSpec((part, cols), lambda j: (jnp.minimum(j, 1), 0)),
-            pl.BlockSpec((part, cols), lambda j: (jnp.maximum(j - 2, 0), 0)),
-            wide, pl.BlockSpec((part, 4), lambda j: (j, 0)), line, wide, line,
+            wide, wide, pl.BlockSpec((part, 4), lambda j: (j, 0)), line, wide, line,
             pl.BlockSpec(memory_space=pltpu.SMEM),
         ],
         out_specs=[wide, pl.BlockSpec((16, part, cols // 4), lambda j: (0, 0, 0))],
@@ -192,7 +189,7 @@
         compiler_params=pltpu.CompilerParams(vmem_limit_bytes=32 * 2**20),
         cost_estimate=LIGHT,
     )(
-        upper, lower, kept_rows, columns, gain.reshape(1, cols), summed, bias.reshape(1, cols),
+        grad_rows, kept_rows, columns, gain.reshape(1, cols), summed, bias.reshape(1, cols),
         section.reshape(1),
     )
 
@@ -352,162 +349,93 @@
         return (one.astype(f32) + two.astype(f32)).astype(bf16)
 
     seq = lambda *values: lax.optimization_barrier(values)
-
-    sides = [slice(0, row_count // 2), slice(row_count // 2, row_count)]
     either = lambda from_inner, from_outer: jnp.where(inner, from_inner, from_outer)
-    u1a, u1b, a1, b1, a2, b2, a3, b3, a4, b4, a5, b5, x2 = (
-        [None, None] for unused in range(13)
-    )
 
     c_all = lax.all_gather(upstream, "mp", axis=0, tiled=True)
-    for k in range(2):
-        u1a[k] = along(fresh_rows[sides[k]], PAIRS)
-        u1b[k] = along(fresh_rows[sides[k]], MIDDLE)
+    u1a, u1b = along(fresh_rows, PAIRS), along(fresh_rows, MIDDLE)
     fresh, kept = fresh_rows.astype(f32), kept_rows.astype(f32)
     sums = jnp.stack(
         [jnp.sum(fresh, 1), jnp.sum(fresh * fresh, 1), jnp.sum(kept, 1), jnp.sum(kept * kept, 1)]
     )
-    u1a[0], u1b[0], sums = seq(u1a[0], u1b[0], sums)
     sums = sums + flip(sums, "mp", 1)
     stats = (sums + flip(sums, "mp", 2)) / full_width
     kept_hat, kept_inv = standardize(kept_rows, stats[2], stats[3])
     normed_kept = normed(kept_rows, stats[2:], gain, shift)
-
-    u1a[0], u1b[0], normed_kept, stats = seq(u1a[0], u1b[0], normed_kept, stats)
     pair_stats = jnp.stack([stats[:2], along(stats[:2], PAIRS)])
-    sent, stats = seq(either(u1b[0], normed_kept[sides[0]]), stats)
-    a1[0], b1[0] = along(sent, PAIRS), along(u1a[0], MIDDLE)
-    u1a[1], u1b[1], normed_kept, stats = seq(u1a[1], u1b[1], normed_kept, stats)
-    sent, stats = seq(either(u1b[1], normed_kept[sides[1]]), stats)
-    a1[1], b1[1] = along(sent, PAIRS), along(u1a[1], MIDDLE)
-    pair_stats, stats, u1a[1] = seq(pair_stats, stats, u1a[1])
+    u1a, u1b, normed_kept, pair_stats = seq(u1a, u1b, normed_kept, pair_stats)
+
+    a1, b1 = along(either(u1b, normed_kept), PAIRS), along(u1a, MIDDLE)
     h_stack = shares(
-        [
-            normed(fresh_rows, stats, gain, shift),
-            normed(jnp.concatenate(u1a), pair_stats[1], gain, shift),
-        ],
+        [normed(fresh_rows, stats, gain, shift), normed(u1a, pair_stats[1], gain, shift)],
         w, False, None, 0, 4, 4 * row_count,
     )
-
-    a1[0], b1[0], h_stack, pair_stats = seq(a1[0], b1[0], h_stack, pair_stats)
-    a2[0], b2[0] = along(b1[0], OUTWARD), along(a1[0], MIDDLE)
+    a1, b1, h_stack, c_all, pair_stats = seq(a1, b1, h_stack, c_all, pair_stats)
+
+    a2, b2 = along(b1, OUTWARD), along(a1, MIDDLE)
     all_stats = jnp.concatenate([pair_stats, along(pair_stats, [(s, s ^ 2) for s in range(4)])])
-    a1[1], b1[1], h_stack, all_stats, c_all = seq(a1[1], b1[1], h_stack, all_stats, c_all)
-    a2[1], b2[1] = along(b1[1], OUTWARD), along(a1[1], MIDDLE)
     g_stack = None
     for first in (0, 2):
         blocks = [((c_all, 0, b), (c_all, 1, b)) for b in (first, first + 1)]
         g_stack = shares(blocks, w, True, g_stack, first, 4, 4 * row_count)
-
-    def g_block(k, side):
-        return lax.dynamic_slice(
-            g_stack, (dp ^ k, side.start, 0), (1, side.stop - side.start, col_count)
-        )[0]
-
-    a2[0], b2[0], g_stack, normed_kept = seq(a2[0], b2[0], g_stack, normed_kept)
-    sent, g_stack = seq(either(b2[0], g_block(3, sides[0])), g_stack)
-    a3[0], b3[0] = along(sent, PAIRS), along(normed_kept[sides[0]], MIDDLE)
-    a2[1], b2[1], g_stack, normed_kept = seq(a2[1], b2[1], g_stack, normed_kept)
-    sent, h_stack = seq(either(b2[1], g_block(3, sides[1])), h_stack)
-    a3[1], b3[1] = along(sent, PAIRS), along(normed_kept[sides[1]], MIDDLE)
-    u2 = jnp.where(inner, jnp.concatenate(u1b), jnp.concatenate(a1))
-    u3 = jnp.where(inner, jnp.concatenate(b1), jnp.concatenate(a2))
+    a2, b2, g_stack, all_stats, normed_kept = seq(a2, b2, g_stack, all_stats, normed_kept)
+    g_block = lambda k: pick(g_stack, dp ^ k)
+
+    a3, b3 = along(either(b2, g_block(3)), PAIRS), along(normed_kept, MIDDLE)
+    two, three = jnp.where(inner, 3, 2), jnp.where(inner, 2, 3)
     h_stack = shares(
         [
-            normed(u2, pick(all_stats, jnp.where(inner, 3, 2)), gain, shift),
-            normed(u3, pick(all_stats, jnp.where(inner, 2, 3)), gain, shift),
+            normed(either(u1b, a1), pick(all_stats, two), gain, shift),
+            normed(either(b1, a2), pick(all_stats, three), gain, shift),
         ],
         w, False, h_stack, 2, 4, 4 * row_count,
     )
-
-    nothing = jnp.zeros((row_count // 2, col_count), bf16)
-
-    def fourth(k, chain):
-        x2[k] = added(g_block(2, sides[k]), jnp.where(inner, a3[k], nothing))
-        sent, x2[k], chain = seq(either(normed_kept[sides[k]], x2[k]), x2[k], chain)
-        a4[k], b4[k] = along(sent, PAIRS), along(x2[k], MIDDLE)
-        return chain
-
-    a3[0], b3[0], h_stack = seq(a3[0], b3[0], h_stack)
-    h_stack = fourth(0, h_stack)
-
-    places = [lax.bitwise_xor(dp, b) for b in range(4)]
+    a3, b3, h_stack = seq(a3, b3, h_stack)
+
+    x2 = added(g_block(2), jnp.where(inner, a3, jnp.zeros_like(a3)))
+    a4, b4 = along(either(normed_kept, x2), PAIRS), along(x2, MIDDLE)
+    places = [dp ^ b for b in range(4)]
     places = [jnp.where(inner & (at >= 2), at ^ 1, at) for at in places]
     h_all = reorder(h_stack, places)
-    a3[1], b3[1], h_all = seq(a3[1], b3[1], h_all)
     summed = lax.psum_scatter(h_all, "mp", scatter_dimension=0, tiled=True)
-    c_all = fourth(1, c_all)
     bias_grad = jnp.sum(c_all, 0, dtype=f32)
-    c_all = reorder(
-        c_all.reshape(4, row_count, col_count),
-        [dp, dp ^ 1, jnp.where(inner, dp ^ 3, dp ^ 2), jnp.where(inner, dp ^ 2, dp ^ 3)],
-    )
-
-    def fifth(k, chain):
-        one, two, chain = seq(
-            added(g_block(1, sides[k]), b4[k]), added(g_block(3, sides[k]), a4[k]), chain
-        )
-        a5[k], b5[k] = along(one, PAIRS), along(two, MIDDLE)
-        return chain
-
-    a4[0], b4[0], c_all, bias_grad = seq(a4[0], b4[0], c_all, bias_grad)
-    c_all = fifth(0, c_all)
-    a4[1], b4[1], c_all = seq(a4[1], b4[1], c_all)
-    c_all = fifth(1, c_all)
-
-    def gradient(k):
-        rows = g_block(0, sides[k]).astype(f32) + a5[k].astype(f32) + b5[k].astype(f32)
-        scaled, hat = rows * gain, kept_hat[sides[k]]
-        return (
-            rows,
-            jnp.stack([jnp.sum(scaled, 1), jnp.sum(scaled * hat, 1)]),
-            jnp.stack([jnp.sum(rows * hat, 0), jnp.sum(rows, 0)]),
-        )
-
-    near1 = jnp.concatenate(b3)
-    a5[0], b5[0], near1, c_all = seq(a5[0], b5[0], near1, c_all)
-    near3 = [along(near1[:, :half], OUTWARD), None]
-    upper, upper_terms, upper_sums = gradient(0)
-    a5[1], b5[1], upper_terms, upper_sums = seq(a5[1], b5[1], upper_terms, upper_sums)
-    lower, lower_terms, lower_sums = gradient(1)
-    row_terms = jnp.concatenate([upper_terms, lower_terms], 1)
+    c_all = reorder(c_all.reshape(4, row_count, col_count), [dp, dp ^ 1, dp ^ two, dp ^ three])
+    a4, b4, c_all, bias_grad = seq(a4, b4, c_all, bias_grad)
+
+    a5 = along(added(g_block(1), b4), PAIRS)
+    b5 = along(added(g_block(3), a4), MIDDLE)
+    near3 = [along(b3[:, :half], OUTWARD), None]
+    a5, b5, near3[0], b3 = seq(a5, b5, near3[0], b3)
+
+    near3[1] = along(b3[:, half:], OUTWARD)
+    grad_rows = g_block(0).astype(f32) + a5.astype(f32) + b5.astype(f32)
+    scaled = grad_rows * gain
+    row_terms = jnp.stack([jnp.sum(scaled, 1), jnp.sum(scaled * kept_hat, 1)])
+    column_sums = jnp.stack([jnp.sum(grad_rows * kept_hat, 0), jnp.sum(grad_rows, 0)])
     row_terms = row_terms + flip(row_terms, "mp", 1)
-    sent, row_terms = seq(near1[:, half:], row_terms)
-    near3[1] = along(sent, OUTWARD)
     row_terms = (row_terms + flip(row_terms, "mp", 2)) / full_width
     columns = jnp.stack([stats[2], kept_inv, row_terms[0], row_terms[1]], 1)
-    near3[0], columns = seq(near3[0], columns)
+    near3[1], columns = seq(near3[1], columns)
     passed, outgoing = boundary(
-        upper, lower, kept_rows, columns, gain, summed, bias.reshape(col_count), section
-    )
-    outgoing = flip(outgoing, "section", 1)
+        grad_rows, kept_rows, columns, gain, summed, bias.reshape(col_count), section
+    )
     arrived = lax.all_to_all(outgoing, ("dp", "mp"), split_axis=0, concat_axis=0, tiled=True)
 
-    column_sums, c_all, outgoing = seq(upper_sums + lower_sums, c_all, outgoing)
-    column_sums = column_sums + along(column_sums, PAIRS)
-    column_grads = column_sums + along(column_sums, [(s, s ^ 2) for s in range(4)])
-    width = half // 2
-    early = [
-        normed_kept,
-        jnp.where(inner, jnp.concatenate(a1), jnp.concatenate(a4)),
-        jnp.where(inner, jnp.concatenate(b2), jnp.concatenate(a3)),
-    ]
+    c_all, outgoing, near3[0], normed_kept = seq(c_all, outgoing, near3[0], normed_kept)
+    early = [normed_kept, either(a1, a4), either(b2, a3)]
     weight_grad = None
-    for k in range(4):
-        last = near3[k // 2]
-        if weight_grad is None:
-            last, c_all = seq(last, c_all)
-        else:
-            last, weight_grad = seq(last, weight_grad)
-        cut = lambda value: value[:, k * width:(k + 1) * width]
+    for k in range(2):
+        cut = lambda value: value[:, k * half:(k + 1) * half]
         own, one, three = (cut(value) for value in early)
-        two = jnp.where(inner, cut(near1), last[:, (k % 2) * width:(k % 2 + 1) * width])
-        weight_grad = grad_block(
-            jnp.concatenate([own, one, two, three]), c_all, weight_grad, k, 4
-        )
-        if k == 2:
-            arrived, column_grads, weight_grad = seq(arrived, column_grads, weight_grad)
-    next_in = joined(arrived, section)
+        kept_all = jnp.concatenate([own, one, either(cut(b3), near3[k]), three])
+        if weight_grad is not None:
+            kept_all, weight_grad = seq(kept_all, weight_grad)
+        weight_grad = grad_block(kept_all, c_all, weight_grad, k, 2)
+        if k == 0:
+            column_sums, weight_grad = seq(column_sums, weight_grad)
+            column_sums = column_sums + along(column_sums, PAIRS)
+            column_grads = column_sums + along(column_sums, [(s, s ^ 2) for s in range(4)])
+    arrived, column_grads, weight_grad = seq(arrived, column_grads, weight_grad)
+    next_in = joined(flip(arrived, "section", 1), section)
 
     return (
         next_in.reshape(fwd_in.shape),

time: 369 us -> 367 us (level)
  starting transfers between devices: 79.5 us -> 53.5 us
  waiting for transfers between devices: 108 us -> 133 us
    ppermute x30 -> x18, starting transfers between devices: 70.3 us -> 42.4 us  [shards_of_four(): along = lambda value, pairs: lax.ppermute(value, 'dp', pairs)]
    ppermute x30 -> x18, waiting for transfers between devices: 102 us -> 125 us  [shards_of_four(): along = lambda value, pairs: lax.ppermute(value, 'dp', pairs)]
    select_n x8 -> x0, other arithmetic: 9.24 us -> none  [the longest x1 2.58 us: shards_of_four(): u3 = jnp.where(inner, jnp.concatenate(b1), jnp.concatenate(a2))]
    select_n x6 -> x7, other arithmetic: 10.3 us -> 18.1 us  [shards_of_four(): jnp.where(inner, from_inner, from_outer)]
    convert_element_type x2 -> x1, other arithmetic: 1.18 us -> 5.14 us  [added(): return (one.astype(f32) + two.astype(f32)).astype(bf16)]
    pallas_call x4 -> x2, Pallas kernels: 31.7 us -> 28.2 us  [grad_block(): pl.pallas_call(grad_kernel, grid=(cols // step,), in_specs=specs, out_spe...]
    unnamed x111 -> x52, local copies, waits for them, and re-layouts: 28.9 us -> 27.8 us
  transfers between devices with their start and end apart: 38 -> 26, of which waited for: 12 -> 10; matrix products, arithmetic and copies ran while one was open for 11% -> 11% of each run, Pallas kernels for 23% -> 24%
where the time goes in v4:
time: 367 us; the launch traced here: 366 us
  waiting for transfers between devices  133 us (36%)
  Pallas kernels  95.4 us (26%)
  starting transfers between devices  53.5 us (15%)
  local copies, waits for them, and re-layouts  36 us (10%)
  other arithmetic  33.2 us (9%)
  between operations  14.6 us (4%)
    ppermute x18, waiting for transfers between devices, shards_of_four(): along = lambda value, pairs: lax.ppermute(value, 'dp', pairs)  125 us
    pallas_call x4, Pallas kernels, shares(): pl.pallas_call(functools.partial(share_kernel, count, turned), grid=(cols...  52.4 us
    ppermute x18, starting transfers between devices, shards_of_four(): along = lambda value, pairs: lax.ppermute(value, 'dp', pairs)  42.4 us
    pallas_call x2, Pallas kernels, grad_block(): pl.pallas_call(grad_kernel, grid=(cols // step,), in_specs=specs, out_spe...  28.2 us
    unnamed x52, local copies, waits for them, and re-layouts  27.8 us
    select_n x7, other arithmetic, shards_of_four(): jnp.where(inner, from_inner, from_outer)  18.1 us
    pallas_call x5, Pallas kernels, normed(): pl.pallas_call(normed_kernel, grid=(count // part,), in_specs=[wide, pl.B...  7.77 us
    ppermute x5, waiting for transfers between devices, flip(): return lax.ppermute(value, axis, [(s, s ^ mask) for s in range(n)])  7.62 us
  transfers between devices with their start and end apart: 26, of which 10 were waited for; matrix products, arithmetic and copies ran while one was open for 11% of the time, Pallas kernels for 24%

profile of v4, /device:TPU:0, one launch (start us, length us, event | category | flops | bytes accessed | tf_op | source)
XLA Modules:
  0.0 365.7 jit_solution(252912873929546953)
XLA Ops:
  10.5 4.7 %collective-permute-start = (bf16[256,3072]{1,0:T(8,128)(2,1)S(1)}, bf16[256,3072]{1,0:T(8,128)(2,1)}, u32[]{:S(2)}, u32[]{:S(2)}) collective-permute-start(bf16[256,3072]{1,0:T(8,128)(2,1)S(1)} %bitcast.134), channel_id=1, source_target_pairs={{0,4},{4,0},{8,12},{12,8},{1,5},{5,1},{9,13},{13,9},{2,6},{6,2},{1... | collective-permute-start | bytes 4718600 | tf_op jit(solution)/shard_map/ppermute | solution.py:341
  26.4 23.1 %collective-permute-done.4 = f32[2,256]{1,0:T(2,128)S(1)} collective-permute-done((f32[2,256]{1,0:T(2,128)S(1)}, f32[2,256]{1,0:T(2,128)S(1)}, u32[]{:S(2)}, u32[]{:S(2)}) %collective-permute-start.4) | collective-permute-done | bytes 2080 | tf_op jit(solution)/shard_map/ppermute | solution.py:341
  49.5 2.7 broadcast_select_fusion.5
  57.1 2.7 shard_map.112.refs_2_.refs_3_
  59.9 13.0 %shard_map.113.refs_5_ = bf16[4,256,3072]{2,1,0:T(8,128)(2,1)S(1)} custom-call(bf16[256,3072]{1,0:T(8,128)(2,1)S(1)} %shard_map.111.refs_0_.refs_1_, bf16[256,3072]{1,0:T(8,128)(2,1)S(1)} %shard_map.111.refs_0_.refs_1_, bf16[256,3072]{1,0:T(8,128)(2,1)S(1)} %shard_map.112.refs_2_.refs_3_, bf16[256,3072]{1,0:T(8,128)(2,1)S(1)} %shard_map.112.refs_2_.refs_3_, ...), custom_call_target="tpu_custom_call" | custom-call | flops 1 | bytes 1 | tf_op jit(solution)/shard_map/pallas_call | solution.py:96
  72.9 2.7 copy-done.6
  75.6 12.3 %collective-permute-done.5 = bf16[256,3072]{1,0:T(8,128)(2,1)} collective-permute-done((bf16[256,3072]{1,0:T(8,128)(2,1)}, bf16[256,3072]{1,0:T(8,128)(2,1)}, u32[]{:S(2)}, u32[]{:S(2)}) %collective-permute-start.5) | collective-permute-done | bytes 1572896 | tf_op jit(solution)/shard_map/ppermute | solution.py:341
  91.1 5.4 %collective-permute-start.9 = (f32[2,2,256]{2,1,0:T(2,128)S(1)}, f32[2,2,256]{2,1,0:T(2,128)S(1)}, u32[]{:S(2)}, u32[]{:S(2)}) collective-permute-start(f32[2,2,256]{2,1,0:T(2,128)S(1)} %pad_maximum_fusion.5), channel_id=1, source_target_pairs={{0,8},{4,12},{8,0},{12,4},{1,9},{5,13},{9,1},{13,5},{2,10},{6,14},... | collective-permute-start | bytes 12296 | tf_op jit(solution)/shard_map/ppermute | solution.py:341
  96.5 2.8 copy-done
  99.3 13.1 %shard_map.114.refs_5_ = bf16[4,256,3072]{2,1,0:T(8,128)(2,1)S(1)} custom-call(bf16[1024,3072]{1,0:T(8,128)(2,1)S(1)} %bitcast.112, bf16[1024,3072]{1,0:T(8,128)(2,1)S(1)} %bitcast.113, bf16[1024,3072]{1,0:T(8,128)(2,1)S(1)} %bitcast.114, bf16[1024,3072]{1,0:T(8,128)(2,1)S(1)} %bitcast.115, bf16[3072,3072]{1,0:T(8,128)(2,1)} %bitcast.138), custom_call_target="tpu_custom_call" | custom-call | flops 1 | bytes 1 | tf_op jit(solution)/shard_map/pallas_call | solution.py:96
  112.5 2.7 copy-done.3
  115.2 2.8 copy-done.1
  117.9 2.8 copy-done.4
  120.7 13.1 %shard_map.115 = bf16[4,256,3072]{2,1,0:T(8,128)(2,1)S(1)} custom-call(bf16[1024,3072]{1,0:T(8,128)(2,1)S(1)} %bitcast.116, bf16[1024,3072]{1,0:T(8,128)(2,1)S(1)} %bitcast.117, bf16[1024,3072]{1,0:T(8,128)(2,1)S(1)} %bitcast.118, bf16[1024,3072]{1,0:T(8,128)(2,1)S(1)} %bitcast.119, bf16[3072,3072]{1,0:T(8,128)(2,1)} %bitcast.139, ...), custom_call_target="tpu_custom_call", output_to_operand_aliasing={{}: (5, {})} | custom-call | flops 1 | bytes 1 | tf_op jit(solution)/shard_map/pallas_call | solution.py:96
  140.0 2.9 broadcast_select_fusion.4.rows_ref
  148.4 13.0 %shard_map.118.stack_ref = bf16[4,256,3072]{2,1,0:T(8,128)(2,1)S(1)} custom-call(bf16[256,3072]{1,0:T(8,128)(2,1)S(1)} %shard_map.116.refs_0_.refs_1_, bf16[256,3072]{1,0:T(8,128)(2,1)S(1)} %shard_map.116.refs_0_.refs_1_, bf16[256,3072]{1,0:T(8,128)(2,1)S(1)} %shard_map.117.refs_2_.refs_3_, ...), custom_call_target="tpu_custom_call", output_to_operand_aliasing={{}: (5, {})} | custom-call | flops 1 | bytes 1 | tf_op jit(solution)/shard_map/pallas_call | solution.py:96
  161.4 9.6 %collective-permute-done.10 = bf16[256,3072]{1,0:T(8,128)(2,1)} collective-permute-done((bf16[256,3072]{1,0:T(8,128)(2,1)}, bf16[256,3072]{1,0:T(8,128)(2,1)}, u32[]{:S(2)}, u32[]{:S(2)}) %collective-permute-start.10) | collective-permute-done | bytes 1572896 | tf_op jit(solution)/shard_map/ppermute | solution.py:341
  172.0 2.7 copy-done.8
  174.7 5.4 %broadcast_select_fusion.2 = (bf16[256,3072]{1,0:T(8,128)(2,1)}, bf16[256,3072]{1,0:T(8,128)(2,1)}, bf16[256,3072]{1,0:T(8,128)(2,1)}) fusion(bf16[256,3072]{1,0:T(8,128)(2,1)} %shard_map.110, pred[]{:T(512)S(6)} %or.3, bf16[256,3072]{1,0:T(8,128)(2,1)} %collective-permute-done.10, bf16[4,256,3072]{2,1,0:T(8,128)(2,1)} %copy-done.5, s32[]{:T(128)S(6)} %select_n.89, ...), kind=kLoop, calls=%fused_computation.26 | loop fusion | flops 5505024 | bytes 11010053 | tf_op jit(solution)/shard_map/jit(_where)/select_n | solution.py:352
  180.2 4.6 %collective-permute-start.12 = (bf16[256,3072]{1,0:T(8,128)(2,1)}, bf16[256,3072]{1,0:T(8,128)(2,1)}, u32[]{:S(2)}, u32[]{:S(2)}) collective-permute-start(bf16[256,3072]{1,0:T(8,128)(2,1)} %get-tuple-element.92), channel_id=1, source_target_pairs={{0,4},{4,0},{8,12},{12,8},{1,5},{5,1},{9,13},{13,9},{2,6},{6,2},{1... | collective-permute-start | bytes 4718600 | tf_op jit(solution)/shard_map/ppermute | solution.py:341
  186.7 2.8 copy-done.2
  194.7 21.9 %collective-permute-done.12 = bf16[256,3072]{1,0:T(8,128)(2,1)} collective-permute-done((bf16[256,3072]{1,0:T(8,128)(2,1)}, bf16[256,3072]{1,0:T(8,128)(2,1)}, u32[]{:S(2)}, u32[]{:S(2)}) %collective-permute-start.12) | collective-permute-done | bytes 1572896 | tf_op jit(solution)/shard_map/ppermute | solution.py:341
  216.7 5.1 %add_convert_fusion = (bf16[256,3072]{1,0:T(8,128)(2,1)}, bf16[256,3072]{1,0:T(8,128)(2,1)S(1)}) fusion(bf16[256,3072]{1,0:T(8,128)(2,1)} %collective-permute-done.12, bf16[4,256,3072]{2,1,0:T(8,128)(2,1)} %copy-done.5, s32[]{:T(128)S(6)} %select_n.90, bf16[256,3072]{1,0:T(8,128)(2,1)} %collective-permute-done.13, s32[]{:T(128)S(6)} %select_n.88), kind=kLoop, calls=%fused_computation.21 | loop fusion | flops 6291456 | bytes 9437192 | tf_op jit(solution)/shard_map/convert_element_type | solution.py:349
  223.8 4.1 %collective-permute-start.14 = (bf16[256,3072]{1,0:T(8,128)(2,1)S(1)}, bf16[256,3072]{1,0:T(8,128)(2,1)}, u32[]{:S(2)}, u32[]{:S(2)}) collective-permute-start(bf16[256,3072]{1,0:T(8,128)(2,1)S(1)} %get-tuple-element.99), channel_id=1, source_target_pairs={{0,4},{4,0},{8,12},{12,8},{1,5},{5,1},{9,13},{13,9},{2,6},{6,2},{1... | collective-permute-start | bytes 4718600 | tf_op jit(solution)/shard_map/ppermute | solution.py:341
  231.3 44.0 %collective-permute-done.16 = bf16[256,1536]{1,0:T(8,128)(2,1)} collective-permute-done((bf16[256,1536]{1,0:T(8,128)(2,1)}, bf16[256,1536]{1,0:T(8,128)(2,1)}, u32[]{:S(2)}, u32[]{:S(2)}) %collective-permute-start.16) | collective-permute-done | bytes 786464 | tf_op jit(solution)/shard_map/ppermute | solution.py:341
  275.3 5.8 %fusion.6 = (f32[3072]{0:T(1024)S(1)}, f32[256]{0:T(256)S(1)}, f32[256]{0:T(256)S(1)}, f32[3072]{0:T(1024)S(1)}, f32[256,3072]{1,0:T(8,128)}) fusion(f32[256]{0:T(256)S(1)} %add_rsqrt_fusion, f32[256]{0:T(256)S(1)} %bitcast.166, bf16[1,1,1,256,3072]{4,3,2,1,0:T(8,128)(2,1)S(1)} %copy-done.10, f32[3072]{0:T(1024)S(1)} %bitcast.136, ...), kind=kLoop, calls=%fused_computation.12 | loop fusion | flops 11789824 | bytes 9478148 | tf_op jit(solution)/shard_map/reduce_sum | solution.py:413
  289.1 11.2 %collective-permute-done.17 = bf16[256,1536]{1,0:T(8,128)(2,1)} collective-permute-done((bf16[256,1536]{1,0:T(8,128)(2,1)S(1)}, bf16[256,1536]{1,0:T(8,128)(2,1)}, u32[]{:S(2)}, u32[]{:S(2)}) %collective-permute-start.17) | collective-permute-done | bytes 786464 | tf_op jit(solution)/shard_map/ppermute | solution.py:341
  303.7 3.3 shard_map.121
  307.0 4.9 %all-to-all-start = ((bf16[16,64,768]{2,1,0:T(8,128)(2,1)}), bf16[16,64,768]{2,1,0:T(8,128)(2,1)S(1)}, u32[]{:S(2)}, u32[]{:S(2)}) async-start(bf16[16,64,768]{2,1,0:T(8,128)(2,1)} %get-tuple-element.67), calls=%async_computation.1 | async-start | bytes 3145728 | tf_op jit(solution)/shard_map/all_to_all | solution.py:421
  318.4 14.1 %shard_map.122.rest_0_ = f32[3072,3072]{1,0:T(8,128)} custom-call(bf16[1024,1536]{1,0:T(8,128)(2,1)S(1)} %pad_maximum_fusion.v_ref, bf16[1024,3072]{1,0:T(8,128)(2,1)S(1)} %bitcast.128), custom_call_target="tpu_custom_call" | custom-call | flops 1 | bytes 1 | tf_op jit(solution)/shard_map/pallas_call | solution.py:43
  339.0 14.1 %shard_map.123 = f32[3072,3072]{1,0:T(8,128)} custom-call(bf16[1024,1536]{1,0:T(8,128)(2,1)S(1)} %pad_maximum_fusion.1.v_ref, bf16[1024,3072]{1,0:T(8,128)(2,1)S(1)} %bitcast.129, f32[3072,3072]{1,0:T(8,128)} %shard_map.122.rest_0_), custom_call_target="tpu_custom_call", output_to_operand_aliasing={{}: (2, {})} | custom-call | flops 1 | bytes 1 | tf_op jit(solution)/shard_map/pallas_call | solution.py:43
  353.8 3.4 collective-permute-done.22.pieces_ref
  (143 shorter events, 74.0 us)
Async XLA Ops:
  7.2 80.7 %all-gather.3.cloned.1.call-start = ((), (), s32[]{:S(2)}) async-start(), calls=%async_computation.3 | async-start | bytes 7864320 | tf_op jit(solution)/shard_map/all_gather | solution.py:354
  7.9 292.5 %reduce-scatter.2.cloned.1.call-start = ((), (), s32[]{:S(2)}) async-start(), calls=%async_computation.2 | async-start | bytes 7864320 | tf_op jit(solution)/shard_map/reduce_scatter | solution.py:399
  8.6 15.6 %copy-start.15 = (f32[1,3072]{1,0:T(1,128)S(1)}, f32[1,3072]{1,0:T(1,128)}, u32[]{:S(2)}) copy-start(f32[1,3072]{1,0:T(1,128)} %gain_ref.11) | copy-start | bytes 36868
  8.6 15.6 %copy-start.16 = (f32[1,3072]{1,0:T(1,128)S(1)}, f32[1,3072]{1,0:T(1,128)}, u32[]{:S(2)}) copy-start(f32[1,3072]{1,0:T(1,128)} %shift_ref.9) | copy-start | bytes 36868
  8.6 41.0 %collective-permute-start.1 = (bf16[256,3072]{1,0:T(8,128)(2,1)S(1)}, bf16[256,3072]{1,0:T(8,128)(2,1)}, u32[]{:S(2)}, u32[]{:S(2)}) collective-permute-start(bf16[256,3072]{1,0:T(8,128)(2,1)S(1)} %bitcast.133), channel_id=1, source_target_pairs={{4,8},{8,4},{5,9},{9,5},{6,10},{10,6},{7,11},{11,7},{20,24},{24,20... | collective-permute-start | bytes 4718600 | tf_op jit(solution)/shard_map/ppermute | solution.py:341
  10.5 39.0 %collective-permute-start = (bf16[256,3072]{1,0:T(8,128)(2,1)S(1)}, bf16[256,3072]{1,0:T(8,128)(2,1)}, u32[]{:S(2)}, u32[]{:S(2)}) collective-permute-start(bf16[256,3072]{1,0:T(8,128)(2,1)S(1)} %bitcast.134), channel_id=1, source_target_pairs={{0,4},{4,0},{8,12},{12,8},{1,5},{5,1},{9,13},{13,9},{2,6},{6,2},{1... | collective-permute-start | bytes 4718600 | tf_op jit(solution)/shard_map/ppermute | solution.py:341
  16.5 3.7 %collective-permute-start.2 = (f32[4,256]{1,0:T(4,128)S(1)}, f32[4,256]{1,0:T(4,128)S(1)}, u32[]{:S(2)}, u32[]{:S(2)}) collective-permute-start(f32[4,256]{1,0:T(4,128)S(1)} %pad_maximum_fusion.4), channel_id=1, source_target_pairs={{0,1},{1,0},{2,3},{3,2},{4,5},{5,4},{6,7},{7,6},{8,9},{9,8},{10,11... | collective-permute-start | bytes 12296 | tf_op jit(solution)/shard_map/ppermute | solution.py:16
  20.2 3.7 %collective-permute-start.3 = (f32[4,256]{1,0:T(4,128)S(1)}, f32[4,256]{1,0:T(4,128)S(1)}, u32[]{:S(2)}, u32[]{:S(2)}) collective-permute-start(f32[4,256]{1,0:T(4,128)S(1)} %fusion.28), channel_id=1, source_target_pairs={{0,2},{1,3},{2,0},{3,1},{4,6},{5,7},{6,4},{7,5},{8,10},{9,11},{10,... | collective-permute-start | bytes 12296 | tf_op jit(solution)/shard_map/ppermute | solution.py:16
  23.9 25.6 %collective-permute-start.4 = (f32[2,256]{1,0:T(2,128)S(1)}, f32[2,256]{1,0:T(2,128)S(1)}, u32[]{:S(2)}, u32[]{:S(2)}) collective-permute-start(f32[2,256]{1,0:T(2,128)S(1)} %get-tuple-element.118), channel_id=1, source_target_pairs={{0,4},{4,0},{8,12},{12,8},{1,5},{5,1},{9,13},{13,9},{2,6},{6,2},{1... | collective-permute-start | bytes 6152 | tf_op jit(solution)/shard_map/ppermute | solution.py:341
  52.3 35.6 %collective-permute-start.5 = (bf16[256,3072]{1,0:T(8,128)(2,1)}, bf16[256,3072]{1,0:T(8,128)(2,1)}, u32[]{:S(2)}, u32[]{:S(2)}) collective-permute-start(bf16[256,3072]{1,0:T(8,128)(2,1)} %broadcast_select_fusion.5), channel_id=1, source_target_pairs={{0,4},{4,0},{8,12},{12,8},{1,5},{5,1},{9,13},{13,9},{2,6},{6,2},{1... | collective-permute-start | bytes 4718600 | tf_op jit(solution)/shard_map/ppermute | solution.py:341
  54.0 33.9 %collective-permute-start.6 = (bf16[256,3072]{1,0:T(8,128)(2,1)}, bf16[256,3072]{1,0:T(8,128)(2,1)}, u32[]{:S(2)}, u32[]{:S(2)}) collective-permute-start(bf16[256,3072]{1,0:T(8,128)(2,1)} %collective-permute-done.rows_ref), channel_id=1, source_target_pairs={{4,8},{8,4},{5,9},{9,5},{6,10},{10,6},{7,11},{11,7},{20,24},{24,20... | collective-permute-start | bytes 4718600 | tf_op jit(solution)/shard_map/ppermute | solution.py:341
  87.9 46.0 %collective-permute-start.7 = (bf16[256,3072]{1,0:T(8,128)(2,1)}, bf16[256,3072]{1,0:T(8,128)(2,1)S(1)}, u32[]{:S(2)}, u32[]{:S(2)}) collective-permute-start(bf16[256,3072]{1,0:T(8,128)(2,1)} %collective-permute-done.6), channel_id=1, source_target_pairs={{4,0},{8,12},{5,1},{9,13},{6,2},{10,14},{7,3},{11,15},{20,16},{24,... | collective-permute-start | bytes 4718600 | tf_op jit(solution)/shard_map/ppermute | solution.py:341
  89.2 44.8 %collective-permute-start.8 = (bf16[256,3072]{1,0:T(8,128)(2,1)}, bf16[256,3072]{1,0:T(8,128)(2,1)}, u32[]{:S(2)}, u32[]{:S(2)}) collective-permute-start(bf16[256,3072]{1,0:T(8,128)(2,1)} %collective-permute-done.5), channel_id=1, source_target_pairs={{4,8},{8,4},{5,9},{9,5},{6,10},{10,6},{7,11},{11,7},{20,24},{24,20... | collective-permute-start | bytes 4718600 | tf_op jit(solution)/shard_map/ppermute | solution.py:341
  91.1 42.8 %collective-permute-start.9 = (f32[2,2,256]{2,1,0:T(2,128)S(1)}, f32[2,2,256]{2,1,0:T(2,128)S(1)}, u32[]{:S(2)}, u32[]{:S(2)}) collective-permute-start(f32[2,2,256]{2,1,0:T(2,128)S(1)} %pad_maximum_fusion.5), channel_id=1, source_target_pairs={{0,8},{4,12},{8,0},{12,4},{1,9},{5,13},{9,1},{13,5},{2,10},{6,14},... | collective-permute-start | bytes 12296 | tf_op jit(solution)/shard_map/ppermute | solution.py:341
  133.9 9.0 %copy-start.5 = (bf16[4,256,3072]{2,1,0:T(8,128)(2,1)}, bf16[4,256,3072]{2,1,0:T(8,128)(2,1)S(1)}, u32[]{:S(2)}) copy-start(bf16[4,256,3072]{2,1,0:T(8,128)(2,1)S(1)} %shard_map.115) | copy-start | bytes 18874372
  135.5 35.5 %collective-permute-start.10 = (bf16[256,3072]{1,0:T(8,128)(2,1)}, bf16[256,3072]{1,0:T(8,128)(2,1)}, u32[]{:S(2)}, u32[]{:S(2)}) collective-permute-start(bf16[256,3072]{1,0:T(8,128)(2,1)} %bitcast_select_fusion), channel_id=1, source_target_pairs={{0,4},{4,0},{8,12},{12,8},{1,5},{5,1},{9,13},{13,9},{2,6},{6,2},{1... | collective-permute-start | bytes 4718600 | tf_op jit(solution)/shard_map/ppermute | solution.py:341
  138.1 32.8 %collective-permute-start.11 = (bf16[256,3072]{1,0:T(8,128)(2,1)}, bf16[256,3072]{1,0:T(8,128)(2,1)}, u32[]{:S(2)}, u32[]{:S(2)}) collective-permute-start(bf16[256,3072]{1,0:T(8,128)(2,1)} %shard_map.110), channel_id=1, source_target_pairs={{4,8},{8,4},{5,9},{9,5},{6,10},{10,6},{7,11},{11,7},{20,24},{24,20... | collective-permute-start | bytes 4718600 | tf_op jit(solution)/shard_map/ppermute | solution.py:341
  174.7 18.5 %slice-start = ((s8[6291456]{0:T(1024)(128)(4,1)}), s8[2097152]{0:T(1024)(128)(4,1)S(1)}, s32[]{:S(2)}) async-start(s8[6291456]{0:T(1024)(128)(4,1)} %bitcast.121), calls=%async_computation.4 | async-start | bytes 4194304
  180.2 36.5 %collective-permute-start.12 = (bf16[256,3072]{1,0:T(8,128)(2,1)}, bf16[256,3072]{1,0:T(8,128)(2,1)}, u32[]{:S(2)}, u32[]{:S(2)}) collective-permute-start(bf16[256,3072]{1,0:T(8,128)(2,1)} %get-tuple-element.92), channel_id=1, source_target_pairs={{0,4},{4,0},{8,12},{12,8},{1,5},{5,1},{9,13},{13,9},{2,6},{6,2},{1... | collective-permute-start | bytes 4718600 | tf_op jit(solution)/shard_map/ppermute | solution.py:341
  184.8 31.9 %collective-permute-start.13 = (bf16[256,3072]{1,0:T(8,128)(2,1)}, bf16[256,3072]{1,0:T(8,128)(2,1)}, u32[]{:S(2)}, u32[]{:S(2)}) collective-permute-start(bf16[256,3072]{1,0:T(8,128)(2,1)} %get-tuple-element.93), channel_id=1, source_target_pairs={{4,8},{8,4},{5,9},{9,5},{6,10},{10,6},{7,11},{11,7},{20,24},{24,20... | collective-permute-start | bytes 4718600 | tf_op jit(solution)/shard_map/ppermute | solution.py:341
  221.8 53.5 %copy-start.10 = (bf16[1,1,1,256,3072]{4,3,2,1,0:T(8,128)(2,1)S(1)}, bf16[1,1,1,256,3072]{4,3,2,1,0:T(8,128)(2,1)}, u32[]{:S(2)}) copy-start(bf16[1,1,1,256,3072]{4,3,2,1,0:T(8,128)(2,1)} %param.8) | copy-start | bytes 4718596
  221.8 53.5 %collective-permute-start.15 = (bf16[256,3072]{1,0:T(8,128)(2,1)}, bf16[256,3072]{1,0:T(8,128)(2,1)}, u32[]{:S(2)}, u32[]{:S(2)}) collective-permute-start(bf16[256,3072]{1,0:T(8,128)(2,1)} %get-tuple-element.98), channel_id=1, source_target_pairs={{4,8},{8,4},{5,9},{9,5},{6,10},{10,6},{7,11},{11,7},{20,24},{24,20... | collective-permute-start | bytes 4718600 | tf_op jit(solution)/shard_map/ppermute | solution.py:341
  223.8 51.5 %collective-permute-start.14 = (bf16[256,3072]{1,0:T(8,128)(2,1)S(1)}, bf16[256,3072]{1,0:T(8,128)(2,1)}, u32[]{:S(2)}, u32[]{:S(2)}) collective-permute-start(bf16[256,3072]{1,0:T(8,128)(2,1)S(1)} %get-tuple-element.99), channel_id=1, source_target_pairs={{0,4},{4,0},{8,12},{12,8},{1,5},{5,1},{9,13},{13,9},{2,6},{6,2},{1... | collective-permute-start | bytes 4718600 | tf_op jit(solution)/shard_map/ppermute | solution.py:341
  230.0 45.3 %collective-permute-start.16 = (bf16[256,1536]{1,0:T(8,128)(2,1)}, bf16[256,1536]{1,0:T(8,128)(2,1)}, u32[]{:S(2)}, u32[]{:S(2)}) collective-permute-start(bf16[256,1536]{1,0:T(8,128)(2,1)} %slice.94), channel_id=1, source_target_pairs={{4,0},{8,12},{5,1},{9,13},{6,2},{10,14},{7,3},{11,15},{20,16},{24,... | collective-permute-start | bytes 2359304 | tf_op jit(solution)/shard_map/ppermute | solution.py:341
  281.1 4.0 %collective-permute-start.18 = (f32[2,256]{1,0:T(2,128)S(1)}, f32[2,256]{1,0:T(2,128)S(1)}, u32[]{:S(2)}, u32[]{:S(2)}) collective-permute-start(f32[2,256]{1,0:T(2,128)S(1)} %pad_maximum_fusion.12), channel_id=1, source_target_pairs={{0,1},{1,0},{2,3},{3,2},{4,5},{5,4},{6,7},{7,6},{8,9},{9,8},{10,11... | collective-permute-start | bytes 6152 | tf_op jit(solution)/shard_map/ppermute | solution.py:16
  283.9 16.4 %collective-permute-start.17 = (bf16[256,1536]{1,0:T(8,128)(2,1)S(1)}, bf16[256,1536]{1,0:T(8,128)(2,1)}, u32[]{:S(2)}, u32[]{:S(2)}) collective-permute-start(bf16[256,1536]{1,0:T(8,128)(2,1)S(1)} %slice.95), channel_id=1, source_target_pairs={{4,0},{8,12},{5,1},{9,13},{6,2},{10,14},{7,3},{11,15},{20,16},{24,... | collective-permute-start | bytes 2359304 | tf_op jit(solution)/shard_map/ppermute | solution.py:341
  285.2 3.8 %collective-permute-start.19 = (f32[2,256]{1,0:T(2,128)S(1)}, f32[2,256]{1,0:T(2,128)S(1)}, u32[]{:S(2)}, u32[]{:S(2)}) collective-permute-start(f32[2,256]{1,0:T(2,128)S(1)} %fusion.27), channel_id=1, source_target_pairs={{0,2},{1,3},{2,0},{3,1},{4,6},{5,7},{6,4},{7,5},{8,10},{9,11},{10,... | collective-permute-start | bytes 6152 | tf_op jit(solution)/shard_map/ppermute | solution.py:16
  286.6 13.8 %copy-start.17 = (f32[1,3072]{1,0:T(1,128)S(1)}, f32[1,3072]{1,0:T(1,128)}, u32[]{:S(2)}) copy-start(f32[1,3072]{1,0:T(1,128)} %bias_ref.1) | copy-start | bytes 36868
  307.0 46.7 %all-to-all-start = ((bf16[16,64,768]{2,1,0:T(8,128)(2,1)}), bf16[16,64,768]{2,1,0:T(8,128)(2,1)S(1)}, u32[]{:S(2)}, u32[]{:S(2)}) async-start(bf16[16,64,768]{2,1,0:T(8,128)(2,1)} %get-tuple-element.67), calls=%async_computation.1 | async-start | bytes 3145728 | tf_op jit(solution)/shard_map/all_to_all | solution.py:421
  332.5 3.8 %collective-permute-start.20 = (f32[2,3072]{1,0:T(2,128)S(1)}, f32[2,3072]{1,0:T(2,128)S(1)}, u32[]{:S(2)}, u32[]{:S(2)}) collective-permute-start(f32[2,3072]{1,0:T(2,128)S(1)} %pad_maximum_fusion.2), channel_id=1, source_target_pairs={{0,4},{4,0},{8,12},{12,8},{1,5},{5,1},{9,13},{13,9},{2,6},{6,2},{1... | collective-permute-start | bytes 73736 | tf_op jit(solution)/shard_map/ppermute | solution.py:341
  336.3 16.8 %collective-permute-start.21 = (f32[2,3072]{1,0:T(2,128)S(1)}, f32[2,3072]{1,0:T(2,128)S(1)}, u32[]{:S(2)}, u32[]{:S(2)}) collective-permute-start(f32[2,3072]{1,0:T(2,128)S(1)} %add.126), channel_id=1, source_target_pairs={{0,8},{4,12},{8,0},{12,4},{1,9},{5,13},{9,1},{13,5},{2,10},{6,14},... | collective-permute-start | bytes 73736 | tf_op jit(solution)/shard_map/ppermute | solution.py:341
  353.8 3.4 collective-permute-start.22
  (20 other events, 67.5 us)
Sparse Core Ops, SparseCore 0:
  9.9 72.8 all-gather.2
  174.8 71.4 reduce-scatter.1

commit v5 on v4

--- a/solution.py
+++ b/solution.py
@@ -8,6 +8,7 @@
 from jax.sharding import PartitionSpec as P
 
 eps = 1e-05
+GRANT = 56 * 2**20
 LIGHT = pl.CostEstimate(flops=1, bytes_accessed=1, transcendentals=0)
 
 
@@ -48,7 +49,7 @@
         out_shape=jax.ShapeDtypeStruct((width * blocks, cols), jnp.float32),
         scratch_shapes=[pltpu.VMEM((width, tokens), jnp.bfloat16)],
         input_output_aliases=aliases,
-        compiler_params=pltpu.CompilerParams(vmem_limit_bytes=32 * 2**20),
+        compiler_params=pltpu.CompilerParams(vmem_limit_bytes=GRANT),
         cost_estimate=LIGHT,
     )(*operands)
 
@@ -100,7 +101,7 @@
         out_specs=pl.BlockSpec((count, rows, step), lambda j: (place // count, 0, j)),
         out_shape=jax.ShapeDtypeStruct((total, rows, cols), jnp.bfloat16),
         input_output_aliases=aliases,
-        compiler_params=pltpu.CompilerParams(vmem_limit_bytes=32 * 2**20),
+        compiler_params=pltpu.CompilerParams(vmem_limit_bytes=GRANT),
         cost_estimate=LIGHT,
     )(*operands)
 
@@ -124,7 +125,7 @@
         in_specs=[wide, pl.BlockSpec((part, 2), lambda j: (j, 0)), line, line],
         out_specs=wide,
         out_shape=jax.ShapeDtypeStruct((count, cols), jnp.bfloat16),
-        compiler_params=pltpu.CompilerParams(vmem_limit_bytes=32 * 2**20),
+        compiler_params=pltpu.CompilerParams(vmem_limit_bytes=GRANT),
         cost_estimate=LIGHT,
     )(rows, stats, gain.reshape(1, cols), shift.reshape(1, cols))
 
@@ -144,10 +145,112 @@
             out_specs=pl.BlockSpec((1, rows, cols), lambda j, order: (j, 0, 0)),
         ),
         out_shape=jax.ShapeDtypeStruct(stack.shape, stack.dtype),
-        compiler_params=pltpu.CompilerParams(vmem_limit_bytes=32 * 2**20),
+        compiler_params=pltpu.CompilerParams(vmem_limit_bytes=GRANT),
         cost_estimate=LIGHT,
     )(jnp.stack(order).astype(jnp.int32), stack)
     return out.reshape(count * rows, cols)
+
+
+def turn_kernel(at_ref, share_ref, arrived_ref, kept_ref, sent_ref, sum_ref):
+    inner = at_ref[1] == 1
+    f32 = jnp.float32
+    arrived = arrived_ref[...].astype(f32)
+    total = share_ref[0].astype(f32) + jnp.where(inner, arrived, jnp.zeros_like(arrived))
+    total = total.astype(jnp.bfloat16)
+    sum_ref[...] = total
+    sent_ref[...] = jnp.where(inner, kept_ref[...], total)
+
+
+def turn(stack, at, arrived, kept, inner):
+    count, rows, cols = stack.shape
+    part = 64
+    wide = pl.BlockSpec((part, cols), lambda j, at: (j, 0))
+    return pl.pallas_call(
+        turn_kernel,
+        grid_spec=pltpu.PrefetchScalarGridSpec(
+            num_scalar_prefetch=1,
+            grid=(rows // part,),
+            in_specs=[pl.BlockSpec((1, part, cols), lambda j, at: (at[0], j, 0)), wide, wide],
+            out_specs=[wide, wide],
+        ),
+        out_shape=[jax.ShapeDtypeStruct((rows, cols), stack.dtype)] * 2,
+        compiler_params=pltpu.CompilerParams(vmem_limit_bytes=GRANT),
+        cost_estimate=LIGHT,
+    )(jnp.stack([at, inner.astype(jnp.int32)]).astype(jnp.int32), stack, arrived, kept)
+
+
+def joint_sums_kernel(at_ref, one_ref, two_ref, first_ref, second_ref, out_one, out_two):
+    f32, bf16 = jnp.float32, jnp.bfloat16
+    out_one[...] = (one_ref[0].astype(f32) + first_ref[...].astype(f32)).astype(bf16)
+    out_two[...] = (two_ref[0].astype(f32) + second_ref[...].astype(f32)).astype(bf16)
+
+
+def joint_sums(stack, at_one, at_two, first, second):
+    count, rows, cols = stack.shape
+    part = 64
+    wide = pl.BlockSpec((part, cols), lambda j, at: (j, 0))
+    return pl.pallas_call(
+        joint_sums_kernel,
+        grid_spec=pltpu.PrefetchScalarGridSpec(
+            num_scalar_prefetch=1,
+            grid=(rows // part,),
+            in_specs=[
+                pl.BlockSpec((1, part, cols), lambda j, at: (at[0], j, 0)),
+                pl.BlockSpec((1, part, cols), lambda j, at: (at[1], j, 0)),
+                wide,
+                wide,
+            ],
+            out_specs=[wide, wide],
+        ),
+        out_shape=[jax.ShapeDtypeStruct((rows, cols), stack.dtype)] * 2,
+        compiler_params=pltpu.CompilerParams(vmem_limit_bytes=GRANT),
+        cost_estimate=LIGHT,
+    )(jnp.stack([at_one, at_two]).astype(jnp.int32), stack, stack, first, second)
+
+
+def gradient_kernel(at_ref, share_ref, a_ref, b_ref, kept_ref, stats_ref, gain_ref, rows_ref, terms_ref, sums_ref):
+    f32 = jnp.float32
+    stats = stats_ref[...]
+    rows = share_ref[0].astype(f32) + a_ref[...].astype(f32) + b_ref[...].astype(f32)
+    hat = (kept_ref[...].astype(f32) - stats[:, 0:1]) * stats[:, 1:2]
+    rows_ref[...] = rows
+    scaled = rows * gain_ref[...]
+    terms_ref[:, 0:1] = jnp.sum(scaled, 1, keepdims=True)
+    terms_ref[:, 1:2] = jnp.sum(scaled * hat, 1, keepdims=True)
+
+    @pl.when(pl.program_id(0) == 0)
+    def _():
+        sums_ref[...] = jnp.zeros_like(sums_ref)
+
+    sums_ref[0:1, :] += jnp.sum(rows * hat, 0, keepdims=True)
+    sums_ref[1:2, :] += jnp.sum(rows, 0, keepdims=True)
+
+
+def gradient(stack, at, a, b, kept_rows, stats, gain):
+    count, rows, cols = stack.shape
+    part = 64
+    wide = pl.BlockSpec((part, cols), lambda j, at: (j, 0))
+    narrow = pl.BlockSpec((part, 2), lambda j, at: (j, 0))
+    return pl.pallas_call(
+        gradient_kernel,
+        grid_spec=pltpu.PrefetchScalarGridSpec(
+            num_scalar_prefetch=1,
+            grid=(rows // part,),
+            in_specs=[
+                pl.BlockSpec((1, part, cols), lambda j, at: (at[0], j, 0)),
+                wide, wide, wide, narrow,
+                pl.BlockSpec((1, cols), lambda j, at: (0, 0)),
+            ],
+            out_specs=[wide, narrow, pl.BlockSpec((2, cols), lambda j, at: (0, 0))],
+        ),
+        out_shape=[
+            jax.ShapeDtypeStruct((rows, cols), jnp.float32),
+            jax.ShapeDtypeStruct((rows, 2), jnp.float32),
+            jax.ShapeDtypeStruct((2, cols), jnp.float32),
+        ],
+        compiler_params=pltpu.CompilerParams(vmem_limit_bytes=GRANT),
+        cost_estimate=LIGHT,
+    )(at.reshape(1).astype(jnp.int32), stack, a, b, kept_rows, stats, gain.reshape(1, cols))
 
 
 def boundary_kernel(g_ref, kept_ref, columns_ref, gain_ref, h_ref, bias_ref, section_ref, passed_ref, out_ref):
@@ -186,7 +289,7 @@
             jax.ShapeDtypeStruct((rows, cols), jnp.bfloat16),
             jax.ShapeDtypeStruct((16, part, cols // 4), jnp.bfloat16),
         ],
-        compiler_params=pltpu.CompilerParams(vmem_limit_bytes=32 * 2**20),
+        compiler_params=pltpu.CompilerParams(vmem_limit_bytes=GRANT),
         cost_estimate=LIGHT,
     )(
         grad_rows, kept_rows, columns, gain.reshape(1, cols), summed, bias.reshape(1, cols),
@@ -213,7 +316,7 @@
         ],
         out_specs=pl.BlockSpec((part, 4 * width), lambda j: (j, 0)),
         out_shape=jax.ShapeDtypeStruct((4 * part, 4 * width), pieces.dtype),
-        compiler_params=pltpu.CompilerParams(vmem_limit_bytes=32 * 2**20),
+        compiler_params=pltpu.CompilerParams(vmem_limit_bytes=GRANT),
         cost_estimate=LIGHT,
     )(pieces, section.reshape(1))
 
@@ -341,13 +444,6 @@
     along = lambda value, pairs: lax.ppermute(value, "dp", pairs)
     pick = lambda stack, k: lax.dynamic_index_in_dim(stack, k, 0, keepdims=False)
 
-    def standardize(values, mean, square_mean):
-        inverse = lax.rsqrt(square_mean - mean * mean + eps)
-        return (values.astype(f32) - mean[:, None]) * inverse[:, None], inverse
-
-    def added(one, two):
-        return (one.astype(f32) + two.astype(f32)).astype(bf16)
-
     seq = lambda *values: lax.optimization_barrier(values)
     either = lambda from_inner, from_outer: jnp.where(inner, from_inner, from_outer)
 
@@ -359,7 +455,7 @@
     )
     sums = sums + flip(sums, "mp", 1)
     stats = (sums + flip(sums, "mp", 2)) / full_width
-    kept_hat, kept_inv = standardize(kept_rows, stats[2], stats[3])
+    kept_inv = lax.rsqrt(stats[3] - stats[2] * stats[2] + eps)
     normed_kept = normed(kept_rows, stats[2:], gain, shift)
     pair_stats = jnp.stack([stats[:2], along(stats[:2], PAIRS)])
     u1a, u1b, normed_kept, pair_stats = seq(u1a, u1b, normed_kept, pair_stats)
@@ -391,8 +487,9 @@
     )
     a3, b3, h_stack = seq(a3, b3, h_stack)
 
-    x2 = added(g_block(2), jnp.where(inner, a3, jnp.zeros_like(a3)))
-    a4, b4 = along(either(normed_kept, x2), PAIRS), along(x2, MIDDLE)
+    sent, x2 = turn(g_stack, dp ^ 2, a3, normed_kept, inner)
+    h_stack, c_all, x2 = seq(h_stack, c_all, x2)
+    a4, b4 = along(sent, PAIRS), along(x2, MIDDLE)
     places = [dp ^ b for b in range(4)]
     places = [jnp.where(inner & (at >= 2), at ^ 1, at) for at in places]
     h_all = reorder(h_stack, places)
@@ -401,20 +498,23 @@
     c_all = reorder(c_all.reshape(4, row_count, col_count), [dp, dp ^ 1, dp ^ two, dp ^ three])
     a4, b4, c_all, bias_grad = seq(a4, b4, c_all, bias_grad)
 
-    a5 = along(added(g_block(1), b4), PAIRS)
-    b5 = along(added(g_block(3), a4), MIDDLE)
+    one, two_sums = joint_sums(g_stack, dp ^ 1, dp ^ 3, b4, a4)
+    a5, b5 = along(one, PAIRS), along(two_sums, MIDDLE)
     near3 = [along(b3[:, :half], OUTWARD), None]
     a5, b5, near3[0], b3 = seq(a5, b5, near3[0], b3)
 
     near3[1] = along(b3[:, half:], OUTWARD)
-    grad_rows = g_block(0).astype(f32) + a5.astype(f32) + b5.astype(f32)
-    scaled = grad_rows * gain
-    row_terms = jnp.stack([jnp.sum(scaled, 1), jnp.sum(scaled * kept_hat, 1)])
-    column_sums = jnp.stack([jnp.sum(grad_rows * kept_hat, 0), jnp.sum(grad_rows, 0)])
+    grad_rows, row_terms, column_sums = gradient(
+        g_stack, dp, a5, b5, kept_rows, jnp.stack([stats[2], kept_inv], 1), gain
+    )
+    row_terms = row_terms.T
     row_terms = row_terms + flip(row_terms, "mp", 1)
+    column_sums = column_sums + along(column_sums, PAIRS)
+    row_terms, column_sums = seq(row_terms, column_sums)
     row_terms = (row_terms + flip(row_terms, "mp", 2)) / full_width
+    column_grads = column_sums + along(column_sums, [(s, s ^ 2) for s in range(4)])
     columns = jnp.stack([stats[2], kept_inv, row_terms[0], row_terms[1]], 1)
-    near3[1], columns = seq(near3[1], columns)
+    near3[1], columns, column_grads = seq(near3[1], columns, column_grads)
     passed, outgoing = boundary(
         grad_rows, kept_rows, columns, gain, summed, bias.reshape(col_count), section
     )
@@ -426,15 +526,12 @@
     for k in range(2):
         cut = lambda value: value[:, k * half:(k + 1) * half]
         own, one, three = (cut(value) for value in early)
-        kept_all = jnp.concatenate([own, one, either(cut(b3), near3[k]), three])
+        last = near3[k]
         if weight_grad is not None:
-            kept_all, weight_grad = seq(kept_all, weight_grad)
+            last, weight_grad = seq(last, weight_grad)
+        kept_all = jnp.concatenate([own, one, either(cut(b3), last), three])
         weight_grad = grad_block(kept_all, c_all, weight_grad, k, 2)
-        if k == 0:
-            column_sums, weight_grad = seq(column_sums, weight_grad)
-            column_sums = column_sums + along(column_sums, PAIRS)
-            column_grads = column_sums + along(column_sums, [(s, s ^ 2) for s in range(4)])
-    arrived, column_grads, weight_grad = seq(arrived, column_grads, weight_grad)
+    arrived, weight_grad = seq(arrived, weight_grad)
     next_in = joined(flip(arrived, "section", 1), section)
 
     return (

time: 367 us -> 367 us (level)
  Pallas kernels: 95.4 us -> 153 us
  waiting for transfers between devices: 133 us -> 111 us
  local copies, waits for them, and re-layouts: 36 us -> 14.6 us
  other arithmetic: 33.2 us -> 25.9 us
  starting transfers between devices: 53.5 us -> 46.7 us
    ppermute x18, waiting for transfers between devices: 125 us -> 101 us  [shards_of_four(): along = lambda value, pairs: lax.ppermute(value, 'dp', pairs)]
    unnamed x52 -> x28, local copies, waits for them, and re-layouts: 27.8 us -> 5.94 us
    pallas_call x0 -> x3, Pallas kernels: none -> 16.7 us  [the longest x1 5.8 us: gradient(): pl.pallas_call(gradient_kernel, grid_spec=pltpu.PrefetchScalarGridSpec(nu...]
    pallas_call x2, Pallas kernels: 2.05 us -> 14.3 us  [reorder(): pl.pallas_call(reorder_kernel, grid_spec=pltpu.PrefetchScalarGridSpec(num...]
    pallas_call x5, Pallas kernels: 7.77 us -> 19.9 us  [normed(): pl.pallas_call(normed_kernel, grid=(count // part,), in_specs=[wide, pl.B...]
    pallas_call x4, Pallas kernels: 52.4 us -> 60.6 us  [shares(): pl.pallas_call(functools.partial(share_kernel, count, turned), grid=(cols...]
    ppermute x18, starting transfers between devices: 42.4 us -> 35.6 us  [shards_of_four(): along = lambda value, pairs: lax.ppermute(value, 'dp', pairs)]
    reduce_sum x1 -> x0, other arithmetic: 5.78 us -> none  [shards_of_four(): jnp.sum(grad_rows * kept_hat, 0)]
  transfers between devices with their start and end apart: 26 -> 26, of which waited for: 10 -> 13; matrix products, arithmetic and copies ran while one was open for 11% -> 9% of each run, Pallas kernels for 24% -> 36%
where the time goes in v5:
time: 367 us; the launch traced here: 365 us
  Pallas kernels  153 us (42%)
  waiting for transfers between devices  111 us (30%)
  starting transfers between devices  46.7 us (13%)
  other arithmetic  25.9 us (7%)
  local copies, waits for them, and re-layouts  14.6 us (4%)
  between operations  14.4 us (4%)
    ppermute x18, waiting for transfers between devices, shards_of_four(): along = lambda value, pairs: lax.ppermute(value, 'dp', pairs)  101 us
    pallas_call x4, Pallas kernels, shares(): pl.pallas_call(functools.partial(share_kernel, count, turned), grid=(cols...  60.6 us
    ppermute x18, starting transfers between devices, shards_of_four(): along = lambda value, pairs: lax.ppermute(value, 'dp', pairs)  35.6 us
    pallas_call x2, Pallas kernels, grad_block(): pl.pallas_call(grad_kernel, grid=(cols // step,), in_specs=specs, out_spe...  32.2 us
    pallas_call x5, Pallas kernels, normed(): pl.pallas_call(normed_kernel, grid=(count // part,), in_specs=[wide, pl.B...  19.9 us
    select_n x8, other arithmetic, shards_of_four(): jnp.where(inner, from_inner, from_outer)  14.8 us
    pallas_call x2, Pallas kernels, reorder(): pl.pallas_call(reorder_kernel, grid_spec=pltpu.PrefetchScalarGridSpec(num...  14.3 us
    ppermute x5, waiting for transfers between devices, flip(): return lax.ppermute(value, axis, [(s, s ^ mask) for s in range(n)])  9.27 us
  transfers between devices with their start and end apart: 26, of which 13 were waited for; matrix products, arithmetic and copies ran while one was open for 9% of the time, Pallas kernels for 36%

profile of v5, /device:TPU:0, one launch (start us, length us, event | category | flops | bytes accessed | tf_op | source)
XLA Modules:
  0.0 365.1 jit_solution(18159015235839462261)
XLA Ops:
  8.7 5.8 %collective-permute-start = (bf16[256,3072]{1,0:T(8,128)(2,1)}, bf16[256,3072]{1,0:T(8,128)(2,1)}, u32[]{:S(2)}, u32[]{:S(2)}) collective-permute-start(bf16[256,3072]{1,0:T(8,128)(2,1)} %bitcast.121), channel_id=1, source_target_pairs={{0,4},{4,0},{8,12},{12,8},{1,5},{5,1},{9,13},{13,9},{2,6},{6,2},{1... | collective-permute-start | bytes 4718600 | tf_op jit(solution)/shard_map/ppermute | solution.py:444
  18.8 2.1 collective-permute-done.2
  25.6 4.0 %shard_map.110.kept_ref = bf16[256,3072]{1,0:T(8,128)(2,1)} custom-call(bf16[256,3072]{1,0:T(8,128)(2,1)} %bitcast.117, f32[256,2]{1,0:T(8,128)} %copy.43.stats_ref, f32[1,3072]{1,0:T(1,128)} %gain_ref.13, f32[1,3072]{1,0:T(1,128)} %shift_ref.9), custom_call_target="tpu_custom_call" | custom-call | flops 1 | bytes 1 | tf_op jit(solution)/shard_map/pallas_call | solution.py:122
  29.5 19.5 %collective-permute-done.4 = f32[2,256]{1,0:T(2,128)S(1)} collective-permute-done((f32[2,256]{1,0:T(2,128)S(1)}, f32[2,256]{1,0:T(2,128)S(1)}, u32[]{:S(2)}, u32[]{:S(2)}) %collective-permute-start.4) | collective-permute-done | bytes 2080 | tf_op jit(solution)/shard_map/ppermute | solution.py:444
  55.7 4.0 %shard_map.111.refs_0_.refs_1_ = bf16[256,3072]{1,0:T(8,128)(2,1)} custom-call(bf16[256,3072]{1,0:T(8,128)(2,1)} %bitcast.122, f32[256,2]{1,0:T(8,128)} %copy.44.stats_ref, f32[1,3072]{1,0:T(1,128)} %gain_ref.13, f32[1,3072]{1,0:T(1,128)} %shift_ref.9), custom_call_target="tpu_custom_call" | custom-call | flops 1 | bytes 1 | tf_op jit(solution)/shard_map/pallas_call | solution.py:122
  59.6 4.0 %shard_map.112.refs_2_.refs_3_ = bf16[256,3072]{1,0:T(8,128)(2,1)} custom-call(bf16[256,3072]{1,0:T(8,128)(2,1)} %collective-permute-done.rows_ref, f32[256,2]{1,0:T(8,128)} %copy.45.stats_ref, f32[1,3072]{1,0:T(1,128)} %gain_ref.13, f32[1,3072]{1,0:T(1,128)} %shift_ref.9), custom_call_target="tpu_custom_call" | custom-call | flops 1 | bytes 1 | tf_op jit(solution)/shard_map/pallas_call | solution.py:122
  63.6 15.1 %shard_map.113.refs_5_ = bf16[4,256,3072]{2,1,0:T(8,128)(2,1)} custom-call(bf16[256,3072]{1,0:T(8,128)(2,1)} %shard_map.111.refs_0_.refs_1_, bf16[256,3072]{1,0:T(8,128)(2,1)} %shard_map.111.refs_0_.refs_1_, bf16[256,3072]{1,0:T(8,128)(2,1)} %shard_map.112.refs_2_.refs_3_, bf16[256,3072]{1,0:T(8,128)(2,1)} %shard_map.112.refs_2_.refs_3_, ...), custom_call_target="tpu_custom_call" | custom-call | flops 1 | bytes 1 | tf_op jit(solution)/shard_map/pallas_call | solution.py:97
  78.7 8.4 %collective-permute-done.5 = bf16[256,3072]{1,0:T(8,128)(2,1)S(1)} collective-permute-done((bf16[256,3072]{1,0:T(8,128)(2,1)S(1)}, bf16[256,3072]{1,0:T(8,128)(2,1)S(1)}, u32[]{:S(2)}, u32[]{:S(2)}) %collective-permute-start.5) | collective-permute-done | bytes 1572896 | tf_op jit(solution)/shard_map/ppermute | solution.py:444
  90.3 6.7 %collective-permute-start.9 = (f32[2,2,256]{2,1,0:T(2,128)S(1)}, f32[2,2,256]{2,1,0:T(2,128)S(1)}, u32[]{:S(2)}, u32[]{:S(2)}) collective-permute-start(f32[2,2,256]{2,1,0:T(2,128)S(1)} %pad_maximum_fusion.4), channel_id=1, source_target_pairs={{0,8},{4,12},{8,0},{12,4},{1,9},{5,13},{9,1},{13,5},{2,10},{6,14},... | collective-permute-start | bytes 12296 | tf_op jit(solution)/shard_map/ppermute | solution.py:444
  97.6 15.2 %shard_map.114.refs_5_ = bf16[4,256,3072]{2,1,0:T(8,128)(2,1)} custom-call(bf16[1024,3072]{1,0:T(8,128)(2,1)} %bitcast.97, bf16[1024,3072]{1,0:T(8,128)(2,1)} %bitcast.98, bf16[1024,3072]{1,0:T(8,128)(2,1)} %bitcast.99, bf16[1024,3072]{1,0:T(8,128)(2,1)} %bitcast.100, bf16[3072,3072]{1,0:T(8,128)(2,1)} %bitcast.110), custom_call_target="tpu_custom_call" | custom-call | flops 1 | bytes 1 | tf_op jit(solution)/shard_map/pallas_call | solution.py:97
  112.8 15.2 %shard_map.115.share_ref.one_ref.two_ref = bf16[4,256,3072]{2,1,0:T(8,128)(2,1)} custom-call(bf16[1024,3072]{1,0:T(8,128)(2,1)} %bitcast.101, bf16[1024,3072]{1,0:T(8,128)(2,1)} %bitcast.102, bf16[1024,3072]{1,0:T(8,128)(2,1)} %bitcast.103, bf16[1024,3072]{1,0:T(8,128)(2,1)} %bitcast.104, ...), custom_call_target="tpu_custom_call", output_to_operand_aliasing={{}: (5, {})} | custom-call | flops 1 | bytes 1 | tf_op jit(solution)/shard_map/pallas_call | solution.py:97
  129.2 2.9 bitcast_select_fusion
  137.8 2.7 broadcast_select_fusion.2.rows_ref
  141.2 4.0 %shard_map.116.refs_0_.refs_1_ = bf16[256,3072]{1,0:T(8,128)(2,1)} custom-call(bf16[256,3072]{1,0:T(8,128)(2,1)} %broadcast_select_fusion.3.rows_ref, f32[256,2]{1,0:T(8,128)} %copy.46.stats_ref, f32[1,3072]{1,0:T(1,128)} %gain_ref.13, f32[1,3072]{1,0:T(1,128)} %shift_ref.9), custom_call_target="tpu_custom_call" | custom-call | flops 1 | bytes 1 | tf_op jit(solution)/shard_map/pallas_call | solution.py:122
  145.1 4.0 %shard_map.117.refs_2_.refs_3_ = bf16[256,3072]{1,0:T(8,128)(2,1)} custom-call(bf16[256,3072]{1,0:T(8,128)(2,1)} %broadcast_select_fusion.2.rows_ref, f32[256,2]{1,0:T(8,128)} %copy.47.stats_ref, f32[1,3072]{1,0:T(1,128)} %gain_ref.13, f32[1,3072]{1,0:T(1,128)} %shift_ref.9), custom_call_target="tpu_custom_call" | custom-call | flops 1 | bytes 1 | tf_op jit(solution)/shard_map/pallas_call | solution.py:122
  149.2 15.1 %shard_map.118.stack_ref = bf16[4,256,3072]{2,1,0:T(8,128)(2,1)} custom-call(bf16[256,3072]{1,0:T(8,128)(2,1)} %shard_map.116.refs_0_.refs_1_, bf16[256,3072]{1,0:T(8,128)(2,1)} %shard_map.116.refs_0_.refs_1_, bf16[256,3072]{1,0:T(8,128)(2,1)} %shard_map.117.refs_2_.refs_3_, ...), custom_call_target="tpu_custom_call", output_to_operand_aliasing={{}: (5, {})} | custom-call | flops 1 | bytes 1 | tf_op jit(solution)/shard_map/pallas_call | solution.py:97
  165.3 5.3 %shard_map.119 = (bf16[256,3072]{1,0:T(8,128)(2,1)}, bf16[256,3072]{1,0:T(8,128)(2,1)}) custom-call(s32[2]{0:T(128)} %pad_add_fusion.1.at_ref, bf16[4,256,3072]{2,1,0:T(8,128)(2,1)} %shard_map.115.share_ref.one_ref.two_ref, bf16[256,3072]{1,0:T(8,128)(2,1)} %collective-permute-done.10.arrived_ref, bf16[256,3072]{1,0:T(8,128)(2,1)} %shard_map.110.kept_ref), custom_call_target="tpu_custom_call" | custom-call | flops 1 | bytes 1 | tf_op jit(solution)/shard_map/pallas_call | solution.py:168
  170.6 6.6 %shard_map.123 = bf16[4,256,3072]{2,1,0:T(8,128)(2,1)} custom-call(s32[4]{0:T(128)} %pad_add_fusion.3.order_ref, bf16[4,256,3072]{2,1,0:T(8,128)(2,1)} %shard_map.118.stack_ref), custom_call_target="tpu_custom_call" | custom-call | flops 1 | bytes 1 | tf_op jit(solution)/shard_map/pallas_call | solution.py:139
  179.2 5.4 %collective-permute-start.12 = (bf16[256,3072]{1,0:T(8,128)(2,1)}, bf16[256,3072]{1,0:T(8,128)(2,1)}, u32[]{:S(2)}, u32[]{:S(2)}) collective-permute-start(bf16[256,3072]{1,0:T(8,128)(2,1)} %get-tuple-element.69), channel_id=1, source_target_pairs={{0,4},{4,0},{8,12},{12,8},{1,5},{5,1},{9,13},{13,9},{2,6},{6,2},{1... | collective-permute-start | bytes 4718600 | tf_op jit(solution)/shard_map/ppermute | solution.py:444
  185.8 7.7 %shard_map.120 = bf16[4,256,3072]{2,1,0:T(8,128)(2,1)} custom-call(s32[4]{0:T(128)} %pad_add_fusion.2.order_ref, bf16[4,256,3072]{2,1,0:T(8,128)(2,1)} %bitcast.105), custom_call_target="tpu_custom_call" | custom-call | flops 1 | bytes 1 | tf_op jit(solution)/shard_map/pallas_call | solution.py:139
  195.0 19.9 %collective-permute-done.12.second_ref = bf16[256,3072]{1,0:T(8,128)(2,1)} collective-permute-done((bf16[256,3072]{1,0:T(8,128)(2,1)}, bf16[256,3072]{1,0:T(8,128)(2,1)}, u32[]{:S(2)}, u32[]{:S(2)}) %collective-permute-start.12) | collective-permute-done | bytes 1572896 | tf_op jit(solution)/shard_map/ppermute | solution.py:444
  215.0 5.6 %shard_map.121 = (bf16[256,3072]{1,0:T(8,128)(2,1)}, bf16[256,3072]{1,0:T(8,128)(2,1)}) custom-call(s32[2]{0:T(128)} %pad_add_fusion.at_ref, bf16[4,256,3072]{2,1,0:T(8,128)(2,1)} %shard_map.115.share_ref.one_ref.two_ref, bf16[4,256,3072]{2,1,0:T(8,128)(2,1)} %shard_map.115.share_ref.one_ref.two_ref, bf16[256,3072]{1,0:T(8,128)(2,1)} %collective-permute-done.13.first_ref, ...), custom_call_target="tpu_custom_call" | custom-call | flops 1 | bytes 1 | tf_op jit(solution)/shard_map/pallas_call | solution.py:192
  223.1 2.1 slice.96
  226.5 42.4 %collective-permute-done.16 = bf16[256,1536]{1,0:T(8,128)(2,1)} collective-permute-done((bf16[256,1536]{1,0:T(8,128)(2,1)}, bf16[256,1536]{1,0:T(8,128)(2,1)}, u32[]{:S(2)}, u32[]{:S(2)}) %collective-permute-start.16) | collective-permute-done | bytes 786464 | tf_op jit(solution)/shard_map/ppermute | solution.py:444
  271.2 5.8 %shard_map.122 = (f32[256,3072]{1,0:T(8,128)}, f32[256,2]{1,0:T(8,128)}, f32[2,3072]{1,0:T(2,128)}) custom-call(s32[1]{0:T(128)} %bitcast.at_ref, bf16[4,256,3072]{2,1,0:T(8,128)(2,1)} %shard_map.115.share_ref.one_ref.two_ref, bf16[256,3072]{1,0:T(8,128)(2,1)} %copy-done.7, bf16[256,3072]{1,0:T(8,128)(2,1)} %copy-done.8, bf16[256,3072]{1,0:T(8,128)(2,1)} %bitcast.118, ...), custom_call_target="tpu_custom_call" | custom-call | flops 1 | bytes 1 | tf_op jit(solution)/shard_map/pallas_call | solution.py:234
  291.9 5.5 %collective-permute-done.17 = bf16[256,1536]{1,0:T(8,128)(2,1)} collective-permute-done((bf16[256,1536]{1,0:T(8,128)(2,1)S(1)}, bf16[256,1536]{1,0:T(8,128)(2,1)}, u32[]{:S(2)}, u32[]{:S(2)}) %collective-permute-start.17) | collective-permute-done | bytes 786464 | tf_op jit(solution)/shard_map/ppermute | solution.py:444
  298.1 5.8 %shard_map.124 = (bf16[256,3072]{1,0:T(8,128)(2,1)}, bf16[16,64,768]{2,1,0:T(8,128)(2,1)}) custom-call(f32[256,3072]{1,0:T(8,128)} %get-tuple-element.81.g_ref, bf16[256,3072]{1,0:T(8,128)(2,1)} %bitcast.119, f32[256,4]{1,0:T(8,128)} %copy.49.columns_ref, f32[1,3072]{1,0:T(1,128)} %gain_ref.13, bf16[256,3072]{1,0:T(8,128)(2,1)} %reduce-scatter.2.cloned.1.call-done.h_ref, ...), custom_call_target="tpu_custom_call" | custom-call | flops 1 | bytes 1 | tf_op jit(solution)/shard_map/pallas_call | solution.py:280
  303.9 4.5 %all-to-all-start = ((bf16[16,64,768]{2,1,0:T(8,128)(2,1)}), bf16[16,64,768]{2,1,0:T(8,128)(2,1)}, u32[]{:S(2)}, u32[]{:S(2)}) async-start(bf16[16,64,768]{2,1,0:T(8,128)(2,1)} %get-tuple-element.89), calls=%async_computation.1 | async-start | bytes 3145728 | tf_op jit(solution)/shard_map/all_to_all | solution.py:521
  314.9 16.1 %shard_map.125.rest_0_ = f32[3072,3072]{1,0:T(8,128)} custom-call(bf16[1024,1536]{1,0:T(8,128)(2,1)} %pad_maximum_fusion.v_ref, bf16[1024,3072]{1,0:T(8,128)(2,1)} %bitcast.114), custom_call_target="tpu_custom_call" | custom-call | flops 1 | bytes 1 | tf_op jit(solution)/shard_map/pallas_call | solution.py:44
  334.3 16.1 %shard_map.126 = f32[3072,3072]{1,0:T(8,128)} custom-call(bf16[1024,1536]{1,0:T(8,128)(2,1)} %pad_maximum_fusion.1.v_ref, bf16[1024,3072]{1,0:T(8,128)(2,1)} %bitcast.115, f32[3072,3072]{1,0:T(8,128)} %shard_map.125.rest_0_), custom_call_target="tpu_custom_call", output_to_operand_aliasing={{}: (2, {})} | custom-call | flops 1 | bytes 1 | tf_op jit(solution)/shard_map/pallas_call | solution.py:44
  350.4 3.6 collective-permute-done.22.pieces_ref
  355.2 3.1 shard_map.127
  (118 shorter events, 66.6 us)
Async XLA Ops:
  7.2 9.4 %copy-start = (bf16[1,1,1,256,3072]{4,3,2,1,0:T(8,128)(2,1)S(1)}, bf16[1,1,1,256,3072]{4,3,2,1,0:T(8,128)(2,1)}, u32[]{:S(2)}) copy-start(bf16[1,1,1,256,3072]{4,3,2,1,0:T(8,128)(2,1)} %param.8) | copy-start | bytes 4718596
  7.2 80.0 %all-gather.3.cloned.1.call-start = ((), (), s32[]{:S(2)}) async-start(), calls=%async_computation.3 | async-start | bytes 7864320 | tf_op jit(solution)/shard_map/all_gather | solution.py:450
  7.9 290.2 %reduce-scatter.2.cloned.1.call-start = ((), (), s32[]{:S(2)}) async-start(), calls=%async_computation.2 | async-start | bytes 7864320 | tf_op jit(solution)/shard_map/reduce_scatter | solution.py:496
  8.0 41.0 %collective-permute-start.1 = (bf16[256,3072]{1,0:T(8,128)(2,1)}, bf16[256,3072]{1,0:T(8,128)(2,1)S(1)}, u32[]{:S(2)}, u32[]{:S(2)}) collective-permute-start(bf16[256,3072]{1,0:T(8,128)(2,1)} %bitcast.120), channel_id=1, source_target_pairs={{4,8},{8,4},{5,9},{9,5},{6,10},{10,6},{7,11},{11,7},{20,24},{24,20... | collective-permute-start | bytes 4718600 | tf_op jit(solution)/shard_map/ppermute | solution.py:444
  8.7 40.3 %collective-permute-start = (bf16[256,3072]{1,0:T(8,128)(2,1)}, bf16[256,3072]{1,0:T(8,128)(2,1)}, u32[]{:S(2)}, u32[]{:S(2)}) collective-permute-start(bf16[256,3072]{1,0:T(8,128)(2,1)} %bitcast.121), channel_id=1, source_target_pairs={{0,4},{4,0},{8,12},{12,8},{1,5},{5,1},{9,13},{13,9},{2,6},{6,2},{1... | collective-permute-start | bytes 4718600 | tf_op jit(solution)/shard_map/ppermute | solution.py:444
  17.2 3.7 %collective-permute-start.2 = (f32[4,256]{1,0:T(4,128)S(1)}, f32[4,256]{1,0:T(4,128)S(1)}, u32[]{:S(2)}, u32[]{:S(2)}) collective-permute-start(f32[4,256]{1,0:T(4,128)S(1)} %pad_maximum_fusion.3), channel_id=1, source_target_pairs={{0,1},{1,0},{2,3},{3,2},{4,5},{5,4},{6,7},{7,6},{8,9},{9,8},{10,11... | collective-permute-start | bytes 12296 | tf_op jit(solution)/shard_map/ppermute | solution.py:17
  20.9 3.7 %collective-permute-start.3 = (f32[4,256]{1,0:T(4,128)S(1)}, f32[4,256]{1,0:T(4,128)S(1)}, u32[]{:S(2)}, u32[]{:S(2)}) collective-permute-start(f32[4,256]{1,0:T(4,128)S(1)} %fusion.20), channel_id=1, source_target_pairs={{0,2},{1,3},{2,0},{3,1},{4,6},{5,7},{6,4},{7,5},{8,10},{9,11},{10,... | collective-permute-start | bytes 12296 | tf_op jit(solution)/shard_map/ppermute | solution.py:17
  24.6 24.4 %collective-permute-start.4 = (f32[2,256]{1,0:T(2,128)S(1)}, f32[2,256]{1,0:T(2,128)S(1)}, u32[]{:S(2)}, u32[]{:S(2)}) collective-permute-start(f32[2,256]{1,0:T(2,128)S(1)} %get-tuple-element.126), channel_id=1, source_target_pairs={{0,4},{4,0},{8,12},{12,8},{1,5},{5,1},{9,13},{13,9},{2,6},{6,2},{1... | collective-permute-start | bytes 6152 | tf_op jit(solution)/shard_map/ppermute | solution.py:444
  51.8 35.3 %collective-permute-start.5 = (bf16[256,3072]{1,0:T(8,128)(2,1)S(1)}, bf16[256,3072]{1,0:T(8,128)(2,1)S(1)}, u32[]{:S(2)}, u32[]{:S(2)}) collective-permute-start(bf16[256,3072]{1,0:T(8,128)(2,1)S(1)} %broadcast_select_fusion.4), channel_id=1, source_target_pairs={{0,4},{4,0},{8,12},{12,8},{1,5},{5,1},{9,13},{13,9},{2,6},{6,2},{1... | collective-permute-start | bytes 4718600 | tf_op jit(solution)/shard_map/ppermute | solution.py:444
  52.2 35.0 %collective-permute-start.6 = (bf16[256,3072]{1,0:T(8,128)(2,1)}, bf16[256,3072]{1,0:T(8,128)(2,1)}, u32[]{:S(2)}, u32[]{:S(2)}) collective-permute-start(bf16[256,3072]{1,0:T(8,128)(2,1)} %collective-permute-done.rows_ref), channel_id=1, source_target_pairs={{4,8},{8,4},{5,9},{9,5},{6,10},{10,6},{7,11},{11,7},{20,24},{24,20... | collective-permute-start | bytes 4718600 | tf_op jit(solution)/shard_map/ppermute | solution.py:444
  87.2 47.6 %copy-start.3 = (bf16[256,3072]{1,0:T(8,128)(2,1)}, bf16[256,3072]{1,0:T(8,128)(2,1)S(1)}, u32[]{:S(2)}) copy-start(bf16[256,3072]{1,0:T(8,128)(2,1)S(1)} %collective-permute-done.5) | copy-start | bytes 4718596
  87.2 42.0 %collective-permute-start.7 = (bf16[256,3072]{1,0:T(8,128)(2,1)}, bf16[256,3072]{1,0:T(8,128)(2,1)}, u32[]{:S(2)}, u32[]{:S(2)}) collective-permute-start(bf16[256,3072]{1,0:T(8,128)(2,1)} %collective-permute-done.6), channel_id=1, source_target_pairs={{4,0},{8,12},{5,1},{9,13},{6,2},{10,14},{7,3},{11,15},{20,16},{24,... | collective-permute-start | bytes 4718600 | tf_op jit(solution)/shard_map/ppermute | solution.py:444
  88.5 40.7 %collective-permute-start.8 = (bf16[256,3072]{1,0:T(8,128)(2,1)S(1)}, bf16[256,3072]{1,0:T(8,128)(2,1)}, u32[]{:S(2)}, u32[]{:S(2)}) collective-permute-start(bf16[256,3072]{1,0:T(8,128)(2,1)S(1)} %collective-permute-done.5), channel_id=1, source_target_pairs={{4,8},{8,4},{5,9},{9,5},{6,10},{10,6},{7,11},{11,7},{20,24},{24,20... | collective-permute-start | bytes 4718600 | tf_op jit(solution)/shard_map/ppermute | solution.py:444
  90.3 38.8 %collective-permute-start.9 = (f32[2,2,256]{2,1,0:T(2,128)S(1)}, f32[2,2,256]{2,1,0:T(2,128)S(1)}, u32[]{:S(2)}, u32[]{:S(2)}) collective-permute-start(f32[2,2,256]{2,1,0:T(2,128)S(1)} %pad_maximum_fusion.4), channel_id=1, source_target_pairs={{0,8},{4,12},{8,0},{12,4},{1,9},{5,13},{9,1},{13,5},{2,10},{6,14},... | collective-permute-start | bytes 12296 | tf_op jit(solution)/shard_map/ppermute | solution.py:444
  129.1 5.6 %copy-start.6 = (bf16[256,3072]{1,0:T(8,128)(2,1)S(1)}, bf16[256,3072]{1,0:T(8,128)(2,1)}, u32[]{:S(2)}) copy-start(bf16[256,3072]{1,0:T(8,128)(2,1)} %copy-done.5) | copy-start | bytes 4718596
  132.1 33.2 %collective-permute-start.10 = (bf16[256,3072]{1,0:T(8,128)(2,1)}, bf16[256,3072]{1,0:T(8,128)(2,1)}, u32[]{:S(2)}, u32[]{:S(2)}) collective-permute-start(bf16[256,3072]{1,0:T(8,128)(2,1)} %bitcast_select_fusion), channel_id=1, source_target_pairs={{0,4},{4,0},{8,12},{12,8},{1,5},{5,1},{9,13},{13,9},{2,6},{6,2},{1... | collective-permute-start | bytes 4718600 | tf_op jit(solution)/shard_map/ppermute | solution.py:444
  132.9 32.3 %collective-permute-start.11 = (bf16[256,3072]{1,0:T(8,128)(2,1)S(1)}, bf16[256,3072]{1,0:T(8,128)(2,1)}, u32[]{:S(2)}, u32[]{:S(2)}) collective-permute-start(bf16[256,3072]{1,0:T(8,128)(2,1)S(1)} %copy-done.1), channel_id=1, source_target_pairs={{4,8},{8,4},{5,9},{9,5},{6,10},{10,6},{7,11},{11,7},{20,24},{24,20... | collective-permute-start | bytes 4718600 | tf_op jit(solution)/shard_map/ppermute | solution.py:444
  177.2 16.3 %slice-start = ((s8[6291456]{0:T(1024)(128)(4,1)}), s8[2097152]{0:T(1024)(128)(4,1)S(1)}, s32[]{:S(2)}) async-start(s8[6291456]{0:T(1024)(128)(4,1)} %bitcast.106), calls=%async_computation.4 | async-start | bytes 4194304
  177.2 17.8 %collective-permute-start.13 = (bf16[256,3072]{1,0:T(8,128)(2,1)}, bf16[256,3072]{1,0:T(8,128)(2,1)}, u32[]{:S(2)}, u32[]{:S(2)}) collective-permute-start(bf16[256,3072]{1,0:T(8,128)(2,1)} %get-tuple-element.72), channel_id=1, source_target_pairs={{4,8},{8,4},{5,9},{9,5},{6,10},{10,6},{7,11},{11,7},{20,24},{24,20... | collective-permute-start | bytes 4718600 | tf_op jit(solution)/shard_map/ppermute | solution.py:444
  179.2 35.8 %collective-permute-start.12 = (bf16[256,3072]{1,0:T(8,128)(2,1)}, bf16[256,3072]{1,0:T(8,128)(2,1)}, u32[]{:S(2)}, u32[]{:S(2)}) collective-permute-start(bf16[256,3072]{1,0:T(8,128)(2,1)} %get-tuple-element.69), channel_id=1, source_target_pairs={{0,4},{4,0},{8,12},{12,8},{1,5},{5,1},{9,13},{13,9},{2,6},{6,2},{1... | collective-permute-start | bytes 4718600 | tf_op jit(solution)/shard_map/ppermute | solution.py:444
  185.8 7.7 %slice-start.1 = ((s8[6291456]{0:T(1024)(128)(4,1)}), s8[4194304]{0:T(1024)(128)(4,1)S(1)}, s32[]{:S(2)}) async-start(s8[6291456]{0:T(1024)(128)(4,1)} %bitcast.106), calls=%async_computation.5 | async-start | bytes 8388608
  220.6 48.4 %collective-permute-start.14 = (bf16[256,3072]{1,0:T(8,128)(2,1)}, bf16[256,3072]{1,0:T(8,128)(2,1)S(1)}, u32[]{:S(2)}, u32[]{:S(2)}) collective-permute-start(bf16[256,3072]{1,0:T(8,128)(2,1)} %get-tuple-element.76), channel_id=1, source_target_pairs={{0,4},{4,0},{8,12},{12,8},{1,5},{5,1},{9,13},{13,9},{2,6},{6,2},{1... | collective-permute-start | bytes 4718600 | tf_op jit(solution)/shard_map/ppermute | solution.py:444
  222.4 46.6 %collective-permute-start.15 = (bf16[256,3072]{1,0:T(8,128)(2,1)}, bf16[256,3072]{1,0:T(8,128)(2,1)S(1)}, u32[]{:S(2)}, u32[]{:S(2)}) collective-permute-start(bf16[256,3072]{1,0:T(8,128)(2,1)} %get-tuple-element.77), channel_id=1, source_target_pairs={{4,8},{8,4},{5,9},{9,5},{6,10},{10,6},{7,11},{11,7},{20,24},{24,20... | collective-permute-start | bytes 4718600 | tf_op jit(solution)/shard_map/ppermute | solution.py:444
  225.2 43.7 %collective-permute-start.16 = (bf16[256,1536]{1,0:T(8,128)(2,1)}, bf16[256,1536]{1,0:T(8,128)(2,1)}, u32[]{:S(2)}, u32[]{:S(2)}) collective-permute-start(bf16[256,1536]{1,0:T(8,128)(2,1)} %slice.96), channel_id=1, source_target_pairs={{4,0},{8,12},{5,1},{9,13},{6,2},{10,14},{7,3},{11,15},{20,16},{24,... | collective-permute-start | bytes 2359304 | tf_op jit(solution)/shard_map/ppermute | solution.py:444
  277.0 5.7 %collective-permute-start.18 = (f32[2,256]{0,1:T(8,128)}, f32[2,256]{0,1:T(8,128)S(1)}, u32[]{:S(2)}, u32[]{:S(2)}) collective-permute-start(f32[2,256]{0,1:T(8,128)} %bitcast.124), channel_id=1, source_target_pairs={{0,1},{1,0},{2,3},{3,2},{4,5},{5,4},{6,7},{7,6},{8,9},{9,8},{10,11... | collective-permute-start | bytes 6152 | tf_op jit(solution)/shard_map/ppermute | solution.py:17
  280.2 4.2 %collective-permute-start.19 = (f32[2,3072]{1,0:T(2,128)S(1)}, f32[2,3072]{1,0:T(2,128)S(1)}, u32[]{:S(2)}, u32[]{:S(2)}) collective-permute-start(f32[2,3072]{1,0:T(2,128)S(1)} %copy-done.11), channel_id=1, source_target_pairs={{0,4},{4,0},{8,12},{12,8},{1,5},{5,1},{9,13},{13,9},{2,6},{6,2},{1... | collective-permute-start | bytes 73736 | tf_op jit(solution)/shard_map/ppermute | solution.py:444
  281.4 15.9 %collective-permute-start.17 = (bf16[256,1536]{1,0:T(8,128)(2,1)S(1)}, bf16[256,1536]{1,0:T(8,128)(2,1)}, u32[]{:S(2)}, u32[]{:S(2)}) collective-permute-start(bf16[256,1536]{1,0:T(8,128)(2,1)S(1)} %slice.97), channel_id=1, source_target_pairs={{4,0},{8,12},{5,1},{9,13},{6,2},{10,14},{7,3},{11,15},{20,16},{24,... | collective-permute-start | bytes 2359304 | tf_op jit(solution)/shard_map/ppermute | solution.py:444
  284.4 5.0 %collective-permute-start.20 = (f32[2,256]{0,1:T(8,128)S(1)}, f32[2,256]{0,1:T(8,128)S(1)}, u32[]{:S(2)}, u32[]{:S(2)}) collective-permute-start(f32[2,256]{0,1:T(8,128)S(1)} %bitcast_add_fusion), channel_id=1, source_target_pairs={{0,2},{1,3},{2,0},{3,1},{4,6},{5,7},{6,4},{7,5},{8,10},{9,11},{10,... | collective-permute-start | bytes 6152 | tf_op jit(solution)/shard_map/ppermute | solution.py:17
  286.3 4.9 %collective-permute-start.21 = (f32[2,3072]{1,0:T(2,128)S(1)}, f32[2,3072]{1,0:T(2,128)S(1)}, u32[]{:S(2)}, u32[]{:S(2)}) collective-permute-start(f32[2,3072]{1,0:T(2,128)S(1)} %add.88), channel_id=1, source_target_pairs={{0,8},{4,12},{8,0},{12,4},{1,9},{5,13},{9,1},{13,5},{2,10},{6,14},... | collective-permute-start | bytes 73736 | tf_op jit(solution)/shard_map/ppermute | solution.py:444
  303.9 4.6 %copy-start.4 = (bf16[256,3072]{1,0:T(8,128)(2,1)S(1)}, bf16[256,3072]{1,0:T(8,128)(2,1)}, u32[]{:S(2)}) copy-start(bf16[256,3072]{1,0:T(8,128)(2,1)} %copy-done.3) | copy-start | bytes 4718596
  303.9 46.5 %all-to-all-start = ((bf16[16,64,768]{2,1,0:T(8,128)(2,1)}), bf16[16,64,768]{2,1,0:T(8,128)(2,1)}, u32[]{:S(2)}, u32[]{:S(2)}) async-start(bf16[16,64,768]{2,1,0:T(8,128)(2,1)} %get-tuple-element.89), calls=%async_computation.1 | async-start | bytes 3145728 | tf_op jit(solution)/shard_map/all_to_all | solution.py:521
  350.4 3.6 collective-permute-start.22
  (8 other events, 15.6 us)
Sparse Core Ops, SparseCore 0:
  9.9 72.8 all-gather.2
  177.3 72.4 reduce-scatter.1

commit v6 on v2

--- a/solution.py
+++ b/solution.py
@@ -443,6 +443,7 @@
     row_terms = row_terms + flip(row_terms, "mp", 1)
     row_terms = (row_terms + flip(row_terms, "mp", 2)) / full_width
     columns = jnp.stack([stats[2], kept_inv, row_terms[0], row_terms[1]], 1)
+    near3[0], near3[1], columns = seq(near3[0], near3[1], columns)
     passed, outgoing = boundary(
         upper, lower, kept_rows, columns, gain, summed, bias.reshape(col_count), section
     )

time: 356 us -> 346 us (0.972)
  waiting for transfers between devices: 66.6 us -> 56.3 us
    ppermute x28, waiting for transfers between devices: 64.1 us -> 55.7 us  [shards_of_four(): along = lambda value, pairs: lax.ppermute(value, 'dp', pairs)]
  transfers between devices with their start and end apart: 39 -> 39, of which waited for: 8 -> 9; matrix products, arithmetic and copies ran while one was open for 14% -> 15% of each run, Pallas kernels for 30% -> 31%
where the time goes in v6:
time: 346 us; the launch traced here: 344 us
  Pallas kernels  112 us (32%)
  starting transfers between devices  91.3 us (26%)
  waiting for transfers between devices  56.3 us (16%)
  other arithmetic  44.6 us (13%)
  local copies, waits for them, and re-layouts  25.1 us (7%)
  between operations  15.2 us (4%)
    ppermute x28, starting transfers between devices, shards_of_four(): along = lambda value, pairs: lax.ppermute(value, 'dp', pairs)  76.8 us
    pallas_call x7, Pallas kernels, shares(): pl.pallas_call(functools.partial(share_kernel, count, turned), grid=(cols...  75.7 us
    ppermute x28, waiting for transfers between devices, shards_of_four(): along = lambda value, pairs: lax.ppermute(value, 'dp', pairs)  55.7 us
    pallas_call x4, Pallas kernels, grad_block(): pl.pallas_call(grad_kernel, grid=(cols // step,), in_specs=specs, out_spe...  31.7 us
    unnamed x109, local copies, waits for them, and re-layouts  15.1 us
    ppermute x9, starting transfers between devices, flip(): return lax.ppermute(value, axis, [(s, s ^ mask) for s in range(n)])  9.88 us
    convert_element_type x4, other arithmetic, affine(): return (hat * gain + shift).astype(bf16)  9.3 us
  transfers between devices with their start and end apart: 39, of which 9 were waited for; matrix products, arithmetic and copies ran while one was open for 15% of the time, Pallas kernels for 31%

profile of v6, /device:TPU:0, one launch (start us, length us, event | category | flops | bytes accessed | tf_op | source)
XLA Modules:
  0.0 344.4 jit_solution(15326780033639284149)
XLA Ops:
  9.8 3.0 collective-permute-start.3
  19.4 3.3 collective-permute-start
  22.7 10.2 %shard_map.110.refs_5_ = bf16[4,256,3072]{2,1,0:T(8,128)(2,1)S(1)} custom-call(bf16[256,3072]{1,0:T(8,128)(2,1)S(1)} %bitcast.115, bf16[256,3072]{1,0:T(8,128)(2,1)S(1)} %bitcast.116, bf16[3072,3072]{1,0:T(8,128)(2,1)} %bitcast.125), custom_call_target="tpu_custom_call" | custom-call | flops 1 | bytes 1 | tf_op jit(solution)/shard_map/pallas_call | solution.py:96
  42.3 4.9 %add_convert_fusion.3 = (bf16[256,3072]{1,0:T(8,128)(2,1)S(1)}, f32[256,3072]{1,0:T(8,128)}, bf16[256,3072]{1,0:T(8,128)(2,1)S(1)}) fusion(f32[3072]{0:T(1024)S(1)} %bitcast.134, f32[3072]{0:T(1024)S(1)} %bitcast.119, f32[256]{0:T(256)S(1)} %get-tuple-element.245, f32[256]{0:T(256)S(1)} %bitcast.152, bf16[1,1,1,256,3072]{4,3,2,1,0:T(8,128)(2,1)S(1)} %copy-done.6, ...), kind=kLoop, calls=%fused_computation.20 | loop fusion | flops 9437184 | bytes 9465856 | tf_op jit(solution)/shard_map/convert_element_type | solution.py:307
  47.2 10.6 %shard_map.111.refs_3_ = bf16[4,256,3072]{2,1,0:T(8,128)(2,1)S(1)} custom-call(bf16[256,3072]{1,0:T(8,128)(2,1)S(1)} %get-tuple-element.228.refs_0_.refs_1_, bf16[256,3072]{1,0:T(8,128)(2,1)S(1)} %get-tuple-element.228.refs_0_.refs_1_, bf16[3072,3072]{1,0:T(8,128)(2,1)} %bitcast.126), custom_call_target="tpu_custom_call" | custom-call | flops 1 | bytes 1 | tf_op jit(solution)/shard_map/pallas_call | solution.py:96
  62.3 6.5 %collective-permute-start.6 = (bf16[128,3072]{1,0:T(8,128)(2,1)S(1)}, bf16[128,3072]{1,0:T(8,128)(2,1)S(1)}, u32[]{:S(2)}, u32[]{:S(2)}) collective-permute-start(bf16[128,3072]{1,0:T(8,128)(2,1)S(1)} %get-tuple-element.201), channel_id=1, source_target_pairs={{0,4},{4,0},{8,12},{12,8},{1,5},{5,1},{9,13},{13,9},{2,6},{6,2},{1... | collective-permute-start | bytes 2359304 | tf_op jit(solution)/shard_map/ppermute | solution.py:299
  68.8 14.9 %collective-permute-start.13 = (bf16[128,3072]{1,0:T(8,128)(2,1)S(1)}, bf16[128,3072]{1,0:T(8,128)(2,1)S(1)}, u32[]{:S(2)}, u32[]{:S(2)}) collective-permute-start(bf16[128,3072]{1,0:T(8,128)(2,1)S(1)} %get-tuple-element.202), channel_id=1, source_target_pairs={{0,4},{4,0},{8,12},{12,8},{1,5},{5,1},{9,13},{13,9},{2,6},{6,2},{1... | collective-permute-start | bytes 2359304 | tf_op jit(solution)/shard_map/ppermute | solution.py:299
  86.1 10.2 %shard_map.112.refs_3_ = bf16[4,256,3072]{2,1,0:T(8,128)(2,1)S(1)} custom-call(bf16[256,3072]{1,0:T(8,128)(2,1)S(1)} %add_convert_fusion.2.refs_0_.refs_1_, bf16[256,3072]{1,0:T(8,128)(2,1)S(1)} %add_convert_fusion.2.refs_0_.refs_1_, bf16[3072,3072]{1,0:T(8,128)(2,1)} %bitcast.127, ...), custom_call_target="tpu_custom_call", output_to_operand_aliasing={{}: (3, {})} | custom-call | flops 1 | bytes 1 | tf_op jit(solution)/shard_map/pallas_call | solution.py:96
  98.4 13.7 %shard_map.113.refs_3_ = bf16[4,256,3072]{2,1,0:T(8,128)(2,1)S(1)} custom-call(bf16[256,1536]{1,0:T(8,128)(2,1)S(1)} %copy-done.9, bf16[256,3072]{1,0:T(8,128)(2,1)S(1)} %collective-permute-done.12.refs_1_, bf16[256,3072]{1,0:T(8,128)(2,1)S(1)} %collective-permute-done.11.refs_2_.refs_0_, ...), custom_call_target="tpu_custom_call", output_to_operand_aliasing={{}: (5, {})} | custom-call | flops 1 | bytes 1 | tf_op jit(solution)/shard_map/pallas_call | solution.py:96
  113.5 5.5 %collective-permute-start.17 = (f32[2,2,256]{2,1,0:T(2,128)S(1)}, f32[2,2,256]{2,1,0:T(2,128)S(1)}, u32[]{:S(2)}, u32[]{:S(2)}) collective-permute-start(f32[2,2,256]{2,1,0:T(2,128)S(1)} %pad_maximum_fusion.13), channel_id=1, source_target_pairs={{0,8},{4,12},{8,0},{12,4},{1,9},{5,13},{9,1},{13,5},{2,10},{6,14},... | collective-permute-start | bytes 12296 | tf_op jit(solution)/shard_map/ppermute | solution.py:299
  120.0 10.8 %shard_map.114 = bf16[4,256,3072]{2,1,0:T(8,128)(2,1)S(1)} custom-call(bf16[256,3072]{1,0:T(8,128)(2,1)S(1)} %collective-permute-done.11.refs_2_.refs_0_, bf16[256,3072]{1,0:T(8,128)(2,1)S(1)} %collective-permute-done.12.refs_1_, bf16[3072,3072]{1,0:T(8,128)(2,1)} %bitcast.129, ...), custom_call_target="tpu_custom_call", output_to_operand_aliasing={{}: (3, {})} | custom-call | flops 1 | bytes 1 | tf_op jit(solution)/shard_map/pallas_call | solution.py:96
  131.7 3.5 %collective-permute-start.18 = (bf16[128,3072]{1,0:T(8,128)(2,1)S(1)}, bf16[128,3072]{1,0:T(8,128)(2,1)S(1)}, u32[]{:S(2)}, u32[]{:S(2)}) collective-permute-start(bf16[128,3072]{1,0:T(8,128)(2,1)S(1)} %bitcast_select_fusion.1), channel_id=1, source_target_pairs={{0,4},{4,0},{8,12},{12,8},{1,5},{5,1},{9,13},{13,9},{2,6},{6,2},{1... | collective-permute-start | bytes 2359304 | tf_op jit(solution)/shard_map/ppermute | solution.py:299
  136.2 10.1 %shard_map.115.refs_3_ = bf16[4,256,3072]{2,1,0:T(8,128)(2,1)S(1)} custom-call(bf16[256,3072]{1,0:T(8,128)(2,1)S(1)} %add_convert_fusion.1.refs_0_.refs_1_, bf16[256,3072]{1,0:T(8,128)(2,1)S(1)} %add_convert_fusion.1.refs_0_.refs_1_, bf16[3072,3072]{1,0:T(8,128)(2,1)} %bitcast.130, ...), custom_call_target="tpu_custom_call", output_to_operand_aliasing={{}: (3, {})} | custom-call | flops 1 | bytes 1 | tf_op jit(solution)/shard_map/pallas_call | solution.py:96
  150.0 10.1 %shard_map.116 = bf16[4,256,3072]{2,1,0:T(8,128)(2,1)S(1)} custom-call(bf16[256,3072]{1,0:T(8,128)(2,1)S(1)} %add_convert_fusion.refs_0_.refs_1_, bf16[256,3072]{1,0:T(8,128)(2,1)S(1)} %add_convert_fusion.refs_0_.refs_1_, bf16[3072,3072]{1,0:T(8,128)(2,1)} %bitcast.131, bf16[4,256,3072]{2,1,0:T(8,128)(2,1)S(1)} %shard_map.115.refs_3_), custom_call_target="tpu_custom_call", output_to_operand_aliasing={{}: (3, {})} | custom-call | flops 1 | bytes 1 | tf_op jit(solution)/shard_map/pallas_call | solution.py:96
  164.0 3.2 pad_maximum_fusion
  174.2 9.2 %collective-permute-start.20 = (bf16[128,3072]{1,0:T(8,128)(2,1)S(1)}, bf16[128,3072]{1,0:T(8,128)(2,1)S(1)}, u32[]{:S(2)}, u32[]{:S(2)}) collective-permute-start(bf16[128,3072]{1,0:T(8,128)(2,1)S(1)} %copy-done.46), channel_id=1, source_target_pairs={{0,4},{4,0},{8,12},{12,8},{1,5},{5,1},{9,13},{13,9},{2,6},{6,2},{1... | collective-permute-start | bytes 2359304 | tf_op jit(solution)/shard_map/ppermute | solution.py:299
  184.6 4.3 %collective-permute-start.26 = (bf16[128,3072]{1,0:T(8,128)(2,1)S(1)}, bf16[128,3072]{1,0:T(8,128)(2,1)S(1)}, u32[]{:S(2)}, u32[]{:S(2)}) collective-permute-start(bf16[128,3072]{1,0:T(8,128)(2,1)S(1)} %get-tuple-element.133), channel_id=1, source_target_pairs={{0,4},{4,0},{8,12},{12,8},{1,5},{5,1},{9,13},{13,9},{2,6},{6,2},{1... | collective-permute-start | bytes 2359304 | tf_op jit(solution)/shard_map/ppermute | solution.py:299
  192.5 3.2 pad_maximum_fusion.2.c_ref
  195.7 6.1 %collective-permute-done.20 = bf16[128,3072]{1,0:T(8,128)(2,1)S(1)} collective-permute-done((bf16[128,3072]{1,0:T(8,128)(2,1)S(1)}, bf16[128,3072]{1,0:T(8,128)(2,1)S(1)}, u32[]{:S(2)}, u32[]{:S(2)}) %collective-permute-start.20) | collective-permute-done | bytes 786464 | tf_op jit(solution)/shard_map/ppermute | solution.py:299
  202.7 4.2 %collective-permute-start.24 = (bf16[128,3072]{1,0:T(8,128)(2,1)S(1)}, bf16[128,3072]{1,0:T(8,128)(2,1)S(1)}, u32[]{:S(2)}, u32[]{:S(2)}) collective-permute-start(bf16[128,3072]{1,0:T(8,128)(2,1)S(1)} %get-tuple-element.129), channel_id=1, source_target_pairs={{0,4},{4,0},{8,12},{12,8},{1,5},{5,1},{9,13},{13,9},{2,6},{6,2},{1... | collective-permute-start | bytes 2359304 | tf_op jit(solution)/shard_map/ppermute | solution.py:299
  208.9 9.8 %collective-permute-done.26 = bf16[128,3072]{1,0:T(8,128)(2,1)S(1)} collective-permute-done((bf16[128,3072]{1,0:T(8,128)(2,1)S(1)}, bf16[128,3072]{1,0:T(8,128)(2,1)S(1)}, u32[]{:S(2)}, u32[]{:S(2)}) %collective-permute-start.26) | collective-permute-done | bytes 786464 | tf_op jit(solution)/shard_map/ppermute | solution.py:299
  219.6 4.1 %collective-permute-start.28 = (bf16[128,3072]{1,0:T(8,128)(2,1)S(1)}, bf16[128,3072]{1,0:T(8,128)(2,1)S(1)}, u32[]{:S(2)}, u32[]{:S(2)}) collective-permute-start(bf16[128,3072]{1,0:T(8,128)(2,1)S(1)} %get-tuple-element.142), channel_id=1, source_target_pairs={{0,4},{4,0},{8,12},{12,8},{1,5},{5,1},{9,13},{13,9},{2,6},{6,2},{1... | collective-permute-start | bytes 2359304 | tf_op jit(solution)/shard_map/ppermute | solution.py:299
  224.7 8.0 %collective-permute-done.24 = bf16[128,3072]{1,0:T(8,128)(2,1)S(1)} collective-permute-done((bf16[128,3072]{1,0:T(8,128)(2,1)S(1)}, bf16[128,3072]{1,0:T(8,128)(2,1)S(1)}, u32[]{:S(2)}, u32[]{:S(2)}) %collective-permute-start.24) | collective-permute-done | bytes 786464 | tf_op jit(solution)/shard_map/ppermute | solution.py:299
  233.6 10.1 %collective-permute-done.28 = bf16[128,3072]{1,0:T(8,128)(2,1)S(1)} collective-permute-done((bf16[128,3072]{1,0:T(8,128)(2,1)S(1)}, bf16[128,3072]{1,0:T(8,128)(2,1)S(1)}, u32[]{:S(2)}, u32[]{:S(2)}) %collective-permute-start.28) | collective-permute-done | bytes 786464 | tf_op jit(solution)/shard_map/ppermute | solution.py:299
  249.5 2.9 maximum_select_fusion.2
  252.7 13.6 %collective-permute-done.31 = bf16[256,1536]{1,0:T(8,128)(2,1)S(1)} collective-permute-done((bf16[256,1536]{1,0:T(8,128)(2,1)S(1)}, bf16[256,1536]{1,0:T(8,128)(2,1)S(1)}, u32[]{:S(2)}, u32[]{:S(2)}) %collective-permute-start.31) | collective-permute-done | bytes 786464 | tf_op jit(solution)/shard_map/ppermute | solution.py:299
  267.2 7.6 %collective-permute-done.30 = bf16[256,1536]{1,0:T(8,128)(2,1)} collective-permute-done((bf16[256,1536]{1,0:T(8,128)(2,1)S(1)}, bf16[256,1536]{1,0:T(8,128)(2,1)}, u32[]{:S(2)}, u32[]{:S(2)}) %collective-permute-start.30) | collective-permute-done | bytes 786464 | tf_op jit(solution)/shard_map/ppermute | solution.py:299
  281.8 4.7 %all-to-all-start = ((bf16[16,64,768]{2,1,0:T(8,128)(2,1)}), bf16[16,64,768]{2,1,0:T(8,128)(2,1)}, u32[]{:S(2)}, u32[]{:S(2)}) async-start(bf16[16,64,768]{2,1,0:T(8,128)(2,1)} %copy-done.15), calls=%async_computation.1 | async-start | bytes 3145728 | tf_op jit(solution)/shard_map/all_to_all | solution.py:450
  293.1 7.9 %shard_map.118.rest_0_ = f32[3072,3072]{1,0:T(8,128)} custom-call(bf16[1024,768]{1,0:T(8,128)(2,1)S(1)} %pad_maximum_fusion.6.v_ref, bf16[1024,3072]{1,0:T(8,128)(2,1)S(1)} %bitcast.109), custom_call_target="tpu_custom_call" | custom-call | flops 1 | bytes 1 | tf_op jit(solution)/shard_map/pallas_call | solution.py:43
  302.2 7.9 %shard_map.119.rest_0_ = f32[3072,3072]{1,0:T(8,128)} custom-call(bf16[1024,768]{1,0:T(8,128)(2,1)S(1)} %pad_maximum_fusion.7.v_ref, bf16[1024,3072]{1,0:T(8,128)(2,1)S(1)} %bitcast.109, f32[3072,3072]{1,0:T(8,128)} %shard_map.118.rest_0_), custom_call_target="tpu_custom_call", output_to_operand_aliasing={{}: (2, {})} | custom-call | flops 1 | bytes 1 | tf_op jit(solution)/shard_map/pallas_call | solution.py:43
  312.8 7.9 %shard_map.120.rest_0_ = f32[3072,3072]{1,0:T(8,128)} custom-call(bf16[1024,768]{1,0:T(8,128)(2,1)S(1)} %pad_maximum_fusion.8.v_ref, bf16[1024,3072]{1,0:T(8,128)(2,1)S(1)} %bitcast.109, f32[3072,3072]{1,0:T(8,128)} %shard_map.119.rest_0_), custom_call_target="tpu_custom_call", output_to_operand_aliasing={{}: (2, {})} | custom-call | flops 1 | bytes 1 | tf_op jit(solution)/shard_map/pallas_call | solution.py:43
  328.0 7.9 %shard_map.122 = f32[3072,3072]{1,0:T(8,128)} custom-call(bf16[1024,768]{1,0:T(8,128)(2,1)S(1)} %pad_maximum_fusion.9.v_ref, bf16[1024,3072]{1,0:T(8,128)(2,1)S(1)} %copy-done, f32[3072,3072]{1,0:T(8,128)} %shard_map.120.rest_0_), custom_call_target="tpu_custom_call", output_to_operand_aliasing={{}: (2, {})} | custom-call | flops 1 | bytes 1 | tf_op jit(solution)/shard_map/pallas_call | solution.py:43
  (244 shorter events, 89.2 us)
Async XLA Ops:
  7.2 267.8 %reduce-scatter.2.cloned.1.call-start = ((), (), s32[]{:S(2)}) async-start(), calls=%async_computation.2 | async-start | bytes 7864320 | tf_op jit(solution)/shard_map/reduce_scatter | solution.py:397
  9.8 25.8 %collective-permute-start.3 = (bf16[256,1536]{1,0:T(8,128)(2,1)}, bf16[256,1536]{1,0:T(8,128)(2,1)S(1)}, u32[]{:S(2)}, u32[]{:S(2)}) collective-permute-start(bf16[256,1536]{1,0:T(8,128)(2,1)} %get-tuple-element.226), channel_id=1, source_target_pairs={{0,2},{1,3},{2,0},{3,1},{4,6},{5,7},{6,4},{7,5},{8,10},{9,11},{10,... | collective-permute-start | bytes 2359304 | tf_op jit(solution)/shard_map/ppermute | solution.py:16
  12.8 22.8 %collective-permute-start.2 = (bf16[256,1536]{1,0:T(8,128)(2,1)}, bf16[256,1536]{1,0:T(8,128)(2,1)S(1)}, u32[]{:S(2)}, u32[]{:S(2)}) collective-permute-start(bf16[256,1536]{1,0:T(8,128)(2,1)} %get-tuple-element.227), channel_id=1, source_target_pairs={{0,1},{1,0},{2,3},{3,2},{4,5},{5,4},{6,7},{7,6},{8,9},{9,8},{10,11... | collective-permute-start | bytes 2359304 | tf_op jit(solution)/shard_map/ppermute | solution.py:16
  16.9 18.6 %collective-permute-start.4 = (f32[4,256]{1,0:T(4,128)S(1)}, f32[4,256]{1,0:T(4,128)S(1)}, u32[]{:S(2)}, u32[]{:S(2)}) collective-permute-start(f32[4,256]{1,0:T(4,128)S(1)} %pad_maximum_fusion.12), channel_id=1, source_target_pairs={{0,1},{1,0},{2,3},{3,2},{4,5},{5,4},{6,7},{7,6},{8,9},{9,8},{10,11... | collective-permute-start | bytes 12296 | tf_op jit(solution)/shard_map/ppermute | solution.py:16
  17.5 40.3 %collective-permute-start.1 = (bf16[256,3072]{1,0:T(8,128)(2,1)}, bf16[256,3072]{1,0:T(8,128)(2,1)}, u32[]{:S(2)}, u32[]{:S(2)}) collective-permute-start(bf16[256,3072]{1,0:T(8,128)(2,1)} %bitcast), channel_id=1, source_target_pairs={{4,8},{8,4},{5,9},{9,5},{6,10},{10,6},{7,11},{11,7},{20,24},{24,20... | collective-permute-start | bytes 4718600 | tf_op jit(solution)/shard_map/ppermute | solution.py:299
  19.4 38.5 %collective-permute-start = (bf16[256,3072]{1,0:T(8,128)(2,1)}, bf16[256,3072]{1,0:T(8,128)(2,1)}, u32[]{:S(2)}, u32[]{:S(2)}) collective-permute-start(bf16[256,3072]{1,0:T(8,128)(2,1)} %bitcast), channel_id=1, source_target_pairs={{0,4},{4,0},{8,12},{12,8},{1,5},{5,1},{9,13},{13,9},{2,6},{6,2},{1... | collective-permute-start | bytes 4718600 | tf_op jit(solution)/shard_map/ppermute | solution.py:299
  39.0 58.6 %collective-permute-start.12 = (bf16[256,3072]{1,0:T(8,128)(2,1)S(1)}, bf16[256,3072]{1,0:T(8,128)(2,1)S(1)}, u32[]{:S(2)}, u32[]{:S(2)}) collective-permute-start(bf16[256,3072]{1,0:T(8,128)(2,1)S(1)} %pad_maximum_fusion.4), channel_id=1, source_target_pairs={{0,1},{1,0},{2,3},{3,2},{4,5},{5,4},{6,7},{7,6},{8,9},{9,8},{10,11... | collective-permute-start | bytes 4718600 | tf_op jit(solution)/shard_map/ppermute | solution.py:16
  40.6 57.8 %collective-permute-start.11 = (bf16[256,3072]{1,0:T(8,128)(2,1)S(1)}, bf16[256,3072]{1,0:T(8,128)(2,1)S(1)}, u32[]{:S(2)}, u32[]{:S(2)}) collective-permute-start(bf16[256,3072]{1,0:T(8,128)(2,1)S(1)} %pad_maximum_fusion.3), channel_id=1, source_target_pairs={{0,2},{1,3},{2,0},{3,1},{4,6},{5,7},{6,4},{7,5},{8,10},{9,11},{10,... | collective-permute-start | bytes 4718600 | tf_op jit(solution)/shard_map/ppermute | solution.py:16
  42.1 15.7 %collective-permute-start.8 = (f32[2,256]{1,0:T(2,128)S(1)}, f32[2,256]{1,0:T(2,128)S(1)}, u32[]{:S(2)}, u32[]{:S(2)}) collective-permute-start(f32[2,256]{1,0:T(2,128)S(1)} %get-tuple-element.239), channel_id=1, source_target_pairs={{0,4},{4,0},{8,12},{12,8},{1,5},{5,1},{9,13},{13,9},{2,6},{6,2},{1... | collective-permute-start | bytes 6152 | tf_op jit(solution)/shard_map/ppermute | solution.py:299
  60.1 52.1 %collective-permute-start.14 = (bf16[128,3072]{1,0:T(8,128)(2,1)S(1)}, bf16[128,3072]{1,0:T(8,128)(2,1)S(1)}, u32[]{:S(2)}, u32[]{:S(2)}) collective-permute-start(bf16[128,3072]{1,0:T(8,128)(2,1)S(1)} %get-tuple-element.225), channel_id=1, source_target_pairs={{4,8},{8,4},{5,9},{9,5},{6,10},{10,6},{7,11},{11,7},{20,24},{24,20... | collective-permute-start | bytes 2359304 | tf_op jit(solution)/shard_map/ppermute | solution.py:299
  62.3 34.0 %collective-permute-start.6 = (bf16[128,3072]{1,0:T(8,128)(2,1)S(1)}, bf16[128,3072]{1,0:T(8,128)(2,1)S(1)}, u32[]{:S(2)}, u32[]{:S(2)}) collective-permute-start(bf16[128,3072]{1,0:T(8,128)(2,1)S(1)} %get-tuple-element.201), channel_id=1, source_target_pairs={{0,4},{4,0},{8,12},{12,8},{1,5},{5,1},{9,13},{13,9},{2,6},{6,2},{1... | collective-permute-start | bytes 2359304 | tf_op jit(solution)/shard_map/ppermute | solution.py:299
  68.8 43.4 %collective-permute-start.13 = (bf16[128,3072]{1,0:T(8,128)(2,1)S(1)}, bf16[128,3072]{1,0:T(8,128)(2,1)S(1)}, u32[]{:S(2)}, u32[]{:S(2)}) collective-permute-start(bf16[128,3072]{1,0:T(8,128)(2,1)S(1)} %get-tuple-element.202), channel_id=1, source_target_pairs={{0,4},{4,0},{8,12},{12,8},{1,5},{5,1},{9,13},{13,9},{2,6},{6,2},{1... | collective-permute-start | bytes 2359304 | tf_op jit(solution)/shard_map/ppermute | solution.py:299
  96.3 34.5 %collective-permute-start.9 = (bf16[128,3072]{1,0:T(8,128)(2,1)S(1)}, bf16[128,3072]{1,0:T(8,128)(2,1)S(1)}, u32[]{:S(2)}, u32[]{:S(2)}) collective-permute-start(bf16[128,3072]{1,0:T(8,128)(2,1)S(1)} %collective-permute-done.7), channel_id=1, source_target_pairs={{4,0},{8,12},{5,1},{9,13},{6,2},{10,14},{7,3},{11,15},{20,16},{24,... | collective-permute-start | bytes 2359304 | tf_op jit(solution)/shard_map/ppermute | solution.py:299
  97.6 33.2 %collective-permute-start.10 = (bf16[128,3072]{1,0:T(8,128)(2,1)S(1)}, bf16[128,3072]{1,0:T(8,128)(2,1)S(1)}, u32[]{:S(2)}, u32[]{:S(2)}) collective-permute-start(bf16[128,3072]{1,0:T(8,128)(2,1)S(1)} %collective-permute-done.6), channel_id=1, source_target_pairs={{4,8},{8,4},{5,9},{9,5},{6,10},{10,6},{7,11},{11,7},{20,24},{24,20... | collective-permute-start | bytes 2359304 | tf_op jit(solution)/shard_map/ppermute | solution.py:299
  112.2 34.2 %collective-permute-start.15 = (bf16[128,3072]{1,0:T(8,128)(2,1)S(1)}, bf16[128,3072]{1,0:T(8,128)(2,1)S(1)}, u32[]{:S(2)}, u32[]{:S(2)}) collective-permute-start(bf16[128,3072]{1,0:T(8,128)(2,1)S(1)} %collective-permute-done.14), channel_id=1, source_target_pairs={{4,0},{8,12},{5,1},{9,13},{6,2},{10,14},{7,3},{11,15},{20,16},{24,... | collective-permute-start | bytes 2359304 | tf_op jit(solution)/shard_map/ppermute | solution.py:299
  113.5 17.3 %collective-permute-start.17 = (f32[2,2,256]{2,1,0:T(2,128)S(1)}, f32[2,2,256]{2,1,0:T(2,128)S(1)}, u32[]{:S(2)}, u32[]{:S(2)}) collective-permute-start(f32[2,2,256]{2,1,0:T(2,128)S(1)} %pad_maximum_fusion.13), channel_id=1, source_target_pairs={{0,8},{4,12},{8,0},{12,4},{1,9},{5,13},{9,1},{13,5},{2,10},{6,14},... | collective-permute-start | bytes 12296 | tf_op jit(solution)/shard_map/ppermute | solution.py:299
  118.9 27.4 %collective-permute-start.16 = (bf16[128,3072]{1,0:T(8,128)(2,1)S(1)}, bf16[128,3072]{1,0:T(8,128)(2,1)S(1)}, u32[]{:S(2)}, u32[]{:S(2)}) collective-permute-start(bf16[128,3072]{1,0:T(8,128)(2,1)S(1)} %collective-permute-done.13), channel_id=1, source_target_pairs={{4,8},{8,4},{5,9},{9,5},{6,10},{10,6},{7,11},{11,7},{20,24},{24,20... | collective-permute-start | bytes 2359304 | tf_op jit(solution)/shard_map/ppermute | solution.py:299
  131.0 29.1 %collective-permute-start.19 = (bf16[128,3072]{1,0:T(8,128)(2,1)S(1)}, bf16[128,3072]{1,0:T(8,128)(2,1)S(1)}, u32[]{:S(2)}, u32[]{:S(2)}) collective-permute-start(bf16[128,3072]{1,0:T(8,128)(2,1)S(1)} %slice.181), channel_id=1, source_target_pairs={{4,8},{8,4},{5,9},{9,5},{6,10},{10,6},{7,11},{11,7},{20,24},{24,20... | collective-permute-start | bytes 2359304 | tf_op jit(solution)/shard_map/ppermute | solution.py:299
  131.7 28.4 %collective-permute-start.18 = (bf16[128,3072]{1,0:T(8,128)(2,1)S(1)}, bf16[128,3072]{1,0:T(8,128)(2,1)S(1)}, u32[]{:S(2)}, u32[]{:S(2)}) collective-permute-start(bf16[128,3072]{1,0:T(8,128)(2,1)S(1)} %bitcast_select_fusion.1), channel_id=1, source_target_pairs={{0,4},{4,0},{8,12},{12,8},{1,5},{5,1},{9,13},{13,9},{2,6},{6,2},{1... | collective-permute-start | bytes 2359304 | tf_op jit(solution)/shard_map/ppermute | solution.py:299
  147.4 20.3 %collective-permute-start.22 = (bf16[128,3072]{1,0:T(8,128)(2,1)}, bf16[128,3072]{1,0:T(8,128)(2,1)}, u32[]{:S(2)}, u32[]{:S(2)}) collective-permute-start(bf16[128,3072]{1,0:T(8,128)(2,1)} %bitcast_select_fusion), channel_id=1, source_target_pairs={{0,4},{4,0},{8,12},{12,8},{1,5},{5,1},{9,13},{13,9},{2,6},{6,2},{1... | collective-permute-start | bytes 2359304 | tf_op jit(solution)/shard_map/ppermute | solution.py:299
  174.2 27.7 %collective-permute-start.20 = (bf16[128,3072]{1,0:T(8,128)(2,1)S(1)}, bf16[128,3072]{1,0:T(8,128)(2,1)S(1)}, u32[]{:S(2)}, u32[]{:S(2)}) collective-permute-start(bf16[128,3072]{1,0:T(8,128)(2,1)S(1)} %copy-done.46), channel_id=1, source_target_pairs={{0,4},{4,0},{8,12},{12,8},{1,5},{5,1},{9,13},{13,9},{2,6},{6,2},{1... | collective-permute-start | bytes 2359304 | tf_op jit(solution)/shard_map/ppermute | solution.py:299
  183.4 18.5 %collective-permute-start.21 = (bf16[128,3072]{1,0:T(8,128)(2,1)S(1)}, bf16[128,3072]{1,0:T(8,128)(2,1)S(1)}, u32[]{:S(2)}, u32[]{:S(2)}) collective-permute-start(bf16[128,3072]{1,0:T(8,128)(2,1)S(1)} %copy-done.45), channel_id=1, source_target_pairs={{4,8},{8,4},{5,9},{9,5},{6,10},{10,6},{7,11},{11,7},{20,24},{24,20... | collective-permute-start | bytes 2359304 | tf_op jit(solution)/shard_map/ppermute | solution.py:299
  184.6 34.1 %collective-permute-start.26 = (bf16[128,3072]{1,0:T(8,128)(2,1)S(1)}, bf16[128,3072]{1,0:T(8,128)(2,1)S(1)}, u32[]{:S(2)}, u32[]{:S(2)}) collective-permute-start(bf16[128,3072]{1,0:T(8,128)(2,1)S(1)} %get-tuple-element.133), channel_id=1, source_target_pairs={{0,4},{4,0},{8,12},{12,8},{1,5},{5,1},{9,13},{13,9},{2,6},{6,2},{1... | collective-permute-start | bytes 2359304 | tf_op jit(solution)/shard_map/ppermute | solution.py:299
  189.0 29.7 %collective-permute-start.27 = (bf16[128,3072]{1,0:T(8,128)(2,1)S(1)}, bf16[128,3072]{1,0:T(8,128)(2,1)S(1)}, u32[]{:S(2)}, u32[]{:S(2)}) collective-permute-start(bf16[128,3072]{1,0:T(8,128)(2,1)S(1)} %get-tuple-element.134), channel_id=1, source_target_pairs={{4,8},{8,4},{5,9},{9,5},{6,10},{10,6},{7,11},{11,7},{20,24},{24,20... | collective-permute-start | bytes 2359304 | tf_op jit(solution)/shard_map/ppermute | solution.py:299
  202.7 29.9 %collective-permute-start.24 = (bf16[128,3072]{1,0:T(8,128)(2,1)S(1)}, bf16[128,3072]{1,0:T(8,128)(2,1)S(1)}, u32[]{:S(2)}, u32[]{:S(2)}) collective-permute-start(bf16[128,3072]{1,0:T(8,128)(2,1)S(1)} %get-tuple-element.129), channel_id=1, source_target_pairs={{0,4},{4,0},{8,12},{12,8},{1,5},{5,1},{9,13},{13,9},{2,6},{6,2},{1... | collective-permute-start | bytes 2359304 | tf_op jit(solution)/shard_map/ppermute | solution.py:299
  206.9 25.7 %collective-permute-start.25 = (bf16[128,3072]{1,0:T(8,128)(2,1)S(1)}, bf16[128,3072]{1,0:T(8,128)(2,1)S(1)}, u32[]{:S(2)}, u32[]{:S(2)}) collective-permute-start(bf16[128,3072]{1,0:T(8,128)(2,1)S(1)} %get-tuple-element.130), channel_id=1, source_target_pairs={{4,8},{8,4},{5,9},{9,5},{6,10},{10,6},{7,11},{11,7},{20,24},{24,20... | collective-permute-start | bytes 2359304 | tf_op jit(solution)/shard_map/ppermute | solution.py:299
  219.6 24.1 %collective-permute-start.28 = (bf16[128,3072]{1,0:T(8,128)(2,1)S(1)}, bf16[128,3072]{1,0:T(8,128)(2,1)S(1)}, u32[]{:S(2)}, u32[]{:S(2)}) collective-permute-start(bf16[128,3072]{1,0:T(8,128)(2,1)S(1)} %get-tuple-element.142), channel_id=1, source_target_pairs={{0,4},{4,0},{8,12},{12,8},{1,5},{5,1},{9,13},{13,9},{2,6},{6,2},{1... | collective-permute-start | bytes 2359304 | tf_op jit(solution)/shard_map/ppermute | solution.py:299
  223.7 20.0 %collective-permute-start.29 = (bf16[128,3072]{1,0:T(8,128)(2,1)S(1)}, bf16[128,3072]{1,0:T(8,128)(2,1)S(1)}, u32[]{:S(2)}, u32[]{:S(2)}) collective-permute-start(bf16[128,3072]{1,0:T(8,128)(2,1)S(1)} %get-tuple-element.143), channel_id=1, source_target_pairs={{4,8},{8,4},{5,9},{9,5},{6,10},{10,6},{7,11},{11,7},{20,24},{24,20... | collective-permute-start | bytes 2359304 | tf_op jit(solution)/shard_map/ppermute | solution.py:299
  246.3 20.1 %collective-permute-start.31 = (bf16[256,1536]{1,0:T(8,128)(2,1)S(1)}, bf16[256,1536]{1,0:T(8,128)(2,1)S(1)}, u32[]{:S(2)}, u32[]{:S(2)}) collective-permute-start(bf16[256,1536]{1,0:T(8,128)(2,1)S(1)} %get-tuple-element.217), channel_id=1, source_target_pairs={{4,0},{8,12},{5,1},{9,13},{6,2},{10,14},{7,3},{11,15},{20,16},{24,... | collective-permute-start | bytes 2359304 | tf_op jit(solution)/shard_map/ppermute | solution.py:299
  247.6 27.3 %collective-permute-start.30 = (bf16[256,1536]{1,0:T(8,128)(2,1)S(1)}, bf16[256,1536]{1,0:T(8,128)(2,1)}, u32[]{:S(2)}, u32[]{:S(2)}) collective-permute-start(bf16[256,1536]{1,0:T(8,128)(2,1)S(1)} %get-tuple-element.218), channel_id=1, source_target_pairs={{4,0},{8,12},{5,1},{9,13},{6,2},{10,14},{7,3},{11,15},{20,16},{24,... | collective-permute-start | bytes 2359304 | tf_op jit(solution)/shard_map/ppermute | solution.py:299
  281.8 39.5 %all-to-all-start = ((bf16[16,64,768]{2,1,0:T(8,128)(2,1)}), bf16[16,64,768]{2,1,0:T(8,128)(2,1)}, u32[]{:S(2)}, u32[]{:S(2)}) async-start(bf16[16,64,768]{2,1,0:T(8,128)(2,1)} %copy-done.15), calls=%async_computation.1 | async-start | bytes 3145728 | tf_op jit(solution)/shard_map/all_to_all | solution.py:450
  290.0 20.2 %collective-permute-start.34 = (f32[2,3072]{1,0:T(2,128)S(1)}, f32[2,3072]{1,0:T(2,128)S(1)}, u32[]{:S(2)}, u32[]{:S(2)}) collective-permute-start(f32[2,3072]{1,0:T(2,128)S(1)} %maximum_add_fusion), channel_id=1, source_target_pairs={{0,4},{4,0},{8,12},{12,8},{1,5},{5,1},{9,13},{13,9},{2,6},{6,2},{1... | collective-permute-start | bytes 73736 | tf_op jit(solution)/shard_map/ppermute | solution.py:299
  (61 other events, 592.5 us)
Sparse Core Ops, SparseCore 0:
  167.8 76.0 reduce-scatter.1
